TPU v7x, 128 devices: a whole 4x4x4 slice. The times are simulated.
128 devices in a mesh: row: 16 (over y, z), col: 8 (over x, core).
Axes of the slice: x: 4, y: 4, z: 4, core: 2. Of those that a mesh axis runs over, the one named last changes fastest.
Arguments:
- load_vectors: bfloat16 [1024, 64, 384], P(('row', 'col')), may hold values from -6 to 6
- live_panels: int32 [1024], P(('row', 'col')), may hold values from 64 to 128
- self_blocks: bfloat16 [1024, 384, 384], P(('row', 'col')), may hold values from -0.3125 to 0.3125
- near_pairs: int32 [6144, 2], P(('row', 'col')), may hold values from 0 to 1023, as said below
- near_count: int32 [128], P(('row', 'col')), may hold values from 1 to 48, as said below
- near_blocks: bfloat16 [6144, 384, 384], P(('row', 'col')), may hold values from -0.3125 to 0.3125
- far_pairs: int32 [12288, 2], P(('row', 'col')), may hold values from 0 to 1023, as said below
- far_rank: int32 [12288], P(('row', 'col')), may hold values from 8 to 32, as said below
- far_left: bfloat16 [12288, 384, 32], P(('row', 'col')), may hold values from -1 to 1
- far_right: bfloat16 [12288, 384, 32], P(('row', 'col')), may hold values from -0.3125 to 0.3125
Outputs:
- product: float32 [1024, 64, 384], P(('row', 'col'))
Inputs may be any that keep to these rules, and one draw needn't show every extreme that they name: `near_pairs`: slot s of group g = 8 a + b names a row cluster r with r // 64 = a and a column cluster c with (c // 8) mod 8 = b, and r != c. `far_pairs`: the same layout as near_pairs, with 96 slots a group. `near_count`: some group uses all of its slots. `far_rank`: some pair has the largest rank.
All inputs are finite; a program needn't handle non-finite values.
Results may differ from a plain program's by a relative error of at most 0.0065.
Values may be sent and summed in bfloat16 or wider, within the bound.
No kernel may reach another device: no remote copies, remote signals or barrier semaphores. Data moves between devices by JAX's collectives and lax.ppermute only.
A program may use at most 128 MiB of HBM per device.

v0:
```python
import functools

import jax
import jax.numpy as jnp
from jax import lax
from jax.experimental import pallas as pl
from jax.experimental.pallas import tpu as pltpu
from jax.sharding import PartitionSpec as P

NEAR_STEP = 4
FAR_STEP = 8

def pair_kernel(flip, src_of, dst_of, splits, near_pairs, near_count, far_pairs, far_rank, near, proj, back, *refs):
    n_in, n_out = len(splits[0]), len(splits[1])
    sources, outs = refs[:n_in], refs[n_in:n_in + n_out]
    xbuf, nbuf, pbuf, bbuf, acc, obuf, xsem, nsem, psem, bsem, osem = refs[n_in + n_out:]
    near_n, far_n = nbuf.shape[0], far_rank.shape[0]
    spare = acc.shape[0] - 1
    count = near_count[0]
    place = (lax.axis_index("row"), lax.axis_index("col"))
    x_copies, first = [], 0
    for k, size in enumerate(splits[0]):
        x_copies.append(pltpu.make_async_copy(sources[k], xbuf.at[pl.ds(first, size)], xsem.at[k]))
        first += size
    def near_copy(i):
        rows = pl.ds(i * NEAR_STEP, NEAR_STEP)
        return pltpu.make_async_copy(near.at[rows], nbuf.at[rows], nsem.at[i])
    p_copy = pltpu.make_async_copy(proj, pbuf, psem)
    b_copy = pltpu.make_async_copy(back, bbuf, bsem)
    for copy in x_copies:
        copy.start()
    p_copy.start()
    b_copy.start()
    steps = (count + NEAR_STEP - 1) // NEAR_STEP
    @pl.loop(0, acc.shape[0])
    def _(i):
        acc[i] = jnp.zeros(acc.shape[1:], jnp.float32)
    for copy in x_copies:
        copy.wait()
    p_copy.wait()
    b_copy.wait()
    @pl.loop(0, steps)
    def _(i):
        near_copy(i).start()
    rank_n = proj.shape[0] // far_n
    @pl.loop(0, far_n // FAR_STEP)
    def _(i):
        ids = [i * FAR_STEP + u for u in range(FAR_STEP)]
        pairs = [(far_pairs[0, q], far_pairs[1, q], place) for q in ids]
        rows = pl.ds(pl.multiple_of(i * FAR_STEP * rank_n, FAR_STEP * rank_n), FAR_STEP * rank_n)
        x = jnp.concatenate([xbuf[src_of(*pair)] for pair in pairs], axis=0)
        t = lax.dot_general(x, pbuf[rows], (((1,), (1,)), ((), ())), preferred_element_type=jnp.float32)
        lane = lax.broadcasted_iota(jnp.int32, (xbuf.shape[1], FAR_STEP * rank_n), 1)
        parts = []
        for u, q in enumerate(ids):
            keep = (lane >= u * rank_n) & (lane < u * rank_n + far_rank[q])
            parts.append(jnp.where(keep, t[u * xbuf.shape[1]:(u + 1) * xbuf.shape[1]], 0.0).astype(jnp.bfloat16))
        y = jnp.dot(jnp.concatenate(parts, axis=0), bbuf[rows], preferred_element_type=jnp.float32)
        for u, pair in enumerate(pairs):
            acc[dst_of(*pair)] += y[u * xbuf.shape[1]:(u + 1) * xbuf.shape[1]]
    @pl.loop(0, steps)
    def _(i):
        near_copy(i).wait()
        for u in range(NEAR_STEP):
            p = i * NEAR_STEP + u
            src = src_of(near_pairs[0, p], near_pairs[1, p], place)
            dst = dst_of(near_pairs[0, p], near_pairs[1, p], place)
            dst = jnp.where(p < count, dst, spare)
            dims = (((1,), (1,)), ((), ())) if flip else (((1,), (0,)), ((), ()))
            acc[dst] += lax.dot_general(xbuf[src], nbuf[p], dims, preferred_element_type=jnp.float32)
    o_copies, first = [], 0
    for k, size in enumerate(splits[1]):
        @pl.loop(first, first + size)
        def _(i):
            obuf[i] = acc[i].astype(jnp.bfloat16)
        copy = pltpu.make_async_copy(obuf.at[pl.ds(first, size)], outs[k], osem.at[k])
        copy.start()
        o_copies.append(copy)
        first += size
    for copy in o_copies:
        copy.wait()

def pair_product(flip, src_of, dst_of, in_sizes, out_sizes, near_pairs, near_count, far_pairs, far_rank, near, proj, back, sources):
    loads, dof = sources[0].shape[1:]
    smem = pl.BlockSpec(memory_space=pltpu.SMEM)
    hbm = pl.BlockSpec(memory_space=pl.ANY)
    n_dst = sum(out_sizes)
    near_n = near.shape[0]
    return pl.pallas_call(
        functools.partial(pair_kernel, flip, src_of, dst_of, (in_sizes, out_sizes)),
        out_shape=[jax.ShapeDtypeStruct((n, loads, dof), jnp.bfloat16) for n in out_sizes],
        in_specs=[smem] * 4 + [hbm] * (3 + len(sources)),
        out_specs=[hbm] * len(out_sizes),
        scratch_shapes=[
            pltpu.VMEM((sum(in_sizes), loads, dof), jnp.bfloat16),
            pltpu.VMEM(near.shape, jnp.bfloat16),
            pltpu.VMEM(proj.shape, jnp.bfloat16),
            pltpu.VMEM(back.shape, jnp.bfloat16),
            pltpu.VMEM((n_dst + 1, loads, dof), jnp.float32),
            pltpu.VMEM((n_dst, loads, dof), jnp.bfloat16),
            pltpu.SemaphoreType.DMA((len(sources),)),
            pltpu.SemaphoreType.DMA((near_n // NEAR_STEP,)),
            pltpu.SemaphoreType.DMA,
            pltpu.SemaphoreType.DMA,
            pltpu.SemaphoreType.DMA((len(out_sizes),)),
        ],
        compiler_params=pltpu.CompilerParams(vmem_limit_bytes=58 * 2**20),
        cost_estimate=pl.CostEstimate(flops=2 * near_n * loads * dof * dof, bytes_accessed=2 * near.size + 4 * proj.size, transcendentals=0),
    )(near_pairs, near_count, far_pairs, far_rank, near, proj, back, *sources)


SIDE = 4
PER = 8


def row_shift(axis, step):
    pairs = []
    for y in range(SIDE):
        for z in range(SIDE):
            far = ((y + step) % SIDE, z) if axis == 0 else (y, (z + step) % SIDE)
            pairs.append((far[0] * SIDE + far[1], y * SIDE + z))
    return pairs


def col_shift(step, other):
    return [((x + step) % SIDE * 2 + (core ^ other), x * 2 + core) for x in range(SIDE) for core in range(2)]


def row_slot(r, place):
    piece = (r // PER) % (2 * SIDE)
    step = (piece // 2 - place[1] // 2 + SIDE) % SIDE
    return step, (piece % 2) ^ (place[1] % 2), r % PER


def src_rows(r, c, place):
    step, other, j = row_slot(r, place)
    return (step * 2 + other) * PER + j


def dst_rows(r, c, place):
    step, other, j = row_slot(r, place)
    return ((1 - other) * SIDE + step) * PER + j


def src_cols(r, c, place):
    return c // (2 * SIDE * PER) * PER + c % PER


HALF_AT = sum(at << (4 * i) for i, at in enumerate((6, 7, 4, 1, 0, 2, 3, 5)))
RING_OUT = (16, 16, 8, 8, 16)


def dst_cols(r, c, place):
    piece = c // (2 * SIDE * PER)
    dy = (piece // SIDE - place[0] // SIDE + SIDE) % SIDE
    dz = (piece % SIDE - place[0] % SIDE + SIDE) % SIDE
    j = c % PER
    late, half, low = j // 4, (j // 2) % 2, j % 2
    first = jnp.where(late == 0, dz, dy)
    second = jnp.where(late == 0, dy, dz)
    at = lax.shift_right_logical(jnp.int32(HALF_AT - (1 << 32) if HALF_AT >= 1 << 31 else HALF_AT), (first * 2 + half) * 4) & 15
    return late * 64 + at * 8 + second * 2 + low


def wide(v):
    return v.astype(jnp.float32)


def narrow(v):
    return v.astype(jnp.bfloat16)


def ring_sum(parts, axis):
    forth, back, forth_own, back_own, own = parts
    go = lambda v, ax, step: lax.ppermute(v, "row", row_shift(ax, step))
    from_low = go(forth, axis, -1)
    from_high = go(back, axis, 1)
    low_two = go(narrow(wide(forth_own) + wide(from_low[:8])), axis, -1)
    high_two = go(narrow(wide(back_own) + wide(from_high[:8])), axis, 1)
    one = wide(own[:8]) + wide(low_two) + wide(from_high[8:])
    two = wide(own[8:]) + wide(from_low[8:]) + wide(high_two)
    block = lambda d: jnp.concatenate([one[2 * d:2 * d + 2], two[2 * d:2 * d + 2]])
    ax = 1 - axis
    return (
        block(0)
        + wide(go(narrow(block(1)), ax, -1))
        + wide(go(narrow(block(2)), ax, 2))
        + wide(go(narrow(block(3)), ax, 1))
    )


def local(
    load_vectors,
    live_panels,
    self_blocks,
    near_pairs,
    near_count,
    near_blocks,
    far_pairs,
    far_rank,
    far_left,
    far_right,
):
    dof = load_vectors.shape[2]
    panel_of = jnp.arange(dof) % (dof // 3)
    live_dofs = (panel_of[None, :] < live_panels[:, None]).astype(jnp.bfloat16)
    masked = load_vectors * live_dofs[:, None, :]
    col_block = lax.all_gather(masked, "row", axis=0, tiled=True)
    swap = lambda v: lax.ppermute(v, "col", col_shift(0, 1))
    rows = []
    for step in range(SIDE):
        there = masked if step == 0 else lax.ppermute(masked, "col", col_shift(step, 0))
        rows += [there, swap(there)]
    left = jnp.swapaxes(far_left, 1, 2).reshape(-1, dof)
    right = jnp.swapaxes(far_right, 1, 2).reshape(-1, dof)
    lists = (near_pairs.T, near_count, far_pairs.T, far_rank, near_blocks)
    to_cols = pair_product(False, src_rows, dst_cols, [PER] * 8, RING_OUT * 2, *lists, left, right, rows)
    to_rows = pair_product(
        True, src_cols, dst_rows, [PER * SIDE * SIDE], (PER * SIDE, PER * SIDE), *lists, right, left, [col_block]
    )
    early = ring_sum(to_cols[:5], 1)
    late = ring_sum(to_cols[5:], 0)
    col_part = jnp.concatenate([early, late])
    row_sum = (wide(to_rows[1]) + wide(swap(to_rows[0]))).reshape((SIDE, PER) + masked.shape[1:])
    row_part = row_sum[0]
    for step in range(1, SIDE):
        row_part = row_part + wide(lax.ppermute(narrow(row_sum[step]), "col", col_shift(-step, 0)))
    own_part = jnp.einsum("cld,ced->cle", masked, self_blocks, preferred_element_type=jnp.float32)
    return (own_part + row_part + col_part) * live_dofs.astype(jnp.float32)[:, None, :]


def solution(mesh):
    spec = P(("row", "col"))
    return jax.shard_map(local, mesh=mesh, in_specs=(spec,) * 10, out_specs=spec, check_vma=False)
```

profile of v0, /device:TPU:1, one launch (start us, length us, event | category | flops | bytes accessed | tf_op | source)
XLA Modules:
  0.0 166.7 jit_solution(10450193730441312337)
XLA Ops:
  6.5 0.9 fusion.12
  7.4 1.8 %broadcast_multiply_fusion.refs_0_ = bf16[8,64,384]{2,1,0:T(8,128)(2,1)} fusion(bf16[8,64,384]{2,1,0:T(8,128)(2,1)} %param.10, bf16[8,384]{1,0:T(8,128)(2,1)S(1)} %get-tuple-element.59), kind=kLoop, calls=%fused_computation.27 | loop fusion | flops 196608 | bytes 792576 | tf_op jit(solution)/shard_map/mul | solution.py:207
  9.2 0.0 all-gather.2.cloned.1.call-update
  9.2 2.1 %collective-permute-start.9 = (bf16[8,64,384]{2,1,0:T(8,128)(2,1)}, bf16[8,64,384]{2,1,0:T(8,128)(2,1)S(1)}, u32[]{:S(2)}, u32[]{:S(2)}) collective-permute-start(bf16[8,64,384]{2,1,0:T(8,128)(2,1)} %broadcast_multiply_fusion.refs_0_), channel_id=1, source_target_pairs={{6,0},{7,1},{0,2},{1,3},{2,4},{3,5},{4,6},{5,7},{14,8},{15,9},{8,1... | collective-permute-start | bytes 1179656 | tf_op jit(solution)/shard_map/ppermute | solution.py:212
  11.3 1.3 collective-permute-start.5
  12.7 1.7 collective-permute-start.7
  14.4 1.5 collective-permute-start.4
  15.9 5.4 %collective-permute-done.9.refs_6_ = bf16[8,64,384]{2,1,0:T(8,128)(2,1)S(1)} collective-permute-done((bf16[8,64,384]{2,1,0:T(8,128)(2,1)}, bf16[8,64,384]{2,1,0:T(8,128)(2,1)S(1)}, u32[]{:S(2)}, u32[]{:S(2)}) %collective-permute-start.9) | collective-permute-done | bytes 393248 | tf_op jit(solution)/shard_map/ppermute | solution.py:212
  21.2 1.7 %collective-permute-start.10 = (bf16[8,64,384]{2,1,0:T(8,128)(2,1)S(1)}, bf16[8,64,384]{2,1,0:T(8,128)(2,1)S(1)}, u32[]{:S(2)}, u32[]{:S(2)}) collective-permute-start(bf16[8,64,384]{2,1,0:T(8,128)(2,1)S(1)} %collective-permute-done.9.refs_6_), channel_id=1, source_target_pairs={{1,0},{0,1},{3,2},{2,3},{5,4},{4,5},{7,6},{6,7},{9,8},{8,9},{11,10... | collective-permute-start | bytes 1179656 | tf_op jit(solution)/shard_map/ppermute | solution.py:209
  22.9 0.0 collective-permute-done.5.refs_2_
  22.9 1.7 collective-permute-start.6
  24.6 6.4 %collective-permute-done.7.refs_4_ = bf16[8,64,384]{2,1,0:T(8,128)(2,1)S(1)} collective-permute-done((bf16[8,64,384]{2,1,0:T(8,128)(2,1)}, bf16[8,64,384]{2,1,0:T(8,128)(2,1)S(1)}, u32[]{:S(2)}, u32[]{:S(2)}) %collective-permute-start.7) | collective-permute-done | bytes 393248 | tf_op jit(solution)/shard_map/ppermute | solution.py:212
  30.9 1.5 collective-permute-start.8
  33.1 0.0 collective-permute-done.4.refs_1_
  33.2 0.0 collective-permute-done.6.refs_3_
  33.2 0.6 collective-permute-done.8.refs_5_
  33.9 0.1 copy-done.20
  34.0 0.1 copy-done.21
  34.1 0.1 copy-done.22
  34.2 0.4 copy-done.23
  34.6 16.2 %shard_map.101 = (bf16[16,64,384]{2,1,0:T(8,128)(2,1)}, bf16[16,64,384]{2,1,0:T(8,128)(2,1)}, bf16[8,64,384]{2,1,0:T(8,128)(2,1)}, bf16[8,64,384]{2,1,0:T(8,128)...) custom-call(s32[2,48]{1,0:T(2,128)} %bitcast.14, ...), custom_call_target="tpu_custom_call" | custom-call | flops 905969664 | bytes 18874368 | tf_op jit(solution)/shard_map/pallas_call | solution.py:89
  50.9 4.9 %collective-permute-start.11 = (bf16[16,64,384]{2,1,0:T(8,128)(2,1)}, bf16[16,64,384]{2,1,0:T(8,128)(2,1)S(1)}, u32[]{:S(2)}, u32[]{:S(2)}) collective-permute-start(bf16[16,64,384]{2,1,0:T(8,128)(2,1)} %get-tuple-element.21), channel_id=1, source_target_pairs={{24,0},{0,8},{8,16},{16,24},{56,32},{32,40},{40,48},{48,56},{88,64... | collective-permute-start | bytes 2359304 | tf_op jit(solution)/shard_map/ppermute | solution.py:175
  55.8 1.7 %collective-permute-start.20 = (bf16[16,64,384]{2,1,0:T(8,128)(2,1)}, bf16[16,64,384]{2,1,0:T(8,128)(2,1)S(1)}, u32[]{:S(2)}, u32[]{:S(2)}) collective-permute-start(bf16[16,64,384]{2,1,0:T(8,128)(2,1)} %get-tuple-element.27), channel_id=1, source_target_pairs={{32,0},{40,8},{48,16},{56,24},{64,32},{72,40},{80,48},{88,56},{96,... | collective-permute-start | bytes 2359304 | tf_op jit(solution)/shard_map/ppermute | solution.py:175
  57.5 1.8 %collective-permute-start.18 = (bf16[16,64,384]{2,1,0:T(8,128)(2,1)}, bf16[16,64,384]{2,1,0:T(8,128)(2,1)S(1)}, u32[]{:S(2)}, u32[]{:S(2)}) collective-permute-start(bf16[16,64,384]{2,1,0:T(8,128)(2,1)} %get-tuple-element.26), channel_id=1, source_target_pairs={{96,0},{104,8},{112,16},{120,24},{0,32},{8,40},{16,48},{24,56},{32... | collective-permute-start | bytes 2359304 | tf_op jit(solution)/shard_map/ppermute | solution.py:175
  59.3 0.9 fusion.23
  60.3 28.3 %collective-permute-done.11 = bf16[16,64,384]{2,1,0:T(8,128)(2,1)S(1)} collective-permute-done((bf16[16,64,384]{2,1,0:T(8,128)(2,1)}, bf16[16,64,384]{2,1,0:T(8,128)(2,1)S(1)}, u32[]{:S(2)}, u32[]{:S(2)}) %collective-permute-start.11) | collective-permute-done | bytes 786464 | tf_op jit(solution)/shard_map/ppermute | solution.py:175
  88.5 1.0 add_convert_fusion.3
  89.5 0.9 collective-permute-start.12
  90.4 0.0 collective-permute-done.13
  90.4 1.0 add_convert_fusion.2
  91.4 1.8 %collective-permute-start.14 = (bf16[8,64,384]{2,1,0:T(8,128)(2,1)}, bf16[8,64,384]{2,1,0:T(8,128)(2,1)}, u32[]{:S(2)}, u32[]{:S(2)}) collective-permute-start(bf16[8,64,384]{2,1,0:T(8,128)(2,1)} %add_convert_fusion.2), channel_id=1, source_target_pairs={{8,0},{16,8},{24,16},{0,24},{40,32},{48,40},{56,48},{32,56},{72,64... | collective-permute-start | bytes 1179656 | tf_op jit(solution)/shard_map/ppermute | solution.py:175
  93.2 0.9 copy-done.5
  94.0 0.9 add_convert_fusion
  94.9 3.8 %collective-permute-start.21 = (bf16[8,64,384]{2,1,0:T(8,128)(2,1)}, bf16[8,64,384]{2,1,0:T(8,128)(2,1)}, u32[]{:S(2)}, u32[]{:S(2)}) collective-permute-start(bf16[8,64,384]{2,1,0:T(8,128)(2,1)} %add_convert_fusion), channel_id=1, source_target_pairs={{32,0},{40,8},{48,16},{56,24},{64,32},{72,40},{80,48},{88,56},{96,... | collective-permute-start | bytes 1179656 | tf_op jit(solution)/shard_map/ppermute | solution.py:175
  98.7 0.9 copy-done.7
  99.6 0.8 add_convert_fusion.1
  100.5 0.0 all-gather.2.cloned.1.call-done.refs_0_
  100.5 16.3 %shard_map.100 = (bf16[32,64,384]{2,1,0:T(8,128)(2,1)}, bf16[32,64,384]{2,1,0:T(8,128)(2,1)}) custom-call(s32[2,48]{1,0:T(2,128)} %bitcast.15, s32[1]{0:T(128)S(6)} %copy.11.near_count, s32[2,96]{1,0:T(2,128)} %bitcast.17, s32[96]{0:T(128)} %far_rank.3, bf16[48,384,384]{2,1,0:T(8,128)(2,1)} %near.3, bf16[3072,384]{1,0:T(8,128)(2,1)} %bitcast.11, ...), custom_call_target="tpu_custom_call" | custom-call | flops 905969664 | bytes 18874368 | tf_op jit(solution)/shard_map/pallas_call | solution.py:89
  116.8 8.0 %collective-permute-start = (bf16[32,64,384]{2,1,0:T(8,128)(2,1)}, bf16[32,64,384]{2,1,0:T(8,128)(2,1)S(1)}, u32[]{:S(2)}, u32[]{:S(2)}) collective-permute-start(bf16[32,64,384]{2,1,0:T(8,128)(2,1)} %get-tuple-element.18), channel_id=1, source_target_pairs={{1,0},{0,1},{3,2},{2,3},{5,4},{4,5},{7,6},{6,7},{9,8},{8,9},{11,10... | collective-permute-start | bytes 4718600 | tf_op jit(solution)/shard_map/ppermute | solution.py:209
  124.9 1.4 fusion.14
  126.3 0.0 copy-start.6
  126.3 0.1 fusion.19
  126.4 0.1 collective-permute-start.15
  126.5 0.1 collective-permute-start.16
  126.7 0.0 collective-permute-done.21
  126.7 2.7 %collective-permute-start.17 = (bf16[4,64,384]{2,1,0:T(8,128)(2,1)S(1)}, bf16[4,64,384]{2,1,0:T(8,128)(2,1)S(1)}, u32[]{:S(2)}, u32[]{:S(2)}) collective-permute-start(bf16[4,64,384]{2,1,0:T(8,128)(2,1)S(1)} %pad_maximum_fusion.2), channel_id=1, source_target_pairs={{32,0},{40,8},{48,16},{56,24},{64,32},{72,40},{80,48},{88,56},{96,... | collective-permute-start | bytes 589832 | tf_op jit(solution)/shard_map/ppermute | solution.py:175
  129.4 1.4 fusion.16
  130.9 0.1 fusion.21
  131.0 0.1 collective-permute-start.22
  131.2 1.4 collective-permute-start.23
  132.7 0.7 fusion.13
  133.3 0.1 fusion.18
  133.5 4.9 %collective-permute-done.15 = bf16[4,64,384]{2,1,0:T(8,128)(2,1)S(1)} collective-permute-done((bf16[4,64,384]{2,1,0:T(8,128)(2,1)S(1)}, bf16[4,64,384]{2,1,0:T(8,128)(2,1)S(1)}, u32[]{:S(2)}, u32[]{:S(2)}) %collective-permute-start.15) | collective-permute-done | bytes 196640 | tf_op jit(solution)/shard_map/ppermute | solution.py:175
  138.4 1.4 collective-permute-start.1
  139.7 0.9 collective-permute-start.2
  140.6 1.7 %collective-permute-done.22 = bf16[4,64,384]{2,1,0:T(8,128)(2,1)S(1)} collective-permute-done((bf16[4,64,384]{2,1,0:T(8,128)(2,1)S(1)}, bf16[4,64,384]{2,1,0:T(8,128)(2,1)S(1)}, u32[]{:S(2)}, u32[]{:S(2)}) %collective-permute-start.22) | collective-permute-done | bytes 196640 | tf_op jit(solution)/shard_map/ppermute | solution.py:175
  142.3 0.2 collective-permute-start.3
  142.5 0.1 fusion.6
  142.6 1.4 collective-permute-done.24
  144.0 0.1 fusion.8
  144.1 6.3 %collective-permute-done.1 = bf16[8,64,384]{2,1,0:T(8,128)(2,1)S(1)} collective-permute-done((bf16[8,64,384]{2,1,0:T(8,128)(2,1)S(1)}, bf16[8,64,384]{2,1,0:T(8,128)(2,1)S(1)}, u32[]{:S(2)}, u32[]{:S(2)}) %collective-permute-start.1) | collective-permute-done | bytes 393248 | tf_op jit(solution)/shard_map/ppermute | solution.py:227
  150.4 6.5 %collective-permute-done.2 = bf16[8,64,384]{2,1,0:T(8,128)(2,1)S(1)} collective-permute-done((bf16[8,64,384]{2,1,0:T(8,128)(2,1)S(1)}, bf16[8,64,384]{2,1,0:T(8,128)(2,1)S(1)}, u32[]{:S(2)}, u32[]{:S(2)}) %collective-permute-start.2) | collective-permute-done | bytes 393248 | tf_op jit(solution)/shard_map/ppermute | solution.py:227
  156.9 1.7 %collective-permute-done.3 = bf16[8,64,384]{2,1,0:T(8,128)(2,1)S(1)} collective-permute-done((bf16[8,64,384]{2,1,0:T(8,128)(2,1)S(1)}, bf16[8,64,384]{2,1,0:T(8,128)(2,1)S(1)}, u32[]{:S(2)}, u32[]{:S(2)}) %collective-permute-start.3) | collective-permute-done | bytes 393248 | tf_op jit(solution)/shard_map/ppermute | solution.py:227
  158.6 1.2 fusion.4
  (66 shorter events, 0.3 us)
Async XLA Ops:
  6.5 52.8 %copy-start = (bf16[8,384,384]{2,1,0:T(8,128)(2,1)S(1)}, bf16[8,384,384]{2,1,0:T(8,128)(2,1)}, u32[]{:S(2)}) copy-start(bf16[8,384,384]{2,1,0:T(8,128)(2,1)} %param.12) | copy-start | bytes 7077892
  6.5 93.9 %all-gather.2.cloned.1.call-start = ((), (), s32[]{:S(2)}) async-start(), calls=%async_computation | async-start | bytes 6684672 | tf_op jit(solution)/shard_map/all_gather | solution.py:208
  9.2 12.0 %collective-permute-start.9 = (bf16[8,64,384]{2,1,0:T(8,128)(2,1)}, bf16[8,64,384]{2,1,0:T(8,128)(2,1)S(1)}, u32[]{:S(2)}, u32[]{:S(2)}) collective-permute-start(bf16[8,64,384]{2,1,0:T(8,128)(2,1)} %broadcast_multiply_fusion.refs_0_), channel_id=1, source_target_pairs={{6,0},{7,1},{0,2},{1,3},{2,4},{3,5},{4,6},{5,7},{14,8},{15,9},{8,1... | collective-permute-start | bytes 1179656 | tf_op jit(solution)/shard_map/ppermute | solution.py:212
  11.3 11.6 %collective-permute-start.5 = (bf16[8,64,384]{2,1,0:T(8,128)(2,1)}, bf16[8,64,384]{2,1,0:T(8,128)(2,1)S(1)}, u32[]{:S(2)}, u32[]{:S(2)}) collective-permute-start(bf16[8,64,384]{2,1,0:T(8,128)(2,1)} %broadcast_multiply_fusion.refs_0_), channel_id=1, source_target_pairs={{2,0},{3,1},{4,2},{5,3},{6,4},{7,5},{0,6},{1,7},{10,8},{11,9},{12,... | collective-permute-start | bytes 1179656 | tf_op jit(solution)/shard_map/ppermute | solution.py:212
  12.7 18.3 %collective-permute-start.7 = (bf16[8,64,384]{2,1,0:T(8,128)(2,1)}, bf16[8,64,384]{2,1,0:T(8,128)(2,1)S(1)}, u32[]{:S(2)}, u32[]{:S(2)}) collective-permute-start(bf16[8,64,384]{2,1,0:T(8,128)(2,1)} %broadcast_multiply_fusion.refs_0_), channel_id=1, source_target_pairs={{4,0},{5,1},{6,2},{7,3},{0,4},{1,5},{2,6},{3,7},{12,8},{13,9},{14,... | collective-permute-start | bytes 1179656 | tf_op jit(solution)/shard_map/ppermute | solution.py:212
  14.4 18.8 %collective-permute-start.4 = (bf16[8,64,384]{2,1,0:T(8,128)(2,1)}, bf16[8,64,384]{2,1,0:T(8,128)(2,1)S(1)}, u32[]{:S(2)}, u32[]{:S(2)}) collective-permute-start(bf16[8,64,384]{2,1,0:T(8,128)(2,1)} %broadcast_multiply_fusion.refs_0_), channel_id=1, source_target_pairs={{1,0},{0,1},{3,2},{2,3},{5,4},{4,5},{7,6},{6,7},{9,8},{8,9},{11,10... | collective-permute-start | bytes 1179656 | tf_op jit(solution)/shard_map/ppermute | solution.py:209
  21.2 12.6 %copy-start.17 = (bf16[8,64,384]{2,1,0:T(8,128)(2,1)}, bf16[8,64,384]{2,1,0:T(8,128)(2,1)S(1)}, u32[]{:S(2)}) copy-start(bf16[8,64,384]{2,1,0:T(8,128)(2,1)S(1)} %collective-permute-done.9.refs_6_) | copy-start | bytes 1179652
  21.2 12.0 %collective-permute-start.10 = (bf16[8,64,384]{2,1,0:T(8,128)(2,1)S(1)}, bf16[8,64,384]{2,1,0:T(8,128)(2,1)S(1)}, u32[]{:S(2)}, u32[]{:S(2)}) collective-permute-start(bf16[8,64,384]{2,1,0:T(8,128)(2,1)S(1)} %collective-permute-done.9.refs_6_), channel_id=1, source_target_pairs={{1,0},{0,1},{3,2},{2,3},{5,4},{4,5},{7,6},{6,7},{9,8},{8,9},{11,10... | collective-permute-start | bytes 1179656 | tf_op jit(solution)/shard_map/ppermute | solution.py:209
  22.9 11.0 %copy-start.18 = (bf16[8,64,384]{2,1,0:T(8,128)(2,1)}, bf16[8,64,384]{2,1,0:T(8,128)(2,1)S(1)}, u32[]{:S(2)}) copy-start(bf16[8,64,384]{2,1,0:T(8,128)(2,1)S(1)} %collective-permute-done.5.refs_2_) | copy-start | bytes 1179652
  22.9 10.3 %collective-permute-start.6 = (bf16[8,64,384]{2,1,0:T(8,128)(2,1)S(1)}, bf16[8,64,384]{2,1,0:T(8,128)(2,1)S(1)}, u32[]{:S(2)}, u32[]{:S(2)}) collective-permute-start(bf16[8,64,384]{2,1,0:T(8,128)(2,1)S(1)} %collective-permute-done.5.refs_2_), channel_id=1, source_target_pairs={{1,0},{0,1},{3,2},{2,3},{5,4},{4,5},{7,6},{6,7},{9,8},{8,9},{11,10... | collective-permute-start | bytes 1179656 | tf_op jit(solution)/shard_map/ppermute | solution.py:209
  30.9 2.9 %copy-start.19 = (bf16[8,64,384]{2,1,0:T(8,128)(2,1)}, bf16[8,64,384]{2,1,0:T(8,128)(2,1)S(1)}, u32[]{:S(2)}) copy-start(bf16[8,64,384]{2,1,0:T(8,128)(2,1)S(1)} %collective-permute-done.7.refs_4_) | copy-start | bytes 1179652
  30.9 2.9 %collective-permute-start.8 = (bf16[8,64,384]{2,1,0:T(8,128)(2,1)S(1)}, bf16[8,64,384]{2,1,0:T(8,128)(2,1)S(1)}, u32[]{:S(2)}, u32[]{:S(2)}) collective-permute-start(bf16[8,64,384]{2,1,0:T(8,128)(2,1)S(1)} %collective-permute-done.7.refs_4_), channel_id=1, source_target_pairs={{1,0},{0,1},{3,2},{2,3},{5,4},{4,5},{7,6},{6,7},{9,8},{8,9},{11,10... | collective-permute-start | bytes 1179656 | tf_op jit(solution)/shard_map/ppermute | solution.py:209
  33.2 0.8 copy-start.20
  33.2 0.9 copy-start.21
  33.2 1.0 copy-start.22
  33.8 0.8 copy-start.23
  34.6 24.7 %copy-start.1 = (bf16[8,64,384]{2,1,0:T(8,128)(2,1)S(1)}, bf16[8,64,384]{2,1,0:T(8,128)(2,1)}, u32[]{:S(2)}) copy-start(bf16[8,64,384]{2,1,0:T(8,128)(2,1)} %broadcast_multiply_fusion.refs_0_) | copy-start | bytes 1179652
  50.9 37.7 %copy-start.16 = (bf16[8,64,384]{2,1,0:T(8,128)(2,1)S(1)}, bf16[8,64,384]{2,1,0:T(8,128)(2,1)}, u32[]{:S(2)}) copy-start(bf16[8,64,384]{2,1,0:T(8,128)(2,1)} %get-tuple-element.20) | copy-start | bytes 1179652
  50.9 37.7 %collective-permute-start.11 = (bf16[16,64,384]{2,1,0:T(8,128)(2,1)}, bf16[16,64,384]{2,1,0:T(8,128)(2,1)S(1)}, u32[]{:S(2)}, u32[]{:S(2)}) collective-permute-start(bf16[16,64,384]{2,1,0:T(8,128)(2,1)} %get-tuple-element.21), channel_id=1, source_target_pairs={{24,0},{0,8},{8,16},{16,24},{56,32},{32,40},{40,48},{48,56},{88,64... | collective-permute-start | bytes 2359304 | tf_op jit(solution)/shard_map/ppermute | solution.py:175
  55.8 34.6 %collective-permute-start.13 = (bf16[16,64,384]{2,1,0:T(8,128)(2,1)}, bf16[16,64,384]{2,1,0:T(8,128)(2,1)S(1)}, u32[]{:S(2)}, u32[]{:S(2)}) collective-permute-start(bf16[16,64,384]{2,1,0:T(8,128)(2,1)} %get-tuple-element.22), channel_id=1, source_target_pairs={{8,0},{16,8},{24,16},{0,24},{40,32},{48,40},{56,48},{32,56},{72,64... | collective-permute-start | bytes 2359304 | tf_op jit(solution)/shard_map/ppermute | solution.py:175
  55.8 37.3 %collective-permute-start.20 = (bf16[16,64,384]{2,1,0:T(8,128)(2,1)}, bf16[16,64,384]{2,1,0:T(8,128)(2,1)S(1)}, u32[]{:S(2)}, u32[]{:S(2)}) collective-permute-start(bf16[16,64,384]{2,1,0:T(8,128)(2,1)} %get-tuple-element.27), channel_id=1, source_target_pairs={{32,0},{40,8},{48,16},{56,24},{64,32},{72,40},{80,48},{88,56},{96,... | collective-permute-start | bytes 2359304 | tf_op jit(solution)/shard_map/ppermute | solution.py:175
  57.5 32.9 %copy-start.15 = (bf16[8,64,384]{2,1,0:T(8,128)(2,1)S(1)}, bf16[8,64,384]{2,1,0:T(8,128)(2,1)}, u32[]{:S(2)}) copy-start(bf16[8,64,384]{2,1,0:T(8,128)(2,1)} %get-tuple-element.23) | copy-start | bytes 1179652
  57.5 36.5 %copy-start.14 = (bf16[8,64,384]{2,1,0:T(8,128)(2,1)S(1)}, bf16[8,64,384]{2,1,0:T(8,128)(2,1)}, u32[]{:S(2)}) copy-start(bf16[8,64,384]{2,1,0:T(8,128)(2,1)} %get-tuple-element.28) | copy-start | bytes 1179652
  57.5 41.2 %collective-permute-start.18 = (bf16[16,64,384]{2,1,0:T(8,128)(2,1)}, bf16[16,64,384]{2,1,0:T(8,128)(2,1)S(1)}, u32[]{:S(2)}, u32[]{:S(2)}) collective-permute-start(bf16[16,64,384]{2,1,0:T(8,128)(2,1)} %get-tuple-element.26), channel_id=1, source_target_pairs={{96,0},{104,8},{112,16},{120,24},{0,32},{8,40},{16,48},{24,56},{32... | collective-permute-start | bytes 2359304 | tf_op jit(solution)/shard_map/ppermute | solution.py:175
  60.3 39.3 %copy-start.13 = (bf16[8,64,384]{2,1,0:T(8,128)(2,1)S(1)}, bf16[8,64,384]{2,1,0:T(8,128)(2,1)}, u32[]{:S(2)}) copy-start(bf16[8,64,384]{2,1,0:T(8,128)(2,1)} %get-tuple-element.25) | copy-start | bytes 1179652
  88.5 11.9 %copy-start.9 = (bf16[16,64,384]{2,1,0:T(8,128)(2,1)}, bf16[16,64,384]{2,1,0:T(8,128)(2,1)S(1)}, u32[]{:S(2)}) copy-start(bf16[16,64,384]{2,1,0:T(8,128)(2,1)S(1)} %collective-permute-done.11) | copy-start | bytes 2359300
  89.5 35.3 %collective-permute-start.12 = (bf16[8,64,384]{2,1,0:T(8,128)(2,1)}, bf16[8,64,384]{2,1,0:T(8,128)(2,1)S(1)}, u32[]{:S(2)}, u32[]{:S(2)}) collective-permute-start(bf16[8,64,384]{2,1,0:T(8,128)(2,1)} %add_convert_fusion.3), channel_id=1, source_target_pairs={{24,0},{0,8},{8,16},{16,24},{56,32},{32,40},{40,48},{48,56},{88,64... | collective-permute-start | bytes 1179656 | tf_op jit(solution)/shard_map/ppermute | solution.py:175
  90.4 10.0 %copy-start.11 = (bf16[16,64,384]{2,1,0:T(8,128)(2,1)}, bf16[16,64,384]{2,1,0:T(8,128)(2,1)S(1)}, u32[]{:S(2)}) copy-start(bf16[16,64,384]{2,1,0:T(8,128)(2,1)S(1)} %collective-permute-done.13) | copy-start | bytes 2359300
  91.4 33.4 %collective-permute-start.14 = (bf16[8,64,384]{2,1,0:T(8,128)(2,1)}, bf16[8,64,384]{2,1,0:T(8,128)(2,1)}, u32[]{:S(2)}, u32[]{:S(2)}) collective-permute-start(bf16[8,64,384]{2,1,0:T(8,128)(2,1)} %add_convert_fusion.2), channel_id=1, source_target_pairs={{8,0},{16,8},{24,16},{0,24},{40,32},{48,40},{56,48},{32,56},{72,64... | collective-permute-start | bytes 1179656 | tf_op jit(solution)/shard_map/ppermute | solution.py:175
  93.2 0.9 copy-start.5
  94.9 31.8 %collective-permute-start.21 = (bf16[8,64,384]{2,1,0:T(8,128)(2,1)}, bf16[8,64,384]{2,1,0:T(8,128)(2,1)}, u32[]{:S(2)}, u32[]{:S(2)}) collective-permute-start(bf16[8,64,384]{2,1,0:T(8,128)(2,1)} %add_convert_fusion), channel_id=1, source_target_pairs={{32,0},{40,8},{48,16},{56,24},{64,32},{72,40},{80,48},{88,56},{96,... | collective-permute-start | bytes 1179656 | tf_op jit(solution)/shard_map/ppermute | solution.py:175
  98.7 0.9 copy-start.7
  100.5 29.0 %collective-permute-start.19 = (bf16[8,64,384]{2,1,0:T(8,128)(2,1)}, bf16[8,64,384]{2,1,0:T(8,128)(2,1)}, u32[]{:S(2)}, u32[]{:S(2)}) collective-permute-start(bf16[8,64,384]{2,1,0:T(8,128)(2,1)} %add_convert_fusion.1), channel_id=1, source_target_pairs={{96,0},{104,8},{112,16},{120,24},{0,32},{8,40},{16,48},{24,56},{32... | collective-permute-start | bytes 1179656 | tf_op jit(solution)/shard_map/ppermute | solution.py:175
  100.5 24.3 %copy-start.4 = (bf16[16,64,384]{2,1,0:T(8,128)(2,1)S(1)}, bf16[16,64,384]{2,1,0:T(8,128)(2,1)}, u32[]{:S(2)}) copy-start(bf16[16,64,384]{2,1,0:T(8,128)(2,1)} %get-tuple-element.19) | copy-start | bytes 2359300
  100.5 24.3 %copy-start.10 = (bf16[16,64,384]{2,1,0:T(8,128)(2,1)S(1)}, bf16[16,64,384]{2,1,0:T(8,128)(2,1)}, u32[]{:S(2)}) copy-start(bf16[16,64,384]{2,1,0:T(8,128)(2,1)} %copy-done.9) | copy-start | bytes 2359300
  100.5 24.3 %copy-start.12 = (bf16[16,64,384]{2,1,0:T(8,128)(2,1)S(1)}, bf16[16,64,384]{2,1,0:T(8,128)(2,1)}, u32[]{:S(2)}) copy-start(bf16[16,64,384]{2,1,0:T(8,128)(2,1)} %copy-done.11) | copy-start | bytes 2359300
  116.8 14.4 %collective-permute-start = (bf16[32,64,384]{2,1,0:T(8,128)(2,1)}, bf16[32,64,384]{2,1,0:T(8,128)(2,1)S(1)}, u32[]{:S(2)}, u32[]{:S(2)}) collective-permute-start(bf16[32,64,384]{2,1,0:T(8,128)(2,1)} %get-tuple-element.18), channel_id=1, source_target_pairs={{1,0},{0,1},{3,2},{2,3},{5,4},{4,5},{7,6},{6,7},{9,8},{8,9},{11,10... | collective-permute-start | bytes 4718600 | tf_op jit(solution)/shard_map/ppermute | solution.py:209
  126.2 3.2 %copy-start.3 = (bf16[16,64,384]{2,1,0:T(8,128)(2,1)S(1)}, bf16[16,64,384]{2,1,0:T(8,128)(2,1)}, u32[]{:S(2)}) copy-start(bf16[16,64,384]{2,1,0:T(8,128)(2,1)} %get-tuple-element.24) | copy-start | bytes 2359300
  126.3 3.2 %copy-start.6 = (bf16[16,64,384]{2,1,0:T(8,128)(2,1)S(1)}, bf16[16,64,384]{2,1,0:T(8,128)(2,1)}, u32[]{:S(2)}) copy-start(bf16[16,64,384]{2,1,0:T(8,128)(2,1)} %copy-done.5) | copy-start | bytes 2359300
  126.3 3.2 %copy-start.8 = (bf16[16,64,384]{2,1,0:T(8,128)(2,1)S(1)}, bf16[16,64,384]{2,1,0:T(8,128)(2,1)}, u32[]{:S(2)}) copy-start(bf16[16,64,384]{2,1,0:T(8,128)(2,1)} %copy-done.7) | copy-start | bytes 2359300
  126.4 12.0 %collective-permute-start.15 = (bf16[4,64,384]{2,1,0:T(8,128)(2,1)S(1)}, bf16[4,64,384]{2,1,0:T(8,128)(2,1)S(1)}, u32[]{:S(2)}, u32[]{:S(2)}) collective-permute-start(bf16[4,64,384]{2,1,0:T(8,128)(2,1)S(1)} %pad_maximum_fusion), channel_id=1, source_target_pairs={{96,0},{104,8},{112,16},{120,24},{0,32},{8,40},{16,48},{24,56},{32... | collective-permute-start | bytes 589832 | tf_op jit(solution)/shard_map/ppermute | solution.py:175
  126.5 11.9 %collective-permute-start.16 = (bf16[4,64,384]{2,1,0:T(8,128)(2,1)S(1)}, bf16[4,64,384]{2,1,0:T(8,128)(2,1)S(1)}, u32[]{:S(2)}, u32[]{:S(2)}) collective-permute-start(bf16[4,64,384]{2,1,0:T(8,128)(2,1)S(1)} %pad_maximum_fusion.1), channel_id=1, source_target_pairs={{64,0},{72,8},{80,16},{88,24},{96,32},{104,40},{112,48},{120,56},{... | collective-permute-start | bytes 589832 | tf_op jit(solution)/shard_map/ppermute | solution.py:175
  126.7 13.1 %collective-permute-start.17 = (bf16[4,64,384]{2,1,0:T(8,128)(2,1)S(1)}, bf16[4,64,384]{2,1,0:T(8,128)(2,1)S(1)}, u32[]{:S(2)}, u32[]{:S(2)}) collective-permute-start(bf16[4,64,384]{2,1,0:T(8,128)(2,1)S(1)} %pad_maximum_fusion.2), channel_id=1, source_target_pairs={{32,0},{40,8},{48,16},{56,24},{64,32},{72,40},{80,48},{88,56},{96,... | collective-permute-start | bytes 589832 | tf_op jit(solution)/shard_map/ppermute | solution.py:175
  130.9 1.8 %copy-start.2 = (bf16[32,64,384]{2,1,0:T(8,128)(2,1)S(1)}, bf16[32,64,384]{2,1,0:T(8,128)(2,1)}, u32[]{:S(2)}) copy-start(bf16[32,64,384]{2,1,0:T(8,128)(2,1)} %get-tuple-element.17) | copy-start | bytes 4718596
  131.0 11.4 %collective-permute-start.22 = (bf16[4,64,384]{2,1,0:T(8,128)(2,1)S(1)}, bf16[4,64,384]{2,1,0:T(8,128)(2,1)S(1)}, u32[]{:S(2)}, u32[]{:S(2)}) collective-permute-start(bf16[4,64,384]{2,1,0:T(8,128)(2,1)S(1)} %pad_maximum_fusion.3), channel_id=1, source_target_pairs={{24,0},{0,8},{8,16},{16,24},{56,32},{32,40},{40,48},{48,56},{88,64... | collective-permute-start | bytes 589832 | tf_op jit(solution)/shard_map/ppermute | solution.py:175
  131.2 11.4 %collective-permute-start.23 = (bf16[4,64,384]{2,1,0:T(8,128)(2,1)S(1)}, bf16[4,64,384]{2,1,0:T(8,128)(2,1)S(1)}, u32[]{:S(2)}, u32[]{:S(2)}) collective-permute-start(bf16[4,64,384]{2,1,0:T(8,128)(2,1)S(1)} %pad_maximum_fusion.4), channel_id=1, source_target_pairs={{16,0},{24,8},{0,16},{8,24},{48,32},{56,40},{32,48},{40,56},{80,64... | collective-permute-start | bytes 589832 | tf_op jit(solution)/shard_map/ppermute | solution.py:175
  138.4 5.6 %collective-permute-start.24 = (bf16[4,64,384]{2,1,0:T(8,128)(2,1)S(1)}, bf16[4,64,384]{2,1,0:T(8,128)(2,1)S(1)}, u32[]{:S(2)}, u32[]{:S(2)}) collective-permute-start(bf16[4,64,384]{2,1,0:T(8,128)(2,1)S(1)} %pad_maximum_fusion.5), channel_id=1, source_target_pairs={{8,0},{16,8},{24,16},{0,24},{40,32},{48,40},{56,48},{32,56},{72,64... | collective-permute-start | bytes 589832 | tf_op jit(solution)/shard_map/ppermute | solution.py:175
  138.4 12.0 %collective-permute-start.1 = (bf16[8,64,384]{2,1,0:T(8,128)(2,1)S(1)}, bf16[8,64,384]{2,1,0:T(8,128)(2,1)S(1)}, u32[]{:S(2)}, u32[]{:S(2)}) collective-permute-start(bf16[8,64,384]{2,1,0:T(8,128)(2,1)S(1)} %get-tuple-element.39), channel_id=1, source_target_pairs={{6,0},{7,1},{0,2},{1,3},{2,4},{3,5},{4,6},{5,7},{14,8},{15,9},{8,1... | collective-permute-start | bytes 1179656 | tf_op jit(solution)/shard_map/ppermute | solution.py:227
  139.7 17.1 %collective-permute-start.2 = (bf16[8,64,384]{2,1,0:T(8,128)(2,1)S(1)}, bf16[8,64,384]{2,1,0:T(8,128)(2,1)S(1)}, u32[]{:S(2)}, u32[]{:S(2)}) collective-permute-start(bf16[8,64,384]{2,1,0:T(8,128)(2,1)S(1)} %get-tuple-element.41), channel_id=1, source_target_pairs={{4,0},{5,1},{6,2},{7,3},{0,4},{1,5},{2,6},{3,7},{12,8},{13,9},{14,... | collective-permute-start | bytes 1179656 | tf_op jit(solution)/shard_map/ppermute | solution.py:227
  142.3 16.3 %collective-permute-start.3 = (bf16[8,64,384]{2,1,0:T(8,128)(2,1)S(1)}, bf16[8,64,384]{2,1,0:T(8,128)(2,1)S(1)}, u32[]{:S(2)}, u32[]{:S(2)}) collective-permute-start(bf16[8,64,384]{2,1,0:T(8,128)(2,1)S(1)} %get-tuple-element.40), channel_id=1, source_target_pairs={{2,0},{3,1},{4,2},{5,3},{6,4},{7,5},{0,6},{1,7},{10,8},{11,9},{12,... | collective-permute-start | bytes 1179656 | tf_op jit(solution)/shard_map/ppermute | solution.py:227
Sparse Core Ops, SparseCore 0:
  9.5 80.4 all-gather.1
where the time goes:
time: 167 us
  waiting for transfers between devices  63.3 us (38%)
  starting transfers between devices  41.3 us (25%)
  Pallas kernels  32.5 us (19%)
  between operations  14.4 us (9%)
  other arithmetic  11.3 us (7%)
  local copies, waits for them, and re-layouts  2.91 us (2%)
    ppermute x14, waiting for transfers between devices, ring_sum(): go = lambda v, ax, step: lax.ppermute(v, 'row', row_shift(ax, step))  36.3 us
    pallas_call x2, Pallas kernels, pair_product(): pl.pallas_call(functools.partial(pair_kernel, flip, src_of, dst_of, (in_s...  32.5 us
    ppermute x14, starting transfers between devices, ring_sum(): go = lambda v, ax, step: lax.ppermute(v, 'row', row_shift(ax, step))  19.3 us
    ppermute x3, waiting for transfers between devices, local(): lax.ppermute(narrow(row_sum[step]), 'col', col_shift(-step, 0))  14.6 us
    ppermute x5, starting transfers between devices, local(): swap = lambda v: lax.ppermute(v, 'col', col_shift(0, 1))  14.4 us
    ppermute x3, waiting for transfers between devices, local(): lax.ppermute(masked, 'col', col_shift(step, 0))  11.8 us
    ppermute x3, starting transfers between devices, local(): lax.ppermute(masked, 'col', col_shift(step, 0))  5.12 us
    convert_element_type x4, other arithmetic, narrow(): return v.astype(jnp.bfloat16)  3.63 us
  transfers between devices with their start and end apart: 26, of which 10 were waited for; matrix products, arithmetic and copies ran while one was open for 5% of the time, Pallas kernels for 19%

commit v1 on v0

v1 whole, which is shorter than its diff:
```python
import functools

import jax
import jax.numpy as jnp
from jax import lax
from jax.experimental import pallas as pl
from jax.experimental.pallas import tpu as pltpu
from jax.sharding import PartitionSpec as P

NEAR_STEP = 4
FAR_STEP = 8

def pair_kernel(flip, src_of, dst_of, splits, near_pairs, near_count, far_pairs, far_rank, near, proj, back, *refs):
    n_in, n_out = len(refs) - 11 - len(splits[1]), len(splits[1])
    sources, outs = refs[:n_in], refs[n_in:n_in + n_out]
    xbuf, nbuf, pbuf, bbuf, acc, obuf, xsem, nsem, psem, bsem, osem = refs[n_in + n_out:]
    near_n, far_n = nbuf.shape[0], far_rank.shape[0]
    spare = acc.shape[0] - 1
    count = near_count[0]
    place = (lax.axis_index("row"), lax.axis_index("col"))
    x_copies, first = [], 0
    for n, (k, where, size) in enumerate(splits[0]):
        source = sources[k] if where is None else sources[k].at[where]
        x_copies.append(pltpu.make_async_copy(source, xbuf.at[pl.ds(first, size)], xsem.at[n]))
        first += size
    def near_copy(i):
        rows = pl.ds(i * NEAR_STEP, NEAR_STEP)
        return pltpu.make_async_copy(near.at[rows], nbuf.at[rows], nsem.at[i])
    p_copy = pltpu.make_async_copy(proj, pbuf, psem)
    b_copy = pltpu.make_async_copy(back, bbuf, bsem)
    for copy in x_copies:
        copy.start()
    p_copy.start()
    b_copy.start()
    steps = (count + NEAR_STEP - 1) // NEAR_STEP
    @pl.loop(0, acc.shape[0])
    def _(i):
        acc[i] = jnp.zeros(acc.shape[1:], jnp.float32)
    for copy in x_copies:
        copy.wait()
    p_copy.wait()
    b_copy.wait()
    @pl.loop(0, steps)
    def _(i):
        near_copy(i).start()
    rank_n = proj.shape[0] // far_n
    @pl.loop(0, far_n // FAR_STEP)
    def _(i):
        ids = [i * FAR_STEP + u for u in range(FAR_STEP)]
        pairs = [(far_pairs[0, q], far_pairs[1, q], place) for q in ids]
        rows = pl.ds(pl.multiple_of(i * FAR_STEP * rank_n, FAR_STEP * rank_n), FAR_STEP * rank_n)
        x = jnp.concatenate([xbuf[src_of(*pair)] for pair in pairs], axis=0)
        t = lax.dot_general(x, pbuf[rows], (((1,), (1,)), ((), ())), preferred_element_type=jnp.float32)
        lane = lax.broadcasted_iota(jnp.int32, (xbuf.shape[1], FAR_STEP * rank_n), 1)
        parts = []
        for u, q in enumerate(ids):
            keep = (lane >= u * rank_n) & (lane < u * rank_n + far_rank[q])
            parts.append(jnp.where(keep, t[u * xbuf.shape[1]:(u + 1) * xbuf.shape[1]], 0.0).astype(jnp.bfloat16))
        y = jnp.dot(jnp.concatenate(parts, axis=0), bbuf[rows], preferred_element_type=jnp.float32)
        for u, pair in enumerate(pairs):
            acc[dst_of(*pair)] += y[u * xbuf.shape[1]:(u + 1) * xbuf.shape[1]]
    @pl.loop(0, steps)
    def _(i):
        near_copy(i).wait()
        for u in range(NEAR_STEP):
            p = i * NEAR_STEP + u
            src = src_of(near_pairs[0, p], near_pairs[1, p], place)
            dst = dst_of(near_pairs[0, p], near_pairs[1, p], place)
            dst = jnp.where(p < count, dst, spare)
            dims = (((1,), (1,)), ((), ())) if flip else (((1,), (0,)), ((), ()))
            acc[dst] += lax.dot_general(xbuf[src], nbuf[p], dims, preferred_element_type=jnp.float32)
    o_copies, first = [], 0
    for k, size in enumerate(splits[1]):
        @pl.loop(first, first + size)
        def _(i):
            obuf[i] = acc[i].astype(jnp.bfloat16)
        copy = pltpu.make_async_copy(obuf.at[pl.ds(first, size)], outs[k], osem.at[k])
        copy.start()
        o_copies.append(copy)
        first += size
    for copy in o_copies:
        copy.wait()

def pair_product(flip, vmem_mib, src_of, dst_of, in_sizes, out_sizes, near_pairs, near_count, far_pairs, far_rank, near, proj, back, sources):
    loads, dof = sources[0].shape[-2:]
    smem = pl.BlockSpec(memory_space=pltpu.SMEM)
    hbm = pl.BlockSpec(memory_space=pl.ANY)
    n_dst = sum(out_sizes)
    near_n = near.shape[0]
    return pl.pallas_call(
        functools.partial(pair_kernel, flip, src_of, dst_of, (in_sizes, out_sizes)),
        out_shape=[jax.ShapeDtypeStruct((n, loads, dof), jnp.bfloat16) for n in out_sizes],
        in_specs=[smem] * 4 + [hbm] * (3 + len(sources)),
        out_specs=[hbm] * len(out_sizes),
        scratch_shapes=[
            pltpu.VMEM((sum(size for _, _, size in in_sizes), loads, dof), jnp.bfloat16),
            pltpu.VMEM(near.shape, jnp.bfloat16),
            pltpu.VMEM(proj.shape, jnp.bfloat16),
            pltpu.VMEM(back.shape, jnp.bfloat16),
            pltpu.VMEM((n_dst + 1, loads, dof), jnp.float32),
            pltpu.VMEM((n_dst, loads, dof), jnp.bfloat16),
            pltpu.SemaphoreType.DMA((len(in_sizes),)),
            pltpu.SemaphoreType.DMA((near_n // NEAR_STEP,)),
            pltpu.SemaphoreType.DMA,
            pltpu.SemaphoreType.DMA,
            pltpu.SemaphoreType.DMA((len(out_sizes),)),
        ],
        compiler_params=pltpu.CompilerParams(vmem_limit_bytes=vmem_mib * 2**20),
        cost_estimate=pl.CostEstimate(flops=2 * near_n * loads * dof * dof, bytes_accessed=2 * near.size + 4 * proj.size, transcendentals=0),
    )(near_pairs, near_count, far_pairs, far_rank, near, proj, back, *sources)


SIDE = 4
PER = 8


def col_shift(step, other):
    return [((x + step) % SIDE * 2 + (core ^ other), x * 2 + core) for x in range(SIDE) for core in range(2)]


def plane_shift(first, step):
    pairs = []
    for y in range(SIDE):
        for z in range(SIDE):
            for col in range(2 * SIDE):
                along_y = (col % 2 == 0) == (first == 1)
                far = ((y + step) % SIDE, z) if along_y else (y, (z + step) % SIDE)
                pairs.append(((far[0] * SIDE + far[1]) * 2 * SIDE + col, (y * SIDE + z) * 2 * SIDE + col))
    return pairs


def row_place(r, place):
    piece = (r // PER) % (2 * SIDE)
    return (piece // 2 - place[1] // 2 + SIDE) % SIDE, (piece % 2) ^ (place[1] % 2), r % PER


def src_rows(r, c, place):
    step, other, j = row_place(r, place)
    near_step = jnp.where(place[1] % 2 == 0, SIDE - 1, 1)
    at = jnp.where(step == 0, other, jnp.where(step == 2, 6 + other, jnp.where(step == near_step, 2 + other, 5 - other)))
    return at * PER + j


def dst_rows(r, c, place):
    step, other, j = row_place(r, place)
    mine = (step == jnp.where(place[1] % 2 == 0, 1, SIDE - 1)) | ((step % 2 == 0) & (other == 0))
    at = jnp.where(step == 0, 3, jnp.where(step == 2, 2, jnp.where(mine, other, 1 - other)))
    return (jnp.where(mine, SIDE, 0) + at) * PER + j


def col_place(c, place):
    piece = c // (2 * SIDE * PER)
    dy = (piece // SIDE - place[0] // SIDE + SIDE) % SIDE
    dz = (piece % SIDE - place[0] % SIDE + SIDE) % SIDE
    j = c % PER
    late = j // 4
    return jnp.where(late == 0, dz, dy), jnp.where(late == 0, dy, dz), late, j % 4


def src_cols(r, c, place):
    first, second, late, j = col_place(c, place)
    return (late ^ (place[1] % 2)) * 64 + first * 16 + second * 4 + j


def dst_cols(r, c, place):
    first, second, late, j = col_place(c, place)
    return (late ^ (place[1] % 2)) * 64 + (first + SIDE - 1) % SIDE * 16 + second * 4 + j


def wide(v):
    return v.astype(jnp.float32)


def narrow(v):
    return v.astype(jnp.bfloat16)


def swap(v):
    return lax.ppermute(v, "col", col_shift(0, 1))


def local(
    load_vectors,
    live_panels,
    self_blocks,
    near_pairs,
    near_count,
    near_blocks,
    far_pairs,
    far_rank,
    far_left,
    far_right,
):
    dof = load_vectors.shape[2]
    panel_of = jnp.arange(dof) % (dof // 3)
    live_dofs = (panel_of[None, :] < live_panels[:, None]).astype(jnp.bfloat16)
    masked = load_vectors * live_dofs[:, None, :]
    core = lax.axis_index("col") % 2
    twin = swap(masked)
    part = lambda v: lax.dynamic_slice_in_dim(v, core * (PER // 2), PER // 2)
    own = jnp.stack([part(masked), part(twin)])
    plane = lambda v, first, step: lax.ppermute(v, ("row", "col"), plane_shift(first, step))
    chip = [((x - 1 + 2 * core) % SIDE * 2 + core, x * 2 + core) for x in range(SIDE) for core in range(2)]
    x_near = lax.ppermute(masked, "col", chip)
    x_cross = lax.ppermute(twin, "col", chip)
    line = [plane(own, 1, step) for step in (1, 3, 2)]
    x_two = lax.ppermute(x_near, "col", chip)
    x_near, x_cross, x_two, line = lax.optimization_barrier((x_near, x_cross, x_two, line))
    line = jnp.stack([own, line[0], line[2], line[1]])
    cols = [line] + [plane(line, 0, step) for step in (1, 2, 3)]
    rows = [masked, twin, x_near, x_cross, swap(x_near), swap(x_cross), x_two, swap(x_two)]
    left = jnp.swapaxes(far_left, 1, 2).reshape(-1, dof)
    right = jnp.swapaxes(far_right, 1, 2).reshape(-1, dof)
    lists = (near_pairs.T, near_count, far_pairs.T, far_rank, near_blocks)
    to_cols = pair_product(False, 44, src_rows, dst_cols, [(k, None, n) for k, n in enumerate((8,) * 8)], (16, 16, 16, 16, 24, 24, 16), *lists, left, right, rows)
    theirs = [swap(to_cols[4]), swap(to_cols[5])]
    cols[1:], theirs = lax.optimization_barrier((cols[1:], theirs))
    theirs = [theirs[0][:16], jnp.concatenate([theirs[0][16:], theirs[1][:8]]), theirs[1][8:], swap(to_cols[6])]
    sums = [jnp.stack([to_cols[k], theirs[k]]) for k in range(SIDE)]
    cols += [swap(v[:, 1]) for v in cols]
    sums_in = [plane(sums[step - 1], 0, -step) for step in (1, 2, 3)]
    pieces = [(k, (at, 0) if k < 4 else at, 4) for k in range(8) for at in range(SIDE)]
    to_rows = pair_product(True, 38, src_cols, dst_rows, pieces, (16,) * 4, *lists, right, left, cols)
    row_near = wide(to_rows[2]) + wide(swap(to_rows[0]))
    row_far = wide(to_rows[3]) + wide(swap(to_rows[1]))
    row_near, row_far, sums_in = lax.optimization_barrier((row_near, row_far, sums_in))
    forth = lax.ppermute(narrow(jnp.concatenate([row_far[:PER], row_near[PER:]])), "col", chip)
    line_sum = (wide(sums[3]) + sum(wide(v) for v in sums_in)).reshape((2, SIDE, PER // 2) + masked.shape[1:])
    ends = [plane(narrow(line_sum[:, step]), 1, -step) for step in (1, 2, 3)]
    forth, ends = lax.optimization_barrier((forth, ends))
    forth_two = lax.ppermute(narrow(row_near[:PER] + wide(forth[:PER])), "col", chip)
    row_part = [row_far[PER:], swap(forth[PER:]), forth_two]
    end = line_sum[:, 0] + sum(wide(v) for v in ends)
    end_in = swap(end[1])
    col_part = jnp.where(core == 0, jnp.concatenate([end[0], end_in]), jnp.concatenate([end_in, end[0]]))
    own_part = jnp.einsum("cld,ced->cle", masked, self_blocks, preferred_element_type=jnp.float32)
    total = own_part + sum(wide(v) for v in row_part) + col_part
    return total * live_dofs.astype(jnp.float32)[:, None, :]


def solution(mesh):
    spec = P(("row", "col"))
    return jax.shard_map(local, mesh=mesh, in_specs=(spec,) * 10, out_specs=spec, check_vma=False)
```

time: 167 us -> 138 us (0.83)
  waiting for transfers between devices: 63.3 us -> 37.2 us
  between operations: 14.4 us -> 1 us
  Pallas kernels: 32.5 us -> 44.4 us
  starting transfers between devices: 41.3 us -> 34.5 us
  other arithmetic: 11.3 us -> 13.6 us
  local copies, waits for them, and re-layouts: 2.91 us -> 4.84 us
    ppermute x25 -> x32, waiting for transfers between devices: 63.2 us -> 37.2 us  [the longest x12 27.8 us: local(): lax.ppermute(v, ('row', 'col'), plane_shift(first, step))]
    pallas_call x2, Pallas kernels: 32.5 us -> 44.4 us  [pair_product(): pl.pallas_call(functools.partial(pair_kernel, flip, src_of, dst_of, (in_s...]
    ppermute x25 -> x32, starting transfers between devices: 41.3 us -> 34.5 us  [the longest x12 17.9 us: local(): lax.ppermute(v, ('row', 'col'), plane_shift(first, step))]
    add x2 -> x4, other arithmetic: 0.16 us -> 3.85 us  [the longest x1 3.29 us: local(): wide(sums[3]) + sum((wide(v) for v in sums_in))]
    convert_element_type x4 -> x1, other arithmetic: 3.63 us -> 0.84 us  [narrow(): return v.astype(jnp.bfloat16)]
    another operation x3 -> x6, other arithmetic: 3.49 us -> 4.48 us  [the longest x4 4.16 us: local(): sums = [jnp.stack([to_cols[k], theirs[k]]) for k in range(SIDE)]]
  transfers between devices with their start and end apart: 26 -> 32, of which waited for: 10 -> 12; matrix products, arithmetic and copies ran while one was open for 5% -> 9% of each run, Pallas kernels for 19% -> 33%
where the time goes in v1:
time: 138 us; the launch traced here: 136 us
  Pallas kernels  44.4 us (32%)
  waiting for transfers between devices  37.2 us (27%)
  starting transfers between devices  34.5 us (25%)
  other arithmetic  13.6 us (10%)
  local copies, waits for them, and re-layouts  4.84 us (4%)
    pallas_call x2, Pallas kernels, pair_product(): pl.pallas_call(functools.partial(pair_kernel, flip, src_of, dst_of, (in_s...  44.4 us
    ppermute x12, waiting for transfers between devices, local(): lax.ppermute(v, ('row', 'col'), plane_shift(first, step))  27.8 us
    ppermute x12, starting transfers between devices, local(): lax.ppermute(v, ('row', 'col'), plane_shift(first, step))  17.9 us
    ppermute x15, starting transfers between devices, swap(): return lax.ppermute(v, 'col', col_shift(0, 1))  8.85 us
    ppermute x15, waiting for transfers between devices, swap(): return lax.ppermute(v, 'col', col_shift(0, 1))  6.73 us
    another operation x4, other arithmetic, local(): sums = [jnp.stack([to_cols[k], theirs[k]]) for k in range(SIDE)]  4.16 us
    add x1, other arithmetic, local(): wide(sums[3]) + sum((wide(v) for v in sums_in))  3.29 us
  transfers between devices with their start and end apart: 32, of which 12 were waited for; matrix products, arithmetic and copies ran while one was open for 9% of the time, Pallas kernels for 33%

profile of v1, /device:TPU:1, one launch (start us, length us, event | category | flops | bytes accessed | tf_op | source)
XLA Modules:
  0.0 136.5 jit_solution(4680643925498945218)
XLA Ops:
  0.0 0.9 fusion.6
  0.9 1.0 broadcast_multiply_fusion.refs_0_
  1.9 1.5 %collective-permute-start = (bf16[8,64,384]{2,1,0:T(8,128)(2,1)S(1)}, bf16[8,64,384]{2,1,0:T(8,128)(2,1)S(1)}, u32[]{:S(2)}, u32[]{:S(2)}) collective-permute-start(bf16[8,64,384]{2,1,0:T(8,128)(2,1)S(1)} %broadcast_multiply_fusion.refs_0_), channel_id=1, source_target_pairs={{1,0},{0,1},{3,2},{2,3},{5,4},{4,5},{7,6},{6,7},{9,8},{8,9},{11,10... | collective-permute-start | bytes 1179656 | tf_op jit(solution)/shard_map/ppermute | solution.py:179
  3.4 2.6 %collective-permute-start.1 = (bf16[8,64,384]{2,1,0:T(8,128)(2,1)S(1)}, bf16[8,64,384]{2,1,0:T(8,128)(2,1)S(1)}, u32[]{:S(2)}, u32[]{:S(2)}) collective-permute-start(bf16[8,64,384]{2,1,0:T(8,128)(2,1)S(1)} %broadcast_multiply_fusion.refs_0_), channel_id=1, source_target_pairs={{6,0},{3,1},{0,2},{5,3},{2,4},{7,5},{4,6},{1,7},{14,8},{11,9},{8,1... | collective-permute-start | bytes 1179656 | tf_op jit(solution)/shard_map/ppermute | solution.py:204
  6.1 3.8 %collective-permute-start.4 = (bf16[2,4,64,384]{3,2,1,0:T(8,128)(2,1)S(1)}, bf16[2,4,64,384]{3,2,1,0:T(8,128)(2,1)S(1)}, u32[]{:S(2)}, u32[]{:S(2)}) collective-permute-start(bf16[2,4,64,384]{3,2,1,0:T(8,128)(2,1)S(1)} %get-tuple-element.73), channel_id=1, source_target_pairs={{32,0},{9,1},{34,2},{11,3},{36,4},{13,5},{38,6},{15,7},{40,8},{17,... | collective-permute-start | bytes 1179656 | tf_op jit(solution)/shard_map/ppermute | solution.py:202
  10.0 1.3 collective-permute-start.6
  11.3 1.3 collective-permute-start.2
  12.6 1.2 collective-permute-start.3
  13.8 5.1 %collective-permute-done.4 = bf16[2,4,64,384]{3,2,1,0:T(8,128)(2,1)S(1)} collective-permute-done((bf16[2,4,64,384]{3,2,1,0:T(8,128)(2,1)S(1)}, bf16[2,4,64,384]{3,2,1,0:T(8,128)(2,1)S(1)}, u32[]{:S(2)}, u32[]{:S(2)}) %collective-permute-start.4) | collective-permute-done | bytes 393248 | tf_op jit(solution)/shard_map/ppermute | solution.py:202
  18.9 3.4 %collective-permute-done.5 = bf16[2,4,64,384]{3,2,1,0:T(8,128)(2,1)S(1)} collective-permute-done((bf16[2,4,64,384]{3,2,1,0:T(8,128)(2,1)S(1)}, bf16[2,4,64,384]{3,2,1,0:T(8,128)(2,1)S(1)}, u32[]{:S(2)}, u32[]{:S(2)}) %collective-permute-start.5) | collective-permute-done | bytes 393248 | tf_op jit(solution)/shard_map/ppermute | solution.py:202
  22.3 0.1 collective-permute-done.3.refs_6_
  22.4 1.4 %collective-permute-start.10 = (bf16[8,64,384]{2,1,0:T(8,128)(2,1)S(1)}, bf16[8,64,384]{2,1,0:T(8,128)(2,1)S(1)}, u32[]{:S(2)}, u32[]{:S(2)}) collective-permute-start(bf16[8,64,384]{2,1,0:T(8,128)(2,1)S(1)} %collective-permute-done.1.refs_2_), channel_id=1, source_target_pairs={{1,0},{0,1},{3,2},{2,3},{5,4},{4,5},{7,6},{6,7},{9,8},{8,9},{11,10... | collective-permute-start | bytes 1179656 | tf_op jit(solution)/shard_map/ppermute | solution.py:179
  23.8 0.5 collective-permute-start.12
  24.3 0.2 pad_maximum_fusion
  24.6 1.2 collective-permute-start.7
  25.8 2.3 %collective-permute-start.8 = (bf16[4,2,4,64,384]{4,3,2,0,1:T(8,128)(2,1)S(1)}, bf16[4,2,4,64,384]{4,3,2,0,1:T(8,128)(2,1)S(1)}, u32[]{:S(2)}, u32[]{:S(2)}) collective-permute-start(bf16[4,2,4,64,384]{4,3,2,0,1:T(8,128)(2,1)S(1)} %pad_maximum_fusion), channel_id=1, source_target_pairs={{16,0},{65,1},{18,2},{67,3},{20,4},{69,5},{22,6},{71,7},{24,8},{73... | collective-permute-start | bytes 4718600 | tf_op jit(solution)/shard_map/ppermute | solution.py:202
  28.8 18.5 %shard_map.100 = (bf16[16,64,384]{2,1,0:T(8,128)(2,1)S(1)}, bf16[16,64,384]{2,1,0:T(8,128)(2,1)S(1)}, bf16[16,64,384]{2,1,0:T(8,128)(2,1)S(1)}, bf16[16,64,384]{...) custom-call(s32[2,48]{1,0:T(2,128)S(1)} %bitcast.65, ...), custom_call_target="tpu_custom_call" | custom-call | flops 905969664 | bytes 18874368 | tf_op jit(solution)/shard_map/pallas_call | solution.py:90
  47.3 0.6 collective-permute-start.13
  47.9 0.1 collective-permute-start.14
  48.1 2.3 %collective-permute-done.13 = bf16[24,64,384]{2,1,0:T(8,128)(2,1)S(1)} collective-permute-done((bf16[24,64,384]{2,1,0:T(8,128)(2,1)S(1)}, bf16[24,64,384]{2,1,0:T(8,128)(2,1)S(1)}, u32[]{:S(2)}, u32[]{:S(2)}) %collective-permute-start.13) | collective-permute-done | bytes 1179680 | tf_op jit(solution)/shard_map/ppermute | solution.py:179
  50.4 0.4 collective-permute-start.15
  50.8 1.3 collective-permute-done.14
  52.1 11.6 %collective-permute-done.9 = bf16[4,2,4,64,384]{4,3,2,0,1:T(8,128)(2,1)S(1)} collective-permute-done((bf16[4,2,4,64,384]{4,3,2,0,1:T(8,128)(2,1)S(1)}, bf16[4,2,4,64,384]{4,3,2,0,1:T(8,128)(2,1)S(1)}, u32[]{:S(2)}, u32[]{:S(2)}) %collective-permute-start.9) | collective-permute-done | bytes 1572896 | tf_op jit(solution)/shard_map/ppermute | solution.py:202
  63.8 0.1 maximum_bitcast_fusion
  63.9 1.4 %pad_maximum_fusion.2 = bf16[2,16,64,384]{3,2,1,0:T(8,128)(2,1)} fusion(bf16[1,16,64,384]{3,2,1,0:T(8,128)(2,1)S(1)} %maximum_bitcast_fusion, bf16[1,16,64,384]{3,2,1,0:T(8,128)(2,1)S(1)} %bitcast.64), kind=kLoop, calls=%fused_computation.3 | loop fusion | flops 786432 | bytes 3145728 | tf_op jit(solution)/shard_map/stack | solution.py:219
  65.3 1.5 %collective-permute-start.22 = (bf16[2,16,64,384]{3,2,1,0:T(8,128)(2,1)}, bf16[2,16,64,384]{3,2,1,0:T(8,128)(2,1)}, u32[]{:S(2)}, u32[]{:S(2)}) collective-permute-start(bf16[2,16,64,384]{3,2,1,0:T(8,128)(2,1)} %pad_maximum_fusion.2), channel_id=1, source_target_pairs={{16,0},{65,1},{18,2},{67,3},{20,4},{69,5},{22,6},{71,7},{24,8},{73... | collective-permute-start | bytes 4718600 | tf_op jit(solution)/shard_map/ppermute | solution.py:202
  66.8 2.4 %collective-permute-start.16 = (bf16[4,4,64,384]{3,2,1,0:T(8,128)(2,1)S(1)}, bf16[4,4,64,384]{3,2,1,0:T(8,128)(2,1)S(1)}, u32[]{:S(2)}, u32[]{:S(2)}) collective-permute-start(bf16[4,4,64,384]{3,2,1,0:T(8,128)(2,1)S(1)} %slice_bitcast_fusion.6), channel_id=1, source_target_pairs={{1,0},{0,1},{3,2},{2,3},{5,4},{4,5},{7,6},{6,7},{9,8},{8,9},{11,10... | collective-permute-start | bytes 2359304 | tf_op jit(solution)/shard_map/ppermute | solution.py:179
  69.3 0.1 collective-permute-start.17
  69.5 0.6 collective-permute-start.18
  70.2 1.4 pad_maximum_fusion.3
  71.6 1.3 pad_maximum_fusion.1
  72.9 1.8 %collective-permute-start.23 = (bf16[2,16,64,384]{3,2,1,0:T(8,128)(2,1)}, bf16[2,16,64,384]{3,2,1,0:T(8,128)(2,1)}, u32[]{:S(2)}, u32[]{:S(2)}) collective-permute-start(bf16[2,16,64,384]{3,2,1,0:T(8,128)(2,1)} %pad_maximum_fusion.3), channel_id=1, source_target_pairs={{8,0},{33,1},{10,2},{35,3},{12,4},{37,5},{14,6},{39,7},{16,8},{41,... | collective-permute-start | bytes 4718600 | tf_op jit(solution)/shard_map/ppermute | solution.py:202
  74.7 0.2 copy.21.refs_0_
  74.9 0.2 copy.22.refs_1_
  75.1 0.2 copy.23.refs_2_
  75.3 0.2 copy.24.refs_3_
  75.6 1.4 %copy-done.1 = bf16[96,384,32]{1,2,0:T(8,128)(2,1)S(1)} copy-done((bf16[96,384,32]{1,2,0:T(8,128)(2,1)S(1)}, bf16[96,384,32]{1,2,0:T(8,128)(2,1)}, u32[]{:S(2)}) %copy-start.1) | copy-done | bytes 2359320
  77.0 25.9 %shard_map.101 = (bf16[16,64,384]{2,1,0:T(8,128)(2,1)S(1)}, bf16[16,64,384]{2,1,0:T(8,128)(2,1)S(1)}, bf16[16,64,384]{2,1,0:T(8,128)(2,1)S(1)}, bf16[16,64,384]{2,1,0:T(8,128)(2,1)S(1)}) custom-call(s32[2,48]{1,0:T(2,128)S(1)} %bitcast.66, s32[1]{0:T(128)S(6)} %copy.33.near_count, s32[2,96]{1,0:T(2,128)S(1)} %bitcast.68, s32[96]{0:T(128)S(1)} %copy-done.4, ...), custom_call_target="tpu_custom_call" | custom-call | flops 905969664 | bytes 18874368 | tf_op jit(solution)/shard_map/pallas_call | solution.py:90
  103.0 0.5 collective-permute-start.19
  103.5 1.8 %collective-permute-done.20 = bf16[16,64,384]{2,1,0:T(8,128)(2,1)S(1)} collective-permute-done((bf16[16,64,384]{2,1,0:T(8,128)(2,1)S(1)}, bf16[16,64,384]{2,1,0:T(8,128)(2,1)S(1)}, u32[]{:S(2)}, u32[]{:S(2)}) %collective-permute-start.20) | collective-permute-done | bytes 786464 | tf_op jit(solution)/shard_map/ppermute | solution.py:179
  105.3 0.1 collective-permute-start.25
  105.4 0.2 convert_add_fusion
  105.6 0.8 collective-permute-done.19
  106.4 0.2 convert_add_fusion.1
  106.7 0.1 copy-done.5
  106.8 0.1 pad_maximum_fusion.4
  107.0 0.5 collective-permute-done.25
  107.5 3.3 %add_add_fusion = f32[2,16,64,384]{3,2,1,0:T(8,128)S(1)} fusion(bf16[2,16,64,384]{3,2,1,0:T(8,128)(2,1)} %collective-permute-done.23, bf16[2,16,64,384]{3,2,1,0:T(8,128)(2,1)} %collective-permute-done.22, bf16[2,16,64,384]{3,2,1,0:T(8,128)(2,1)} %collective-permute-done.21, bf16[1,16,64,384]{3,2,1,0:T(8,128)(2,1)S(1)} %bitcast.73, ...), kind=kLoop, calls=%fused_computation | loop fusion | flops 6291456 | bytes 9437184 | tf_op jit(solution)/shard_map/add | solution.py:228
  110.8 0.2 slice_bitcast_fusion.9
  111.0 1.1 collective-permute-start.26
  112.1 3.1 %collective-permute-start.27 = (bf16[2,4,64,384]{3,2,1,0:T(8,128)(2,1)S(1)}, bf16[2,4,64,384]{3,2,1,0:T(8,128)(2,1)S(1)}, u32[]{:S(2)}, u32[]{:S(2)}) collective-permute-start(bf16[2,4,64,384]{3,2,1,0:T(8,128)(2,1)S(1)} %get-tuple-element.68), channel_id=1, source_target_pairs={{64,0},{17,1},{66,2},{19,3},{68,4},{21,5},{70,6},{23,7},{72,8},{25... | collective-permute-start | bytes 1179656 | tf_op jit(solution)/shard_map/ppermute | solution.py:202
  115.2 1.9 %collective-permute-start.28 = (bf16[2,4,64,384]{3,2,1,0:T(8,128)(2,1)S(1)}, bf16[2,4,64,384]{3,2,1,0:T(8,128)(2,1)S(1)}, u32[]{:S(2)}, u32[]{:S(2)}) collective-permute-start(bf16[2,4,64,384]{3,2,1,0:T(8,128)(2,1)S(1)} %get-tuple-element.67), channel_id=1, source_target_pairs={{32,0},{9,1},{34,2},{11,3},{36,4},{13,5},{38,6},{15,7},{40,8},{17,... | collective-permute-start | bytes 1179656 | tf_op jit(solution)/shard_map/ppermute | solution.py:202
  117.1 2.3 %collective-permute-done.26 = bf16[2,4,64,384]{3,2,1,0:T(8,128)(2,1)S(1)} collective-permute-done((bf16[2,4,64,384]{3,2,1,0:T(8,128)(2,1)S(1)}, bf16[2,4,64,384]{3,2,1,0:T(8,128)(2,1)S(1)}, u32[]{:S(2)}, u32[]{:S(2)}) %collective-permute-start.26) | collective-permute-done | bytes 393248 | tf_op jit(solution)/shard_map/ppermute | solution.py:202
  119.4 5.3 %collective-permute-done.27 = bf16[2,4,64,384]{3,2,1,0:T(8,128)(2,1)S(1)} collective-permute-done((bf16[2,4,64,384]{3,2,1,0:T(8,128)(2,1)S(1)}, bf16[2,4,64,384]{3,2,1,0:T(8,128)(2,1)S(1)}, u32[]{:S(2)}, u32[]{:S(2)}) %collective-permute-start.27) | collective-permute-done | bytes 393248 | tf_op jit(solution)/shard_map/ppermute | solution.py:202
  124.8 0.8 add_convert_fusion
  125.6 0.8 slice.80
  126.4 2.6 %collective-permute-start.30 = (bf16[8,64,384]{2,1,0:T(8,128)(2,1)}, bf16[8,64,384]{2,1,0:T(8,128)(2,1)S(1)}, u32[]{:S(2)}, u32[]{:S(2)}) collective-permute-start(bf16[8,64,384]{2,1,0:T(8,128)(2,1)} %add_convert_fusion), channel_id=1, source_target_pairs={{6,0},{3,1},{0,2},{5,3},{2,4},{7,5},{4,6},{1,7},{14,8},{11,9},{8,1... | collective-permute-start | bytes 1179656 | tf_op jit(solution)/shard_map/ppermute | solution.py:231
  129.0 0.2 fusion
  129.2 0.8 slice_bitcast_fusion.8
  130.0 0.2 collective-permute-start.31
  130.2 0.3 collective-permute-start.29
  130.5 0.9 fusion.8
  131.5 2.6 %collective-permute-done.30 = bf16[8,64,384]{2,1,0:T(8,128)(2,1)S(1)} collective-permute-done((bf16[8,64,384]{2,1,0:T(8,128)(2,1)}, bf16[8,64,384]{2,1,0:T(8,128)(2,1)S(1)}, u32[]{:S(2)}, u32[]{:S(2)}) %collective-permute-start.30) | collective-permute-done | bytes 393248 | tf_op jit(solution)/shard_map/ppermute | solution.py:231
  134.1 2.4 %fusion.2 = f32[8,64,384]{2,1,0:T(8,128)} fusion(f32[4,64,384]{2,1,0:T(8,128)} %collective-permute-done.31, f32[4,64,384]{2,1,0:T(8,128)S(1)} %get-tuple-element.70, f32[8,64,384]{2,1,0:T(8,128)S(1)} %fusion.8, bf16[8,64,384]{2,1,0:T(8,128)(2,1)S(1)} %collective-permute-done.30, bf16[8,64,384]{2,1,0:T(8,128)(2,1)} %collective-permute-done.29, ...), kind=kLoop, calls=%fused_computation.16 | loop fusion | flops 1966080 | bytes 3944449 | tf_op jit(solution)/shard_map/mul | solution.py:238
  (52 shorter events, 1.0 us)
Async XLA Ops:
  0.0 130.5 %copy-start = (bf16[8,384,384]{2,1,0:T(8,128)(2,1)S(1)}, bf16[8,384,384]{2,1,0:T(8,128)(2,1)}, u32[]{:S(2)}) copy-start(bf16[8,384,384]{2,1,0:T(8,128)(2,1)} %param.12) | copy-start | bytes 7077892
  1.9 4.1 %collective-permute-start = (bf16[8,64,384]{2,1,0:T(8,128)(2,1)S(1)}, bf16[8,64,384]{2,1,0:T(8,128)(2,1)S(1)}, u32[]{:S(2)}, u32[]{:S(2)}) collective-permute-start(bf16[8,64,384]{2,1,0:T(8,128)(2,1)S(1)} %broadcast_multiply_fusion.refs_0_), channel_id=1, source_target_pairs={{1,0},{0,1},{3,2},{2,3},{5,4},{4,5},{7,6},{6,7},{9,8},{8,9},{11,10... | collective-permute-start | bytes 1179656 | tf_op jit(solution)/shard_map/ppermute | solution.py:179
  3.4 9.2 %collective-permute-start.1 = (bf16[8,64,384]{2,1,0:T(8,128)(2,1)S(1)}, bf16[8,64,384]{2,1,0:T(8,128)(2,1)S(1)}, u32[]{:S(2)}, u32[]{:S(2)}) collective-permute-start(bf16[8,64,384]{2,1,0:T(8,128)(2,1)S(1)} %broadcast_multiply_fusion.refs_0_), channel_id=1, source_target_pairs={{6,0},{3,1},{0,2},{5,3},{2,4},{7,5},{4,6},{1,7},{14,8},{11,9},{8,1... | collective-permute-start | bytes 1179656 | tf_op jit(solution)/shard_map/ppermute | solution.py:204
  6.1 12.8 %collective-permute-start.4 = (bf16[2,4,64,384]{3,2,1,0:T(8,128)(2,1)S(1)}, bf16[2,4,64,384]{3,2,1,0:T(8,128)(2,1)S(1)}, u32[]{:S(2)}, u32[]{:S(2)}) collective-permute-start(bf16[2,4,64,384]{3,2,1,0:T(8,128)(2,1)S(1)} %get-tuple-element.73), channel_id=1, source_target_pairs={{32,0},{9,1},{34,2},{11,3},{36,4},{13,5},{38,6},{15,7},{40,8},{17,... | collective-permute-start | bytes 1179656 | tf_op jit(solution)/shard_map/ppermute | solution.py:202
  10.0 12.3 %collective-permute-start.5 = (bf16[2,4,64,384]{3,2,1,0:T(8,128)(2,1)S(1)}, bf16[2,4,64,384]{3,2,1,0:T(8,128)(2,1)S(1)}, u32[]{:S(2)}, u32[]{:S(2)}) collective-permute-start(bf16[2,4,64,384]{3,2,1,0:T(8,128)(2,1)S(1)} %get-tuple-element.73), channel_id=1, source_target_pairs={{96,0},{25,1},{98,2},{27,3},{100,4},{29,5},{102,6},{31,7},{104,8},... | collective-permute-start | bytes 1179656 | tf_op jit(solution)/shard_map/ppermute | solution.py:202
  10.0 12.3 %collective-permute-start.6 = (bf16[2,4,64,384]{3,2,1,0:T(8,128)(2,1)S(1)}, bf16[2,4,64,384]{3,2,1,0:T(8,128)(2,1)S(1)}, u32[]{:S(2)}, u32[]{:S(2)}) collective-permute-start(bf16[2,4,64,384]{3,2,1,0:T(8,128)(2,1)S(1)} %get-tuple-element.73), channel_id=1, source_target_pairs={{64,0},{17,1},{66,2},{19,3},{68,4},{21,5},{70,6},{23,7},{72,8},{25... | collective-permute-start | bytes 1179656 | tf_op jit(solution)/shard_map/ppermute | solution.py:202
  11.3 11.0 %collective-permute-start.2 = (bf16[8,64,384]{2,1,0:T(8,128)(2,1)S(1)}, bf16[8,64,384]{2,1,0:T(8,128)(2,1)S(1)}, u32[]{:S(2)}, u32[]{:S(2)}) collective-permute-start(bf16[8,64,384]{2,1,0:T(8,128)(2,1)S(1)} %collective-permute-done.refs_1_), channel_id=1, source_target_pairs={{6,0},{3,1},{0,2},{5,3},{2,4},{7,5},{4,6},{1,7},{14,8},{11,9},{8,1... | collective-permute-start | bytes 1179656 | tf_op jit(solution)/shard_map/ppermute | solution.py:205
  12.6 9.8 %collective-permute-start.3 = (bf16[8,64,384]{2,1,0:T(8,128)(2,1)S(1)}, bf16[8,64,384]{2,1,0:T(8,128)(2,1)S(1)}, u32[]{:S(2)}, u32[]{:S(2)}) collective-permute-start(bf16[8,64,384]{2,1,0:T(8,128)(2,1)S(1)} %collective-permute-done.1.refs_2_), channel_id=1, source_target_pairs={{6,0},{3,1},{0,2},{5,3},{2,4},{7,5},{4,6},{1,7},{14,8},{11,9},{8,1... | collective-permute-start | bytes 1179656 | tf_op jit(solution)/shard_map/ppermute | solution.py:207
  22.4 5.6 %collective-permute-start.10 = (bf16[8,64,384]{2,1,0:T(8,128)(2,1)S(1)}, bf16[8,64,384]{2,1,0:T(8,128)(2,1)S(1)}, u32[]{:S(2)}, u32[]{:S(2)}) collective-permute-start(bf16[8,64,384]{2,1,0:T(8,128)(2,1)S(1)} %collective-permute-done.1.refs_2_), channel_id=1, source_target_pairs={{1,0},{0,1},{3,2},{2,3},{5,4},{4,5},{7,6},{6,7},{9,8},{8,9},{11,10... | collective-permute-start | bytes 1179656 | tf_op jit(solution)/shard_map/ppermute | solution.py:179
  23.8 4.9 %collective-permute-start.11 = (bf16[8,64,384]{2,1,0:T(8,128)(2,1)S(1)}, bf16[8,64,384]{2,1,0:T(8,128)(2,1)S(1)}, u32[]{:S(2)}, u32[]{:S(2)}) collective-permute-start(bf16[8,64,384]{2,1,0:T(8,128)(2,1)S(1)} %collective-permute-done.2.refs_3_), channel_id=1, source_target_pairs={{1,0},{0,1},{3,2},{2,3},{5,4},{4,5},{7,6},{6,7},{9,8},{8,9},{11,10... | collective-permute-start | bytes 1179656 | tf_op jit(solution)/shard_map/ppermute | solution.py:179
  23.8 4.9 %collective-permute-start.12 = (bf16[8,64,384]{2,1,0:T(8,128)(2,1)S(1)}, bf16[8,64,384]{2,1,0:T(8,128)(2,1)S(1)}, u32[]{:S(2)}, u32[]{:S(2)}) collective-permute-start(bf16[8,64,384]{2,1,0:T(8,128)(2,1)S(1)} %collective-permute-done.3.refs_6_), channel_id=1, source_target_pairs={{1,0},{0,1},{3,2},{2,3},{5,4},{4,5},{7,6},{6,7},{9,8},{8,9},{11,10... | collective-permute-start | bytes 1179656 | tf_op jit(solution)/shard_map/ppermute | solution.py:179
  24.3 4.4 %copy-start.2 = (s32[48,2]{0,1:T(2,128)S(1)}, s32[48,2]{0,1:T(2,128)}, u32[]{:S(2)}) copy-start(s32[48,2]{0,1:T(2,128)} %param.13) | copy-start | bytes 1156
  24.3 4.4 %copy-start.3 = (s32[96,2]{0,1:T(2,128)S(1)}, s32[96,2]{0,1:T(2,128)}, u32[]{:S(2)}) copy-start(s32[96,2]{0,1:T(2,128)} %param.16) | copy-start | bytes 2308
  24.3 4.4 %copy-start.4 = (s32[96]{0:T(128)S(1)}, s32[96]{0:T(128)}, u32[]{:S(2)}) copy-start(s32[96]{0:T(128)} %far_rank.3) | copy-start | bytes 1156
  24.6 27.5 %collective-permute-start.7 = (bf16[4,2,4,64,384]{4,3,2,0,1:T(8,128)(2,1)S(1)}, bf16[4,2,4,64,384]{4,3,2,0,1:T(8,128)(2,1)S(1)}, u32[]{:S(2)}, u32[]{:S(2)}) collective-permute-start(bf16[4,2,4,64,384]{4,3,2,0,1:T(8,128)(2,1)S(1)} %pad_maximum_fusion), channel_id=1, source_target_pairs={{8,0},{33,1},{10,2},{35,3},{12,4},{37,5},{14,6},{39,7},{16,8},{41,... | collective-permute-start | bytes 4718600 | tf_op jit(solution)/shard_map/ppermute | solution.py:202
  25.8 26.3 %collective-permute-start.8 = (bf16[4,2,4,64,384]{4,3,2,0,1:T(8,128)(2,1)S(1)}, bf16[4,2,4,64,384]{4,3,2,0,1:T(8,128)(2,1)S(1)}, u32[]{:S(2)}, u32[]{:S(2)}) collective-permute-start(bf16[4,2,4,64,384]{4,3,2,0,1:T(8,128)(2,1)S(1)} %pad_maximum_fusion), channel_id=1, source_target_pairs={{16,0},{65,1},{18,2},{67,3},{20,4},{69,5},{22,6},{71,7},{24,8},{73... | collective-permute-start | bytes 4718600 | tf_op jit(solution)/shard_map/ppermute | solution.py:202
  28.1 35.6 %collective-permute-start.9 = (bf16[4,2,4,64,384]{4,3,2,0,1:T(8,128)(2,1)S(1)}, bf16[4,2,4,64,384]{4,3,2,0,1:T(8,128)(2,1)S(1)}, u32[]{:S(2)}, u32[]{:S(2)}) collective-permute-start(bf16[4,2,4,64,384]{4,3,2,0,1:T(8,128)(2,1)S(1)} %pad_maximum_fusion), channel_id=1, source_target_pairs={{24,0},{97,1},{26,2},{99,3},{28,4},{101,5},{30,6},{103,7},{0,8},{1... | collective-permute-start | bytes 4718600 | tf_op jit(solution)/shard_map/ppermute | solution.py:202
  47.3 3.1 %collective-permute-start.13 = (bf16[24,64,384]{2,1,0:T(8,128)(2,1)S(1)}, bf16[24,64,384]{2,1,0:T(8,128)(2,1)S(1)}, u32[]{:S(2)}, u32[]{:S(2)}) collective-permute-start(bf16[24,64,384]{2,1,0:T(8,128)(2,1)S(1)} %get-tuple-element.42), channel_id=1, source_target_pairs={{1,0},{0,1},{3,2},{2,3},{5,4},{4,5},{7,6},{6,7},{9,8},{8,9},{11,10... | collective-permute-start | bytes 3538952 | tf_op jit(solution)/shard_map/ppermute | solution.py:179
  47.9 4.2 %collective-permute-start.14 = (bf16[24,64,384]{2,1,0:T(8,128)(2,1)S(1)}, bf16[24,64,384]{2,1,0:T(8,128)(2,1)S(1)}, u32[]{:S(2)}, u32[]{:S(2)}) collective-permute-start(bf16[24,64,384]{2,1,0:T(8,128)(2,1)S(1)} %get-tuple-element.43), channel_id=1, source_target_pairs={{1,0},{0,1},{3,2},{2,3},{5,4},{4,5},{7,6},{6,7},{9,8},{8,9},{11,10... | collective-permute-start | bytes 3538952 | tf_op jit(solution)/shard_map/ppermute | solution.py:179
  50.4 22.5 %collective-permute-start.15 = (bf16[4,4,64,384]{3,2,1,0:T(8,128)(2,1)S(1)}, bf16[4,4,64,384]{3,2,1,0:T(8,128)(2,1)S(1)}, u32[]{:S(2)}, u32[]{:S(2)}) collective-permute-start(bf16[4,4,64,384]{3,2,1,0:T(8,128)(2,1)S(1)} %slice_bitcast_fusion.1), channel_id=1, source_target_pairs={{1,0},{0,1},{3,2},{2,3},{5,4},{4,5},{7,6},{6,7},{9,8},{8,9},{11,10... | collective-permute-start | bytes 2359304 | tf_op jit(solution)/shard_map/ppermute | solution.py:179
  65.3 41.3 %collective-permute-start.22 = (bf16[2,16,64,384]{3,2,1,0:T(8,128)(2,1)}, bf16[2,16,64,384]{3,2,1,0:T(8,128)(2,1)}, u32[]{:S(2)}, u32[]{:S(2)}) collective-permute-start(bf16[2,16,64,384]{3,2,1,0:T(8,128)(2,1)} %pad_maximum_fusion.2), channel_id=1, source_target_pairs={{16,0},{65,1},{18,2},{67,3},{20,4},{69,5},{22,6},{71,7},{24,8},{73... | collective-permute-start | bytes 4718600 | tf_op jit(solution)/shard_map/ppermute | solution.py:202
  66.8 7.9 %collective-permute-start.16 = (bf16[4,4,64,384]{3,2,1,0:T(8,128)(2,1)S(1)}, bf16[4,4,64,384]{3,2,1,0:T(8,128)(2,1)S(1)}, u32[]{:S(2)}, u32[]{:S(2)}) collective-permute-start(bf16[4,4,64,384]{3,2,1,0:T(8,128)(2,1)S(1)} %slice_bitcast_fusion.6), channel_id=1, source_target_pairs={{1,0},{0,1},{3,2},{2,3},{5,4},{4,5},{7,6},{6,7},{9,8},{8,9},{11,10... | collective-permute-start | bytes 2359304 | tf_op jit(solution)/shard_map/ppermute | solution.py:179
  69.3 6.2 %collective-permute-start.17 = (bf16[4,4,64,384]{3,2,1,0:T(8,128)(2,1)S(1)}, bf16[4,4,64,384]{3,2,1,0:T(8,128)(2,1)S(1)}, u32[]{:S(2)}, u32[]{:S(2)}) collective-permute-start(bf16[4,4,64,384]{3,2,1,0:T(8,128)(2,1)S(1)} %slice_bitcast_fusion.5), channel_id=1, source_target_pairs={{1,0},{0,1},{3,2},{2,3},{5,4},{4,5},{7,6},{6,7},{9,8},{8,9},{11,10... | collective-permute-start | bytes 2359304 | tf_op jit(solution)/shard_map/ppermute | solution.py:179
  69.5 6.1 %collective-permute-start.18 = (bf16[4,4,64,384]{3,2,1,0:T(8,128)(2,1)S(1)}, bf16[4,4,64,384]{3,2,1,0:T(8,128)(2,1)S(1)}, u32[]{:S(2)}, u32[]{:S(2)}) collective-permute-start(bf16[4,4,64,384]{3,2,1,0:T(8,128)(2,1)S(1)} %slice_bitcast_fusion.4), channel_id=1, source_target_pairs={{1,0},{0,1},{3,2},{2,3},{5,4},{4,5},{7,6},{6,7},{9,8},{8,9},{11,10... | collective-permute-start | bytes 2359304 | tf_op jit(solution)/shard_map/ppermute | solution.py:179
  72.9 33.6 %collective-permute-start.23 = (bf16[2,16,64,384]{3,2,1,0:T(8,128)(2,1)}, bf16[2,16,64,384]{3,2,1,0:T(8,128)(2,1)}, u32[]{:S(2)}, u32[]{:S(2)}) collective-permute-start(bf16[2,16,64,384]{3,2,1,0:T(8,128)(2,1)} %pad_maximum_fusion.3), channel_id=1, source_target_pairs={{8,0},{33,1},{10,2},{35,3},{12,4},{37,5},{14,6},{39,7},{16,8},{41,... | collective-permute-start | bytes 4718600 | tf_op jit(solution)/shard_map/ppermute | solution.py:202
  74.7 31.9 %collective-permute-start.21 = (bf16[2,16,64,384]{3,2,1,0:T(8,128)(2,1)}, bf16[2,16,64,384]{3,2,1,0:T(8,128)(2,1)}, u32[]{:S(2)}, u32[]{:S(2)}) collective-permute-start(bf16[2,16,64,384]{3,2,1,0:T(8,128)(2,1)} %pad_maximum_fusion.1), channel_id=1, source_target_pairs={{24,0},{97,1},{26,2},{99,3},{28,4},{101,5},{30,6},{103,7},{0,8},{1... | collective-permute-start | bytes 4718600 | tf_op jit(solution)/shard_map/ppermute | solution.py:202
  75.3 1.7 %copy-start.1 = (bf16[96,384,32]{1,2,0:T(8,128)(2,1)S(1)}, bf16[96,384,32]{1,2,0:T(8,128)(2,1)}, u32[]{:S(2)}) copy-start(bf16[96,384,32]{1,2,0:T(8,128)(2,1)} %param.19) | copy-start | bytes 7077892
  102.9 2.4 %collective-permute-start.20 = (bf16[16,64,384]{2,1,0:T(8,128)(2,1)S(1)}, bf16[16,64,384]{2,1,0:T(8,128)(2,1)S(1)}, u32[]{:S(2)}, u32[]{:S(2)}) collective-permute-start(bf16[16,64,384]{2,1,0:T(8,128)(2,1)S(1)} %get-tuple-element.50), channel_id=1, source_target_pairs={{1,0},{0,1},{3,2},{2,3},{5,4},{4,5},{7,6},{6,7},{9,8},{8,9},{11,10... | collective-permute-start | bytes 2359304 | tf_op jit(solution)/shard_map/ppermute | solution.py:179
  103.0 3.4 %collective-permute-start.19 = (bf16[16,64,384]{2,1,0:T(8,128)(2,1)S(1)}, bf16[16,64,384]{2,1,0:T(8,128)(2,1)S(1)}, u32[]{:S(2)}, u32[]{:S(2)}) collective-permute-start(bf16[16,64,384]{2,1,0:T(8,128)(2,1)S(1)} %get-tuple-element.48), channel_id=1, source_target_pairs={{1,0},{0,1},{3,2},{2,3},{5,4},{4,5},{7,6},{6,7},{9,8},{8,9},{11,10... | collective-permute-start | bytes 2359304 | tf_op jit(solution)/shard_map/ppermute | solution.py:179
  105.3 2.3 %collective-permute-start.25 = (bf16[16,64,384]{2,1,0:T(8,128)(2,1)S(1)}, bf16[16,64,384]{2,1,0:T(8,128)(2,1)S(1)}, u32[]{:S(2)}, u32[]{:S(2)}) collective-permute-start(bf16[16,64,384]{2,1,0:T(8,128)(2,1)S(1)} %get-tuple-element.59), channel_id=1, source_target_pairs={{1,0},{0,1},{3,2},{2,3},{5,4},{4,5},{7,6},{6,7},{9,8},{8,9},{11,10... | collective-permute-start | bytes 2359304 | tf_op jit(solution)/shard_map/ppermute | solution.py:179
  105.6 1.2 copy-start.5
  106.9 17.9 %collective-permute-start.24 = (bf16[16,64,384]{2,1,0:T(8,128)(2,1)S(1)}, bf16[16,64,384]{2,1,0:T(8,128)(2,1)S(1)}, u32[]{:S(2)}, u32[]{:S(2)}) collective-permute-start(bf16[16,64,384]{2,1,0:T(8,128)(2,1)S(1)} %pad_maximum_fusion.4), channel_id=1, source_target_pairs={{6,0},{3,1},{0,2},{5,3},{2,4},{7,5},{4,6},{1,7},{14,8},{11,9},{8,1... | collective-permute-start | bytes 2359304 | tf_op jit(solution)/shard_map/ppermute | solution.py:227
  111.0 8.4 %collective-permute-start.26 = (bf16[2,4,64,384]{3,2,1,0:T(8,128)(2,1)S(1)}, bf16[2,4,64,384]{3,2,1,0:T(8,128)(2,1)S(1)}, u32[]{:S(2)}, u32[]{:S(2)}) collective-permute-start(bf16[2,4,64,384]{3,2,1,0:T(8,128)(2,1)S(1)} %get-tuple-element.69), channel_id=1, source_target_pairs={{96,0},{25,1},{98,2},{27,3},{100,4},{29,5},{102,6},{31,7},{104,8},... | collective-permute-start | bytes 1179656 | tf_op jit(solution)/shard_map/ppermute | solution.py:202
  112.1 12.7 %collective-permute-start.27 = (bf16[2,4,64,384]{3,2,1,0:T(8,128)(2,1)S(1)}, bf16[2,4,64,384]{3,2,1,0:T(8,128)(2,1)S(1)}, u32[]{:S(2)}, u32[]{:S(2)}) collective-permute-start(bf16[2,4,64,384]{3,2,1,0:T(8,128)(2,1)S(1)} %get-tuple-element.68), channel_id=1, source_target_pairs={{64,0},{17,1},{66,2},{19,3},{68,4},{21,5},{70,6},{23,7},{72,8},{25... | collective-permute-start | bytes 1179656 | tf_op jit(solution)/shard_map/ppermute | solution.py:202
  115.2 9.6 %collective-permute-start.28 = (bf16[2,4,64,384]{3,2,1,0:T(8,128)(2,1)S(1)}, bf16[2,4,64,384]{3,2,1,0:T(8,128)(2,1)S(1)}, u32[]{:S(2)}, u32[]{:S(2)}) collective-permute-start(bf16[2,4,64,384]{3,2,1,0:T(8,128)(2,1)S(1)} %get-tuple-element.67), channel_id=1, source_target_pairs={{32,0},{9,1},{34,2},{11,3},{36,4},{13,5},{38,6},{15,7},{40,8},{17,... | collective-permute-start | bytes 1179656 | tf_op jit(solution)/shard_map/ppermute | solution.py:202
  126.4 7.6 %collective-permute-start.30 = (bf16[8,64,384]{2,1,0:T(8,128)(2,1)}, bf16[8,64,384]{2,1,0:T(8,128)(2,1)S(1)}, u32[]{:S(2)}, u32[]{:S(2)}) collective-permute-start(bf16[8,64,384]{2,1,0:T(8,128)(2,1)} %add_convert_fusion), channel_id=1, source_target_pairs={{6,0},{3,1},{0,2},{5,3},{2,4},{7,5},{4,6},{1,7},{14,8},{11,9},{8,1... | collective-permute-start | bytes 1179656 | tf_op jit(solution)/shard_map/ppermute | solution.py:231
  130.0 4.1 %collective-permute-start.31 = (f32[4,64,384]{2,1,0:T(8,128)}, f32[4,64,384]{2,1,0:T(8,128)}, u32[]{:S(2)}, u32[]{:S(2)}) collective-permute-start(f32[4,64,384]{2,1,0:T(8,128)} %get-tuple-element.71), channel_id=1, source_target_pairs={{1,0},{0,1},{3,2},{2,3},{5,4},{4,5},{7,6},{6,7},{9,8},{8,9},{11,10... | collective-permute-start | bytes 1179656 | tf_op jit(solution)/shard_map/ppermute | solution.py:179
  130.2 3.8 %collective-permute-start.29 = (bf16[8,64,384]{2,1,0:T(8,128)(2,1)}, bf16[8,64,384]{2,1,0:T(8,128)(2,1)}, u32[]{:S(2)}, u32[]{:S(2)}) collective-permute-start(bf16[8,64,384]{2,1,0:T(8,128)(2,1)} %slice.80), channel_id=1, source_target_pairs={{1,0},{0,1},{3,2},{2,3},{5,4},{4,5},{7,6},{6,7},{9,8},{8,9},{11,10... | collective-permute-start | bytes 1179656 | tf_op jit(solution)/shard_map/ppermute | solution.py:179
  130.5 3.5 %copy-start.6 = (f32[16,64,384]{2,1,0:T(8,128)S(1)}, f32[16,64,384]{2,1,0:T(8,128)}, u32[]{:S(2)}) copy-start(f32[16,64,384]{2,1,0:T(8,128)} %copy-done.5) | copy-start | bytes 4718596

commit v2 on v1

--- a/solution.py
+++ b/solution.py
@@ -193,8 +193,7 @@
 ):
     dof = load_vectors.shape[2]
     panel_of = jnp.arange(dof) % (dof // 3)
-    live_dofs = (panel_of[None, :] < live_panels[:, None]).astype(jnp.bfloat16)
-    masked = load_vectors * live_dofs[:, None, :]
+    masked = load_vectors * (panel_of[None, :] < live_panels[:, None]).astype(jnp.bfloat16)[:, None, :]
     core = lax.axis_index("col") % 2
     twin = swap(masked)
     part = lambda v: lax.dynamic_slice_in_dim(v, core * (PER // 2), PER // 2)
@@ -205,7 +204,7 @@
     x_cross = lax.ppermute(twin, "col", chip)
     line = [plane(own, 1, step) for step in (1, 3, 2)]
     x_two = lax.ppermute(x_near, "col", chip)
-    x_near, x_cross, x_two, line = lax.optimization_barrier((x_near, x_cross, x_two, line))
+    x_near, x_cross, line = lax.optimization_barrier((x_near, x_cross, line))
     line = jnp.stack([own, line[0], line[2], line[1]])
     cols = [line] + [plane(line, 0, step) for step in (1, 2, 3)]
     rows = [masked, twin, x_near, x_cross, swap(x_near), swap(x_cross), x_two, swap(x_two)]
@@ -224,18 +223,23 @@
     row_near = wide(to_rows[2]) + wide(swap(to_rows[0]))
     row_far = wide(to_rows[3]) + wide(swap(to_rows[1]))
     row_near, row_far, sums_in = lax.optimization_barrier((row_near, row_far, sums_in))
-    forth = lax.ppermute(narrow(jnp.concatenate([row_far[:PER], row_near[PER:]])), "col", chip)
-    line_sum = (wide(sums[3]) + sum(wide(v) for v in sums_in)).reshape((2, SIDE, PER // 2) + masked.shape[1:])
-    ends = [plane(narrow(line_sum[:, step]), 1, -step) for step in (1, 2, 3)]
-    forth, ends = lax.optimization_barrier((forth, ends))
-    forth_two = lax.ppermute(narrow(row_near[:PER] + wide(forth[:PER])), "col", chip)
-    row_part = [row_far[PER:], swap(forth[PER:]), forth_two]
-    end = line_sum[:, 0] + sum(wide(v) for v in ends)
-    end_in = swap(end[1])
-    col_part = jnp.where(core == 0, jnp.concatenate([end[0], end_in]), jnp.concatenate([end_in, end[0]]))
+    forth = lax.ppermute(narrow(row_far[:PER]), "col", chip)
+    cross = lax.ppermute(narrow(row_near[PER:]), "col", chip)
+    split = lambda v: v.reshape((2, SIDE, PER // 2) + masked.shape[1:])
+    line_in = [split(v) for v in [sums[3], *sums_in]]
+    block = lambda step: sum(wide(v[:, step]) for v in line_in)
+    ends = [plane(narrow(block(step)), 1, -step) for step in (1, 2, 3)]
+    forth_two = lax.ppermute(narrow(row_near[:PER] + wide(forth)), "col", chip)
+    forth_two, ends = lax.optimization_barrier((forth_two, ends))
+    end = block(0)
+    end_in = wide(swap(narrow(end[1] + sum(wide(v[1]) for v in ends))))
+    end_own = end[0] + sum(wide(v[0]) for v in ends)
     own_part = jnp.einsum("cld,ced->cle", masked, self_blocks, preferred_element_type=jnp.float32)
-    total = own_part + sum(wide(v) for v in row_part) + col_part
-    return total * live_dofs.astype(jnp.float32)[:, None, :]
+    base = own_part + row_far[PER:] + wide(swap(cross)) + wide(forth_two)
+    base, end_in = lax.optimization_barrier((base, end_in))
+    total = base + jnp.where(core == 0, jnp.concatenate([end_own, end_in]), jnp.concatenate([end_in, end_own]))
+    live_out = (panel_of[None, :] < lax.optimization_barrier(live_panels)[:, None]).astype(jnp.float32)
+    return total * live_out[:, None, :]
 
 
 def solution(mesh):

time: 138 us -> 132 us (0.957)
  waiting for transfers between devices: 37.2 us -> 28.5 us
  starting transfers between devices: 34.5 us -> 39 us
  local copies, waits for them, and re-layouts: 4.84 us -> 1.69 us
    ppermute x15, starting transfers between devices: 8.85 us -> 15.6 us  [swap(): return lax.ppermute(v, 'col', col_shift(0, 1))]
    ppermute x12, waiting for transfers between devices: 27.8 us -> 21.1 us  [local(): lax.ppermute(v, ('row', 'col'), plane_shift(first, step))]
    add x2 -> x4, other arithmetic: 3.48 us -> 5.39 us  [the longest x2 2.62 us: local(): block = lambda step: sum((wide(v[:, step]) for v in line_in))]
    mul x2, other arithmetic: 3.47 us -> 2.04 us  [the longest x1 1.04 us: local(): load_vectors * (panel_of[None, :] < live_panels[:, None]).astype(jnp.bflo...]
  transfers between devices with their start and end apart: 32 -> 33, of which waited for: 12 -> 9; matrix products, arithmetic and copies ran while one was open for 9% -> 11% of each run, Pallas kernels for 33% -> 34%
where the time goes in v2:
time: 132 us; the launch traced here: 131 us
  Pallas kernels  45.3 us (34%)
  starting transfers between devices  39 us (30%)
  waiting for transfers between devices  28.5 us (22%)
  other arithmetic  14 us (11%)
  matrix products  1.83 us (1%)
  local copies, waits for them, and re-layouts  1.69 us (1%)
    pallas_call x2, Pallas kernels, pair_product(): pl.pallas_call(functools.partial(pair_kernel, flip, src_of, dst_of, (in_s...  45.3 us
    ppermute x12, waiting for transfers between devices, local(): lax.ppermute(v, ('row', 'col'), plane_shift(first, step))  21.1 us
    ppermute x12, starting transfers between devices, local(): lax.ppermute(v, ('row', 'col'), plane_shift(first, step))  16.9 us
    ppermute x15, starting transfers between devices, swap(): return lax.ppermute(v, 'col', col_shift(0, 1))  15.6 us
    ppermute x15, waiting for transfers between devices, swap(): return lax.ppermute(v, 'col', col_shift(0, 1))  6.19 us
    another operation x4, other arithmetic, local(): sums = [jnp.stack([to_cols[k], theirs[k]]) for k in range(SIDE)]  4.15 us
  transfers between devices with their start and end apart: 33, of which 9 were waited for; matrix products, arithmetic and copies ran while one was open for 11% of the time, Pallas kernels for 34%

profile of v2, /device:TPU:1, one launch (start us, length us, event | category | flops | bytes accessed | tf_op | source)
XLA Modules:
  0.0 131.4 jit_solution(12398923158155856623)
XLA Ops:
  0.0 0.9 compare_convert_fusion
  0.9 1.0 broadcast_multiply_fusion.refs_0_
  1.9 1.5 %collective-permute-start = (bf16[8,64,384]{2,1,0:T(8,128)(2,1)S(1)}, bf16[8,64,384]{2,1,0:T(8,128)(2,1)S(1)}, u32[]{:S(2)}, u32[]{:S(2)}) collective-permute-start(bf16[8,64,384]{2,1,0:T(8,128)(2,1)S(1)} %broadcast_multiply_fusion.refs_0_), channel_id=1, source_target_pairs={{1,0},{0,1},{3,2},{2,3},{5,4},{4,5},{7,6},{6,7},{9,8},{8,9},{11,10... | collective-permute-start | bytes 1179656 | tf_op jit(solution)/shard_map/ppermute | solution.py:179
  3.4 2.6 %collective-permute-start.1 = (bf16[8,64,384]{2,1,0:T(8,128)(2,1)S(1)}, bf16[8,64,384]{2,1,0:T(8,128)(2,1)S(1)}, u32[]{:S(2)}, u32[]{:S(2)}) collective-permute-start(bf16[8,64,384]{2,1,0:T(8,128)(2,1)S(1)} %broadcast_multiply_fusion.refs_0_), channel_id=1, source_target_pairs={{6,0},{3,1},{0,2},{5,3},{2,4},{7,5},{4,6},{1,7},{14,8},{11,9},{8,1... | collective-permute-start | bytes 1179656 | tf_op jit(solution)/shard_map/ppermute | solution.py:203
  6.2 3.8 %collective-permute-start.3 = (bf16[2,4,64,384]{3,2,1,0:T(8,128)(2,1)S(1)}, bf16[2,4,64,384]{3,2,1,0:T(8,128)(2,1)S(1)}, u32[]{:S(2)}, u32[]{:S(2)}) collective-permute-start(bf16[2,4,64,384]{3,2,1,0:T(8,128)(2,1)S(1)} %get-tuple-element.75), channel_id=1, source_target_pairs={{32,0},{9,1},{34,2},{11,3},{36,4},{13,5},{38,6},{15,7},{40,8},{17,... | collective-permute-start | bytes 1179656 | tf_op jit(solution)/shard_map/ppermute | solution.py:201
  10.0 1.3 collective-permute-start.5
  11.3 1.3 collective-permute-start.2
  12.6 1.2 collective-permute-start.11
  13.8 5.1 %collective-permute-done.3 = bf16[2,4,64,384]{3,2,1,0:T(8,128)(2,1)S(1)} collective-permute-done((bf16[2,4,64,384]{3,2,1,0:T(8,128)(2,1)S(1)}, bf16[2,4,64,384]{3,2,1,0:T(8,128)(2,1)S(1)}, u32[]{:S(2)}, u32[]{:S(2)}) %collective-permute-start.3) | collective-permute-done | bytes 393248 | tf_op jit(solution)/shard_map/ppermute | solution.py:201
  18.9 3.4 %collective-permute-done.4 = bf16[2,4,64,384]{3,2,1,0:T(8,128)(2,1)S(1)} collective-permute-done((bf16[2,4,64,384]{3,2,1,0:T(8,128)(2,1)S(1)}, bf16[2,4,64,384]{3,2,1,0:T(8,128)(2,1)S(1)}, u32[]{:S(2)}, u32[]{:S(2)}) %collective-permute-start.4) | collective-permute-done | bytes 393248 | tf_op jit(solution)/shard_map/ppermute | solution.py:201
  22.3 0.5 collective-permute-start.9
  22.9 1.0 collective-permute-start.12
  23.9 0.2 pad_maximum_fusion
  24.1 1.6 %collective-permute-start.6 = (bf16[4,2,4,64,384]{4,3,2,0,1:T(8,128)(2,1)S(1)}, bf16[4,2,4,64,384]{4,3,2,0,1:T(8,128)(2,1)S(1)}, u32[]{:S(2)}, u32[]{:S(2)}) collective-permute-start(bf16[4,2,4,64,384]{4,3,2,0,1:T(8,128)(2,1)S(1)} %pad_maximum_fusion), channel_id=1, source_target_pairs={{8,0},{33,1},{10,2},{35,3},{12,4},{37,5},{14,6},{39,7},{16,8},{41,... | collective-permute-start | bytes 4718600 | tf_op jit(solution)/shard_map/ppermute | solution.py:201
  25.7 1.9 %collective-permute-start.7 = (bf16[4,2,4,64,384]{4,3,2,0,1:T(8,128)(2,1)S(1)}, bf16[4,2,4,64,384]{4,3,2,0,1:T(8,128)(2,1)S(1)}, u32[]{:S(2)}, u32[]{:S(2)}) collective-permute-start(bf16[4,2,4,64,384]{4,3,2,0,1:T(8,128)(2,1)S(1)} %pad_maximum_fusion), channel_id=1, source_target_pairs={{16,0},{65,1},{18,2},{67,3},{20,4},{69,5},{22,6},{71,7},{24,8},{73... | collective-permute-start | bytes 4718600 | tf_op jit(solution)/shard_map/ppermute | solution.py:201
  28.3 18.9 %shard_map.100 = (bf16[16,64,384]{2,1,0:T(8,128)(2,1)S(1)}, bf16[16,64,384]{2,1,0:T(8,128)(2,1)S(1)}, bf16[16,64,384]{2,1,0:T(8,128)(2,1)S(1)}, bf16[16,64,384]{...) custom-call(s32[2,48]{1,0:T(2,128)S(1)} %bitcast.94, ...), custom_call_target="tpu_custom_call" | custom-call | flops 905969664 | bytes 18874368 | tf_op jit(solution)/shard_map/pallas_call | solution.py:90
  47.1 0.1 collective-permute-start.13
  47.2 0.5 collective-permute-start.14
  47.7 0.2 copy.14.refs_0_
  47.9 0.1 slice_bitcast_fusion
  48.0 2.1 %collective-permute-done.13 = bf16[24,64,384]{2,1,0:T(8,128)(2,1)S(1)} collective-permute-done((bf16[24,64,384]{2,1,0:T(8,128)(2,1)S(1)}, bf16[24,64,384]{2,1,0:T(8,128)(2,1)S(1)}, u32[]{:S(2)}, u32[]{:S(2)}) %collective-permute-start.13) | collective-permute-done | bytes 1179680 | tf_op jit(solution)/shard_map/ppermute | solution.py:179
  50.1 0.1 collective-permute-start.15
  50.2 1.5 %collective-permute-done.14 = bf16[24,64,384]{2,1,0:T(8,128)(2,1)S(1)} collective-permute-done((bf16[24,64,384]{2,1,0:T(8,128)(2,1)S(1)}, bf16[24,64,384]{2,1,0:T(8,128)(2,1)S(1)}, u32[]{:S(2)}, u32[]{:S(2)}) %collective-permute-start.14) | collective-permute-done | bytes 1179680 | tf_op jit(solution)/shard_map/ppermute | solution.py:179
  51.8 11.9 %collective-permute-done.8 = bf16[4,2,4,64,384]{4,3,2,0,1:T(8,128)(2,1)S(1)} collective-permute-done((bf16[4,2,4,64,384]{4,3,2,0,1:T(8,128)(2,1)S(1)}, bf16[4,2,4,64,384]{4,3,2,0,1:T(8,128)(2,1)S(1)}, u32[]{:S(2)}, u32[]{:S(2)}) %collective-permute-start.8) | collective-permute-done | bytes 1572896 | tf_op jit(solution)/shard_map/ppermute | solution.py:201
  63.6 0.1 slice_bitcast_fusion.5
  63.7 0.2 copy.15.refs_1_
  63.9 0.1 slice_bitcast_fusion.4
  64.0 0.2 copy.16.refs_2_
  64.2 0.1 slice_bitcast_fusion.3
  64.3 0.2 copy.17.refs_3_
  64.6 0.1 maximum_bitcast_fusion
  64.7 1.3 %pad_maximum_fusion.2 = bf16[2,16,64,384]{3,2,1,0:T(8,128)(2,1)} fusion(bf16[1,16,64,384]{3,2,1,0:T(8,128)(2,1)S(1)} %maximum_bitcast_fusion, bf16[1,16,64,384]{3,2,1,0:T(8,128)(2,1)S(1)} %bitcast.93), kind=kLoop, calls=%fused_computation.8 | loop fusion | flops 786432 | bytes 3145728 | tf_op jit(solution)/shard_map/stack | solution.py:218
  66.0 1.5 %collective-permute-start.22 = (bf16[2,16,64,384]{3,2,1,0:T(8,128)(2,1)}, bf16[2,16,64,384]{3,2,1,0:T(8,128)(2,1)S(1)}, u32[]{:S(2)}, u32[]{:S(2)}) collective-permute-start(bf16[2,16,64,384]{3,2,1,0:T(8,128)(2,1)} %pad_maximum_fusion.2), channel_id=1, source_target_pairs={{16,0},{65,1},{18,2},{67,3},{20,4},{69,5},{22,6},{71,7},{24,8},{73... | collective-permute-start | bytes 4718600 | tf_op jit(solution)/shard_map/ppermute | solution.py:201
  67.5 1.9 %collective-permute-start.16 = (bf16[4,4,64,384]{3,2,1,0:T(8,128)(2,1)S(1)}, bf16[4,4,64,384]{3,2,1,0:T(8,128)(2,1)S(1)}, u32[]{:S(2)}, u32[]{:S(2)}) collective-permute-start(bf16[4,4,64,384]{3,2,1,0:T(8,128)(2,1)S(1)} %slice_bitcast_fusion.5), channel_id=1, source_target_pairs={{1,0},{0,1},{3,2},{2,3},{5,4},{4,5},{7,6},{6,7},{9,8},{8,9},{11,10... | collective-permute-start | bytes 2359304 | tf_op jit(solution)/shard_map/ppermute | solution.py:179
  69.4 0.5 collective-permute-start.18
  69.9 0.1 slice_bitcast_fusion.1
  70.0 1.3 %pad_maximum_fusion.3 = bf16[2,16,64,384]{3,2,1,0:T(8,128)(2,1)} fusion(bf16[1,16,64,384]{3,2,1,0:T(8,128)(2,1)S(1)} %slice_bitcast_fusion.1, bf16[1,16,64,384]{3,2,1,0:T(8,128)(2,1)S(1)} %bitcast.92), kind=kLoop, calls=%fused_computation.9 | loop fusion | flops 786432 | bytes 3145728 | tf_op jit(solution)/shard_map/stack | solution.py:218
  71.5 1.4 %pad_maximum_fusion.1 = bf16[2,16,64,384]{3,2,1,0:T(8,128)(2,1)} fusion(bf16[1,16,64,384]{3,2,1,0:T(8,128)(2,1)S(1)} %slice_bitcast_fusion.2, bf16[1,16,64,384]{3,2,1,0:T(8,128)(2,1)S(1)} %bitcast.91), kind=kLoop, calls=%fused_computation.7 | loop fusion | flops 786432 | bytes 3145728 | tf_op jit(solution)/shard_map/stack | solution.py:218
  72.8 1.8 %collective-permute-start.23 = (bf16[2,16,64,384]{3,2,1,0:T(8,128)(2,1)}, bf16[2,16,64,384]{3,2,1,0:T(8,128)(2,1)S(1)}, u32[]{:S(2)}, u32[]{:S(2)}) collective-permute-start(bf16[2,16,64,384]{3,2,1,0:T(8,128)(2,1)} %pad_maximum_fusion.3), channel_id=1, source_target_pairs={{8,0},{33,1},{10,2},{35,3},{12,4},{37,5},{14,6},{39,7},{16,8},{41,... | collective-permute-start | bytes 4718600 | tf_op jit(solution)/shard_map/ppermute | solution.py:201
  74.6 26.4 %shard_map.101 = (bf16[16,64,384]{2,1,0:T(8,128)(2,1)S(1)}, bf16[16,64,384]{2,1,0:T(8,128)(2,1)S(1)}, bf16[16,64,384]{2,1,0:T(8,128)(2,1)S(1)}, bf16[16,64,384]{2,1,0:T(8,128)(2,1)S(1)}) custom-call(s32[2,48]{1,0:T(2,128)S(1)} %bitcast.95, s32[1]{0:T(128)S(6)} %copy.26.near_count, s32[2,96]{1,0:T(2,128)S(1)} %bitcast.97, s32[96]{0:T(128)S(1)} %copy-done.4, ...), custom_call_target="tpu_custom_call" | custom-call | flops 905969664 | bytes 18874368 | tf_op jit(solution)/shard_map/pallas_call | solution.py:90
  101.1 0.1 collective-permute-start.20
  101.2 0.5 collective-permute-start.19
  101.7 1.8 %collective-permute-done.20 = bf16[16,64,384]{2,1,0:T(8,128)(2,1)S(1)} collective-permute-done((bf16[16,64,384]{2,1,0:T(8,128)(2,1)S(1)}, bf16[16,64,384]{2,1,0:T(8,128)(2,1)S(1)}, u32[]{:S(2)}, u32[]{:S(2)}) %collective-permute-start.20) | collective-permute-done | bytes 786464 | tf_op jit(solution)/shard_map/ppermute | solution.py:179
  103.5 0.1 collective-permute-start.28
  103.6 0.2 convert_add_fusion
  103.8 0.8 collective-permute-done.19
  104.6 0.2 convert_add_fusion.1
  104.8 0.2 copy-done.5
  105.0 1.3 collective-permute-start.26
  106.4 0.1 collective-permute-start.24
  106.5 1.6 %convert_add_fusion.2 = (f32[2,1,4,64,384]{4,3,2,1,0:T(8,128)S(1)}, bf16[2,4,64,384]{3,2,1,0:T(8,128)(2,1)}, bf16[2,4,64,384]{3,2,1,0:T(8,128)(2,1)}) fusion(bf16[2,4,4,64,384]{4,3,2,1,0:T(8,128)(2,1)S(1)} %bitcast.104, bf16[2,4,4,64,384]{4,3,2,1,0:T(8,128)(2,1)S(1)} %bitcast.102, bf16[2,4,4,64,384]{4,3,2,1,0:T(8,128)(2,1)S(1)} %bitcast.106, ...), kind=kLoop, calls=%fused_computation.19 | loop fusion | flops 5111808 | bytes 6684672 | tf_op jit(solution)/shard_map/add | solution.py:230
  108.1 1.0 fusion.2
  109.1 2.0 %collective-permute-start.30 = (bf16[2,4,64,384]{3,2,1,0:T(8,128)(2,1)}, bf16[2,4,64,384]{3,2,1,0:T(8,128)(2,1)}, u32[]{:S(2)}, u32[]{:S(2)}) collective-permute-start(bf16[2,4,64,384]{3,2,1,0:T(8,128)(2,1)} %get-tuple-element.71), channel_id=1, source_target_pairs={{64,0},{17,1},{66,2},{19,3},{68,4},{21,5},{70,6},{23,7},{72,8},{25... | collective-permute-start | bytes 1179656 | tf_op jit(solution)/shard_map/ppermute | solution.py:201
  111.1 2.4 %collective-permute-start.31 = (bf16[2,4,64,384]{3,2,1,0:T(8,128)(2,1)}, bf16[2,4,64,384]{3,2,1,0:T(8,128)(2,1)}, u32[]{:S(2)}, u32[]{:S(2)}) collective-permute-start(bf16[2,4,64,384]{3,2,1,0:T(8,128)(2,1)} %get-tuple-element.70), channel_id=1, source_target_pairs={{32,0},{9,1},{34,2},{11,3},{36,4},{13,5},{38,6},{15,7},{40,8},{17,... | collective-permute-start | bytes 1179656 | tf_op jit(solution)/shard_map/ppermute | solution.py:201
  113.5 0.6 collective-permute-start.29
  114.1 0.8 add_convert_fusion.3
  115.0 1.2 collective-permute-done.24
  116.2 5.3 %collective-permute-start.25 = (bf16[8,64,384]{2,1,0:T(8,128)(2,1)}, bf16[8,64,384]{2,1,0:T(8,128)(2,1)}, u32[]{:S(2)}, u32[]{:S(2)}) collective-permute-start(bf16[8,64,384]{2,1,0:T(8,128)(2,1)} %collective-permute-done.24), channel_id=1, source_target_pairs={{1,0},{0,1},{3,2},{2,3},{5,4},{4,5},{7,6},{6,7},{9,8},{8,9},{11,10... | collective-permute-start | bytes 1179656 | tf_op jit(solution)/shard_map/ppermute | solution.py:179
  121.6 1.8 %fusion.18 = f32[8,64,384]{2,1,0:T(8,128)} fusion(bf16[8,64,384]{2,1,0:T(8,128)(2,1)S(1)} %broadcast_multiply_fusion.refs_0_, bf16[8,384,384]{2,1,0:T(8,128)(2,1)S(1)} %copy-done), kind=kOutput, calls=%fused_computation.60 | convolution fusion | flops 150994944 | bytes 3538944 | tf_op jit(solution)/shard_map/cld,ced->cle/dot_general | solution.py:237
  123.4 0.7 collective-permute-done.31
  124.1 1.5 %fusion.10 = (f32[4,64,384]{2,1,0:T(8,128)S(1)}, bf16[4,64,384]{2,1,0:T(8,128)(2,1)S(1)}) fusion(f32[2,1,4,64,384]{4,3,2,1,0:T(8,128)S(1)} %get-tuple-element.69, bf16[2,4,64,384]{3,2,1,0:T(8,128)(2,1)} %collective-permute-done.31, bf16[2,4,64,384]{3,2,1,0:T(8,128)(2,1)} %collective-permute-done.30, bf16[2,4,64,384]{3,2,1,0:T(8,128)(2,1)} %collective-permute-done.29), kind=kLoop, calls=%fused_computation.39 | loop fusion | flops 1277952 | bytes 2555904 | tf_op jit(solution)/shard_map/add | solution.py:236
  125.7 3.4 %collective-permute-start.32 = (bf16[4,64,384]{2,1,0:T(8,128)(2,1)S(1)}, bf16[4,64,384]{2,1,0:T(8,128)(2,1)S(1)}, u32[]{:S(2)}, u32[]{:S(2)}) collective-permute-start(bf16[4,64,384]{2,1,0:T(8,128)(2,1)S(1)} %get-tuple-element.73), channel_id=1, source_target_pairs={{1,0},{0,1},{3,2},{2,3},{5,4},{4,5},{7,6},{6,7},{9,8},{8,9},{11,10... | collective-permute-start | bytes 589832 | tf_op jit(solution)/shard_map/ppermute | solution.py:179
  129.1 1.3 convert_add_fusion.3
  130.4 1.0 fusion.1
  (55 shorter events, 0.6 us)
Async XLA Ops:
  0.0 121.6 %copy-start = (bf16[8,384,384]{2,1,0:T(8,128)(2,1)S(1)}, bf16[8,384,384]{2,1,0:T(8,128)(2,1)}, u32[]{:S(2)}) copy-start(bf16[8,384,384]{2,1,0:T(8,128)(2,1)} %param.12) | copy-start | bytes 7077892
  1.9 4.1 %collective-permute-start = (bf16[8,64,384]{2,1,0:T(8,128)(2,1)S(1)}, bf16[8,64,384]{2,1,0:T(8,128)(2,1)S(1)}, u32[]{:S(2)}, u32[]{:S(2)}) collective-permute-start(bf16[8,64,384]{2,1,0:T(8,128)(2,1)S(1)} %broadcast_multiply_fusion.refs_0_), channel_id=1, source_target_pairs={{1,0},{0,1},{3,2},{2,3},{5,4},{4,5},{7,6},{6,7},{9,8},{8,9},{11,10... | collective-permute-start | bytes 1179656 | tf_op jit(solution)/shard_map/ppermute | solution.py:179
  3.4 9.2 %collective-permute-start.1 = (bf16[8,64,384]{2,1,0:T(8,128)(2,1)S(1)}, bf16[8,64,384]{2,1,0:T(8,128)(2,1)S(1)}, u32[]{:S(2)}, u32[]{:S(2)}) collective-permute-start(bf16[8,64,384]{2,1,0:T(8,128)(2,1)S(1)} %broadcast_multiply_fusion.refs_0_), channel_id=1, source_target_pairs={{6,0},{3,1},{0,2},{5,3},{2,4},{7,5},{4,6},{1,7},{14,8},{11,9},{8,1... | collective-permute-start | bytes 1179656 | tf_op jit(solution)/shard_map/ppermute | solution.py:203
  6.2 12.8 %collective-permute-start.3 = (bf16[2,4,64,384]{3,2,1,0:T(8,128)(2,1)S(1)}, bf16[2,4,64,384]{3,2,1,0:T(8,128)(2,1)S(1)}, u32[]{:S(2)}, u32[]{:S(2)}) collective-permute-start(bf16[2,4,64,384]{3,2,1,0:T(8,128)(2,1)S(1)} %get-tuple-element.75), channel_id=1, source_target_pairs={{32,0},{9,1},{34,2},{11,3},{36,4},{13,5},{38,6},{15,7},{40,8},{17,... | collective-permute-start | bytes 1179656 | tf_op jit(solution)/shard_map/ppermute | solution.py:201
  10.0 12.3 %collective-permute-start.4 = (bf16[2,4,64,384]{3,2,1,0:T(8,128)(2,1)S(1)}, bf16[2,4,64,384]{3,2,1,0:T(8,128)(2,1)S(1)}, u32[]{:S(2)}, u32[]{:S(2)}) collective-permute-start(bf16[2,4,64,384]{3,2,1,0:T(8,128)(2,1)S(1)} %get-tuple-element.75), channel_id=1, source_target_pairs={{96,0},{25,1},{98,2},{27,3},{100,4},{29,5},{102,6},{31,7},{104,8},... | collective-permute-start | bytes 1179656 | tf_op jit(solution)/shard_map/ppermute | solution.py:201
  10.0 12.3 %collective-permute-start.5 = (bf16[2,4,64,384]{3,2,1,0:T(8,128)(2,1)S(1)}, bf16[2,4,64,384]{3,2,1,0:T(8,128)(2,1)S(1)}, u32[]{:S(2)}, u32[]{:S(2)}) collective-permute-start(bf16[2,4,64,384]{3,2,1,0:T(8,128)(2,1)S(1)} %get-tuple-element.75), channel_id=1, source_target_pairs={{64,0},{17,1},{66,2},{19,3},{68,4},{21,5},{70,6},{23,7},{72,8},{25... | collective-permute-start | bytes 1179656 | tf_op jit(solution)/shard_map/ppermute | solution.py:201
  11.3 11.0 %collective-permute-start.2 = (bf16[8,64,384]{2,1,0:T(8,128)(2,1)S(1)}, bf16[8,64,384]{2,1,0:T(8,128)(2,1)S(1)}, u32[]{:S(2)}, u32[]{:S(2)}) collective-permute-start(bf16[8,64,384]{2,1,0:T(8,128)(2,1)S(1)} %collective-permute-done.refs_1_), channel_id=1, source_target_pairs={{6,0},{3,1},{0,2},{5,3},{2,4},{7,5},{4,6},{1,7},{14,8},{11,9},{8,1... | collective-permute-start | bytes 1179656 | tf_op jit(solution)/shard_map/ppermute | solution.py:204
  12.6 10.3 %collective-permute-start.11 = (bf16[8,64,384]{2,1,0:T(8,128)(2,1)S(1)}, bf16[8,64,384]{2,1,0:T(8,128)(2,1)S(1)}, u32[]{:S(2)}, u32[]{:S(2)}) collective-permute-start(bf16[8,64,384]{2,1,0:T(8,128)(2,1)S(1)} %collective-permute-done.1.refs_2_), channel_id=1, source_target_pairs={{6,0},{3,1},{0,2},{5,3},{2,4},{7,5},{4,6},{1,7},{14,8},{11,9},{8,1... | collective-permute-start | bytes 1179656 | tf_op jit(solution)/shard_map/ppermute | solution.py:206
  22.3 5.2 %collective-permute-start.10 = (bf16[8,64,384]{2,1,0:T(8,128)(2,1)S(1)}, bf16[8,64,384]{2,1,0:T(8,128)(2,1)S(1)}, u32[]{:S(2)}, u32[]{:S(2)}) collective-permute-start(bf16[8,64,384]{2,1,0:T(8,128)(2,1)S(1)} %collective-permute-done.2.refs_3_), channel_id=1, source_target_pairs={{1,0},{0,1},{3,2},{2,3},{5,4},{4,5},{7,6},{6,7},{9,8},{8,9},{11,10... | collective-permute-start | bytes 1179656 | tf_op jit(solution)/shard_map/ppermute | solution.py:179
  22.3 5.9 %collective-permute-start.9 = (bf16[8,64,384]{2,1,0:T(8,128)(2,1)S(1)}, bf16[8,64,384]{2,1,0:T(8,128)(2,1)S(1)}, u32[]{:S(2)}, u32[]{:S(2)}) collective-permute-start(bf16[8,64,384]{2,1,0:T(8,128)(2,1)S(1)} %collective-permute-done.1.refs_2_), channel_id=1, source_target_pairs={{1,0},{0,1},{3,2},{2,3},{5,4},{4,5},{7,6},{6,7},{9,8},{8,9},{11,10... | collective-permute-start | bytes 1179656 | tf_op jit(solution)/shard_map/ppermute | solution.py:179
  22.9 5.4 %collective-permute-start.12 = (bf16[8,64,384]{2,1,0:T(8,128)(2,1)S(1)}, bf16[8,64,384]{2,1,0:T(8,128)(2,1)S(1)}, u32[]{:S(2)}, u32[]{:S(2)}) collective-permute-start(bf16[8,64,384]{2,1,0:T(8,128)(2,1)S(1)} %collective-permute-done.11.refs_6_), channel_id=1, source_target_pairs={{1,0},{0,1},{3,2},{2,3},{5,4},{4,5},{7,6},{6,7},{9,8},{8,9},{11,10... | collective-permute-start | bytes 1179656 | tf_op jit(solution)/shard_map/ppermute | solution.py:179
  23.8 4.4 %copy-start.2 = (s32[48,2]{0,1:T(2,128)S(1)}, s32[48,2]{0,1:T(2,128)}, u32[]{:S(2)}) copy-start(s32[48,2]{0,1:T(2,128)} %param.13) | copy-start | bytes 1156
  23.8 4.4 %copy-start.3 = (s32[96,2]{0,1:T(2,128)S(1)}, s32[96,2]{0,1:T(2,128)}, u32[]{:S(2)}) copy-start(s32[96,2]{0,1:T(2,128)} %param.16) | copy-start | bytes 2308
  23.9 4.4 %copy-start.4 = (s32[96]{0:T(128)S(1)}, s32[96]{0:T(128)}, u32[]{:S(2)}) copy-start(s32[96]{0:T(128)} %far_rank.3) | copy-start | bytes 1156
  24.1 27.7 %collective-permute-start.6 = (bf16[4,2,4,64,384]{4,3,2,0,1:T(8,128)(2,1)S(1)}, bf16[4,2,4,64,384]{4,3,2,0,1:T(8,128)(2,1)S(1)}, u32[]{:S(2)}, u32[]{:S(2)}) collective-permute-start(bf16[4,2,4,64,384]{4,3,2,0,1:T(8,128)(2,1)S(1)} %pad_maximum_fusion), channel_id=1, source_target_pairs={{8,0},{33,1},{10,2},{35,3},{12,4},{37,5},{14,6},{39,7},{16,8},{41,... | collective-permute-start | bytes 4718600 | tf_op jit(solution)/shard_map/ppermute | solution.py:201
  25.7 26.1 %collective-permute-start.7 = (bf16[4,2,4,64,384]{4,3,2,0,1:T(8,128)(2,1)S(1)}, bf16[4,2,4,64,384]{4,3,2,0,1:T(8,128)(2,1)S(1)}, u32[]{:S(2)}, u32[]{:S(2)}) collective-permute-start(bf16[4,2,4,64,384]{4,3,2,0,1:T(8,128)(2,1)S(1)} %pad_maximum_fusion), channel_id=1, source_target_pairs={{16,0},{65,1},{18,2},{67,3},{20,4},{69,5},{22,6},{71,7},{24,8},{73... | collective-permute-start | bytes 4718600 | tf_op jit(solution)/shard_map/ppermute | solution.py:201
  27.6 36.1 %collective-permute-start.8 = (bf16[4,2,4,64,384]{4,3,2,0,1:T(8,128)(2,1)S(1)}, bf16[4,2,4,64,384]{4,3,2,0,1:T(8,128)(2,1)S(1)}, u32[]{:S(2)}, u32[]{:S(2)}) collective-permute-start(bf16[4,2,4,64,384]{4,3,2,0,1:T(8,128)(2,1)S(1)} %pad_maximum_fusion), channel_id=1, source_target_pairs={{24,0},{97,1},{26,2},{99,3},{28,4},{101,5},{30,6},{103,7},{0,8},{1... | collective-permute-start | bytes 4718600 | tf_op jit(solution)/shard_map/ppermute | solution.py:201
  47.1 2.9 %collective-permute-start.13 = (bf16[24,64,384]{2,1,0:T(8,128)(2,1)S(1)}, bf16[24,64,384]{2,1,0:T(8,128)(2,1)S(1)}, u32[]{:S(2)}, u32[]{:S(2)}) collective-permute-start(bf16[24,64,384]{2,1,0:T(8,128)(2,1)S(1)} %get-tuple-element.42), channel_id=1, source_target_pairs={{1,0},{0,1},{3,2},{2,3},{5,4},{4,5},{7,6},{6,7},{9,8},{8,9},{11,10... | collective-permute-start | bytes 3538952 | tf_op jit(solution)/shard_map/ppermute | solution.py:179
  47.2 4.5 %collective-permute-start.14 = (bf16[24,64,384]{2,1,0:T(8,128)(2,1)S(1)}, bf16[24,64,384]{2,1,0:T(8,128)(2,1)S(1)}, u32[]{:S(2)}, u32[]{:S(2)}) collective-permute-start(bf16[24,64,384]{2,1,0:T(8,128)(2,1)S(1)} %get-tuple-element.43), channel_id=1, source_target_pairs={{1,0},{0,1},{3,2},{2,3},{5,4},{4,5},{7,6},{6,7},{9,8},{8,9},{11,10... | collective-permute-start | bytes 3538952 | tf_op jit(solution)/shard_map/ppermute | solution.py:179
  50.1 22.8 %collective-permute-start.15 = (bf16[4,4,64,384]{3,2,1,0:T(8,128)(2,1)S(1)}, bf16[4,4,64,384]{3,2,1,0:T(8,128)(2,1)S(1)}, u32[]{:S(2)}, u32[]{:S(2)}) collective-permute-start(bf16[4,4,64,384]{3,2,1,0:T(8,128)(2,1)S(1)} %slice_bitcast_fusion), channel_id=1, source_target_pairs={{1,0},{0,1},{3,2},{2,3},{5,4},{4,5},{7,6},{6,7},{9,8},{8,9},{11,10... | collective-permute-start | bytes 2359304 | tf_op jit(solution)/shard_map/ppermute | solution.py:179
  66.0 38.7 %collective-permute-start.22 = (bf16[2,16,64,384]{3,2,1,0:T(8,128)(2,1)}, bf16[2,16,64,384]{3,2,1,0:T(8,128)(2,1)S(1)}, u32[]{:S(2)}, u32[]{:S(2)}) collective-permute-start(bf16[2,16,64,384]{3,2,1,0:T(8,128)(2,1)} %pad_maximum_fusion.2), channel_id=1, source_target_pairs={{16,0},{65,1},{18,2},{67,3},{20,4},{69,5},{22,6},{71,7},{24,8},{73... | collective-permute-start | bytes 4718600 | tf_op jit(solution)/shard_map/ppermute | solution.py:201
  67.5 7.1 %collective-permute-start.16 = (bf16[4,4,64,384]{3,2,1,0:T(8,128)(2,1)S(1)}, bf16[4,4,64,384]{3,2,1,0:T(8,128)(2,1)S(1)}, u32[]{:S(2)}, u32[]{:S(2)}) collective-permute-start(bf16[4,4,64,384]{3,2,1,0:T(8,128)(2,1)S(1)} %slice_bitcast_fusion.5), channel_id=1, source_target_pairs={{1,0},{0,1},{3,2},{2,3},{5,4},{4,5},{7,6},{6,7},{9,8},{8,9},{11,10... | collective-permute-start | bytes 2359304 | tf_op jit(solution)/shard_map/ppermute | solution.py:179
  69.4 5.2 %collective-permute-start.17 = (bf16[4,4,64,384]{3,2,1,0:T(8,128)(2,1)S(1)}, bf16[4,4,64,384]{3,2,1,0:T(8,128)(2,1)S(1)}, u32[]{:S(2)}, u32[]{:S(2)}) collective-permute-start(bf16[4,4,64,384]{3,2,1,0:T(8,128)(2,1)S(1)} %slice_bitcast_fusion.4), channel_id=1, source_target_pairs={{1,0},{0,1},{3,2},{2,3},{5,4},{4,5},{7,6},{6,7},{9,8},{8,9},{11,10... | collective-permute-start | bytes 2359304 | tf_op jit(solution)/shard_map/ppermute | solution.py:179
  69.4 5.2 %collective-permute-start.18 = (bf16[4,4,64,384]{3,2,1,0:T(8,128)(2,1)S(1)}, bf16[4,4,64,384]{3,2,1,0:T(8,128)(2,1)S(1)}, u32[]{:S(2)}, u32[]{:S(2)}) collective-permute-start(bf16[4,4,64,384]{3,2,1,0:T(8,128)(2,1)S(1)} %slice_bitcast_fusion.3), channel_id=1, source_target_pairs={{1,0},{0,1},{3,2},{2,3},{5,4},{4,5},{7,6},{6,7},{9,8},{8,9},{11,10... | collective-permute-start | bytes 2359304 | tf_op jit(solution)/shard_map/ppermute | solution.py:179
  71.5 3.2 %copy-start.1 = (bf16[96,384,32]{1,2,0:T(8,128)(2,1)S(1)}, bf16[96,384,32]{1,2,0:T(8,128)(2,1)}, u32[]{:S(2)}) copy-start(bf16[96,384,32]{1,2,0:T(8,128)(2,1)} %param.19) | copy-start | bytes 7077892
  72.8 31.9 %collective-permute-start.23 = (bf16[2,16,64,384]{3,2,1,0:T(8,128)(2,1)}, bf16[2,16,64,384]{3,2,1,0:T(8,128)(2,1)S(1)}, u32[]{:S(2)}, u32[]{:S(2)}) collective-permute-start(bf16[2,16,64,384]{3,2,1,0:T(8,128)(2,1)} %pad_maximum_fusion.3), channel_id=1, source_target_pairs={{8,0},{33,1},{10,2},{35,3},{12,4},{37,5},{14,6},{39,7},{16,8},{41,... | collective-permute-start | bytes 4718600 | tf_op jit(solution)/shard_map/ppermute | solution.py:201
  74.6 30.2 %collective-permute-start.21 = (bf16[2,16,64,384]{3,2,1,0:T(8,128)(2,1)}, bf16[2,16,64,384]{3,2,1,0:T(8,128)(2,1)S(1)}, u32[]{:S(2)}, u32[]{:S(2)}) collective-permute-start(bf16[2,16,64,384]{3,2,1,0:T(8,128)(2,1)} %pad_maximum_fusion.1), channel_id=1, source_target_pairs={{24,0},{97,1},{26,2},{99,3},{28,4},{101,5},{30,6},{103,7},{0,8},{1... | collective-permute-start | bytes 4718600 | tf_op jit(solution)/shard_map/ppermute | solution.py:201
  101.1 2.4 %collective-permute-start.20 = (bf16[16,64,384]{2,1,0:T(8,128)(2,1)S(1)}, bf16[16,64,384]{2,1,0:T(8,128)(2,1)S(1)}, u32[]{:S(2)}, u32[]{:S(2)}) collective-permute-start(bf16[16,64,384]{2,1,0:T(8,128)(2,1)S(1)} %get-tuple-element.50), channel_id=1, source_target_pairs={{1,0},{0,1},{3,2},{2,3},{5,4},{4,5},{7,6},{6,7},{9,8},{8,9},{11,10... | collective-permute-start | bytes 2359304 | tf_op jit(solution)/shard_map/ppermute | solution.py:179
  101.2 3.4 %collective-permute-start.19 = (bf16[16,64,384]{2,1,0:T(8,128)(2,1)S(1)}, bf16[16,64,384]{2,1,0:T(8,128)(2,1)S(1)}, u32[]{:S(2)}, u32[]{:S(2)}) collective-permute-start(bf16[16,64,384]{2,1,0:T(8,128)(2,1)S(1)} %get-tuple-element.48), channel_id=1, source_target_pairs={{1,0},{0,1},{3,2},{2,3},{5,4},{4,5},{7,6},{6,7},{9,8},{8,9},{11,10... | collective-permute-start | bytes 2359304 | tf_op jit(solution)/shard_map/ppermute | solution.py:179
  103.5 3.0 %collective-permute-start.28 = (bf16[16,64,384]{2,1,0:T(8,128)(2,1)S(1)}, bf16[16,64,384]{2,1,0:T(8,128)(2,1)S(1)}, u32[]{:S(2)}, u32[]{:S(2)}) collective-permute-start(bf16[16,64,384]{2,1,0:T(8,128)(2,1)S(1)} %get-tuple-element.59), channel_id=1, source_target_pairs={{1,0},{0,1},{3,2},{2,3},{5,4},{4,5},{7,6},{6,7},{9,8},{8,9},{11,10... | collective-permute-start | bytes 2359304 | tf_op jit(solution)/shard_map/ppermute | solution.py:179
  103.8 1.2 copy-start.5
  105.0 9.1 %collective-permute-start.26 = (bf16[8,64,384]{2,1,0:T(8,128)(2,1)S(1)}, bf16[8,64,384]{2,1,0:T(8,128)(2,1)S(1)}, u32[]{:S(2)}, u32[]{:S(2)}) collective-permute-start(bf16[8,64,384]{2,1,0:T(8,128)(2,1)S(1)} %slice.249), channel_id=1, source_target_pairs={{6,0},{3,1},{0,2},{5,3},{2,4},{7,5},{4,6},{1,7},{14,8},{11,9},{8,1... | collective-permute-start | bytes 1179656 | tf_op jit(solution)/shard_map/ppermute | solution.py:226
  106.4 9.9 %collective-permute-start.24 = (bf16[8,64,384]{2,1,0:T(8,128)(2,1)S(1)}, bf16[8,64,384]{2,1,0:T(8,128)(2,1)}, u32[]{:S(2)}, u32[]{:S(2)}) collective-permute-start(bf16[8,64,384]{2,1,0:T(8,128)(2,1)S(1)} %slice.250), channel_id=1, source_target_pairs={{6,0},{3,1},{0,2},{5,3},{2,4},{7,5},{4,6},{1,7},{14,8},{11,9},{8,1... | collective-permute-start | bytes 1179656 | tf_op jit(solution)/shard_map/ppermute | solution.py:227
  109.1 14.3 %collective-permute-start.30 = (bf16[2,4,64,384]{3,2,1,0:T(8,128)(2,1)}, bf16[2,4,64,384]{3,2,1,0:T(8,128)(2,1)}, u32[]{:S(2)}, u32[]{:S(2)}) collective-permute-start(bf16[2,4,64,384]{3,2,1,0:T(8,128)(2,1)} %get-tuple-element.71), channel_id=1, source_target_pairs={{64,0},{17,1},{66,2},{19,3},{68,4},{21,5},{70,6},{23,7},{72,8},{25... | collective-permute-start | bytes 1179656 | tf_op jit(solution)/shard_map/ppermute | solution.py:201
  111.1 13.0 %collective-permute-start.31 = (bf16[2,4,64,384]{3,2,1,0:T(8,128)(2,1)}, bf16[2,4,64,384]{3,2,1,0:T(8,128)(2,1)}, u32[]{:S(2)}, u32[]{:S(2)}) collective-permute-start(bf16[2,4,64,384]{3,2,1,0:T(8,128)(2,1)} %get-tuple-element.70), channel_id=1, source_target_pairs={{32,0},{9,1},{34,2},{11,3},{36,4},{13,5},{38,6},{15,7},{40,8},{17,... | collective-permute-start | bytes 1179656 | tf_op jit(solution)/shard_map/ppermute | solution.py:201
  113.5 10.6 %collective-permute-start.29 = (bf16[2,4,64,384]{3,2,1,0:T(8,128)(2,1)}, bf16[2,4,64,384]{3,2,1,0:T(8,128)(2,1)}, u32[]{:S(2)}, u32[]{:S(2)}) collective-permute-start(bf16[2,4,64,384]{3,2,1,0:T(8,128)(2,1)} %fusion.2), channel_id=1, source_target_pairs={{96,0},{25,1},{98,2},{27,3},{100,4},{29,5},{102,6},{31,7},{104,8},... | collective-permute-start | bytes 1179656 | tf_op jit(solution)/shard_map/ppermute | solution.py:201
  115.0 9.2 %collective-permute-start.27 = (bf16[8,64,384]{2,1,0:T(8,128)(2,1)}, bf16[8,64,384]{2,1,0:T(8,128)(2,1)}, u32[]{:S(2)}, u32[]{:S(2)}) collective-permute-start(bf16[8,64,384]{2,1,0:T(8,128)(2,1)} %add_convert_fusion.3), channel_id=1, source_target_pairs={{6,0},{3,1},{0,2},{5,3},{2,4},{7,5},{4,6},{1,7},{14,8},{11,9},{8,1... | collective-permute-start | bytes 1179656 | tf_op jit(solution)/shard_map/ppermute | solution.py:232
  116.2 12.8 %collective-permute-start.25 = (bf16[8,64,384]{2,1,0:T(8,128)(2,1)}, bf16[8,64,384]{2,1,0:T(8,128)(2,1)}, u32[]{:S(2)}, u32[]{:S(2)}) collective-permute-start(bf16[8,64,384]{2,1,0:T(8,128)(2,1)} %collective-permute-done.24), channel_id=1, source_target_pairs={{1,0},{0,1},{3,2},{2,3},{5,4},{4,5},{7,6},{6,7},{9,8},{8,9},{11,10... | collective-permute-start | bytes 1179656 | tf_op jit(solution)/shard_map/ppermute | solution.py:179
  123.4 5.7 %copy-start.6 = (f32[16,64,384]{2,1,0:T(8,128)S(1)}, f32[16,64,384]{2,1,0:T(8,128)}, u32[]{:S(2)}) copy-start(f32[16,64,384]{2,1,0:T(8,128)} %copy-done.5) | copy-start | bytes 4718596
  123.4 5.7 %copy-start.7 = (f32[8,64,384]{2,1,0:T(8,128)S(1)}, f32[8,64,384]{2,1,0:T(8,128)}, u32[]{:S(2)}) copy-start(f32[8,64,384]{2,1,0:T(8,128)} %fusion.18) | copy-start | bytes 2359300
  125.7 4.7 %collective-permute-start.32 = (bf16[4,64,384]{2,1,0:T(8,128)(2,1)S(1)}, bf16[4,64,384]{2,1,0:T(8,128)(2,1)S(1)}, u32[]{:S(2)}, u32[]{:S(2)}) collective-permute-start(bf16[4,64,384]{2,1,0:T(8,128)(2,1)S(1)} %get-tuple-element.73), channel_id=1, source_target_pairs={{1,0},{0,1},{3,2},{2,3},{5,4},{4,5},{7,6},{6,7},{9,8},{8,9},{11,10... | collective-permute-start | bytes 589832 | tf_op jit(solution)/shard_map/ppermute | solution.py:179

commit v3 on v2

--- a/solution.py
+++ b/solution.py
@@ -211,20 +211,19 @@
     left = jnp.swapaxes(far_left, 1, 2).reshape(-1, dof)
     right = jnp.swapaxes(far_right, 1, 2).reshape(-1, dof)
     lists = (near_pairs.T, near_count, far_pairs.T, far_rank, near_blocks)
-    to_cols = pair_product(False, 44, src_rows, dst_cols, [(k, None, n) for k, n in enumerate((8,) * 8)], (16, 16, 16, 16, 24, 24, 16), *lists, left, right, rows)
-    theirs = [swap(to_cols[4]), swap(to_cols[5])]
-    cols[1:], theirs = lax.optimization_barrier((cols[1:], theirs))
-    theirs = [theirs[0][:16], jnp.concatenate([theirs[0][16:], theirs[1][:8]]), theirs[1][8:], swap(to_cols[6])]
-    sums = [jnp.stack([to_cols[k], theirs[k]]) for k in range(SIDE)]
+    to_cols = pair_product(False, 44, src_rows, dst_cols, [(k, None, n) for k, n in enumerate((8,) * 8)], (16,) * 8, *lists, left, right, rows)
+    sums = [jnp.stack([to_cols[k], swap(to_cols[k + SIDE])]) for k in (0, 2)]
+    cols[1:], sums = lax.optimization_barrier((cols[1:], sums))
+    sums = [sums[0], jnp.stack([to_cols[1], swap(to_cols[5])]), sums[1], jnp.stack([to_cols[3], swap(to_cols[7])])]
     cols += [swap(v[:, 1]) for v in cols]
     sums_in = [plane(sums[step - 1], 0, -step) for step in (1, 2, 3)]
     pieces = [(k, (at, 0) if k < 4 else at, 4) for k in range(8) for at in range(SIDE)]
     to_rows = pair_product(True, 38, src_cols, dst_rows, pieces, (16,) * 4, *lists, right, left, cols)
     row_near = wide(to_rows[2]) + wide(swap(to_rows[0]))
     row_far = wide(to_rows[3]) + wide(swap(to_rows[1]))
-    row_near, row_far, sums_in = lax.optimization_barrier((row_near, row_far, sums_in))
     forth = lax.ppermute(narrow(row_far[:PER]), "col", chip)
     cross = lax.ppermute(narrow(row_near[PER:]), "col", chip)
+    sums_in = lax.optimization_barrier((row_near, row_far, sums_in))[2]
     split = lambda v: v.reshape((2, SIDE, PER // 2) + masked.shape[1:])
     line_in = [split(v) for v in [sums[3], *sums_in]]
     block = lambda step: sum(wide(v[:, step]) for v in line_in)

time: 132 us -> 130 us (0.985)
  Pallas kernels: 45.3 us -> 37 us
  waiting for transfers between devices: 28.5 us -> 35.3 us
    ppermute x12, waiting for transfers between devices: 21.1 us -> 29.7 us  [local(): lax.ppermute(v, ('row', 'col'), plane_shift(first, step))]
    pallas_call x2, Pallas kernels: 45.3 us -> 37 us  [pair_product(): pl.pallas_call(functools.partial(pair_kernel, flip, src_of, dst_of, (in_s...]
    ppermute x12, starting transfers between devices: 16.9 us -> 13.6 us  [local(): lax.ppermute(v, ('row', 'col'), plane_shift(first, step))]
    ppermute x1, starting transfers between devices: 0.04 us -> 3.12 us  [local(): forth_two = lax.ppermute(narrow(row_near[:PER] + wide(forth)), 'col', chip)]
    ppermute x15 -> x16, starting transfers between devices: 15.6 us -> 13.9 us  [swap(): return lax.ppermute(v, 'col', col_shift(0, 1))]
    ppermute x15 -> x16, waiting for transfers between devices: 6.19 us -> 5.23 us  [swap(): return lax.ppermute(v, 'col', col_shift(0, 1))]
    another operation x4 -> x3, other arithmetic: 4.15 us -> 4.03 us  [the longest x2 2.67 us: local(): sums = [jnp.stack([to_cols[k], swap(to_cols[k + SIDE])]) for k in (0, 2)]]
  transfers between devices with their start and end apart: 33 -> 34, of which waited for: 9 -> 14; matrix products, arithmetic and copies ran while one was open for 11% -> 11% of each run, Pallas kernels for 34% -> 29%
where the time goes in v3:
time: 130 us; the launch traced here: 129 us
  starting transfers between devices  38.7 us (30%)
  Pallas kernels  37 us (28%)
  waiting for transfers between devices  35.3 us (27%)
  other arithmetic  13.9 us (11%)
  matrix products  1.83 us (1%)
  local copies, waits for them, and re-layouts  1.71 us (1%)
    pallas_call x2, Pallas kernels, pair_product(): pl.pallas_call(functools.partial(pair_kernel, flip, src_of, dst_of, (in_s...  37 us
    ppermute x12, waiting for transfers between devices, local(): lax.ppermute(v, ('row', 'col'), plane_shift(first, step))  29.7 us
    ppermute x16, starting transfers between devices, swap(): return lax.ppermute(v, 'col', col_shift(0, 1))  13.9 us
    ppermute x12, starting transfers between devices, local(): lax.ppermute(v, ('row', 'col'), plane_shift(first, step))  13.6 us
    ppermute x16, waiting for transfers between devices, swap(): return lax.ppermute(v, 'col', col_shift(0, 1))  5.23 us
    ppermute x1, starting transfers between devices, local(): forth_two = lax.ppermute(narrow(row_near[:PER] + wide(forth)), 'col', chip)  3.12 us
    another operation x2, other arithmetic, local(): sums = [jnp.stack([to_cols[k], swap(to_cols[k + SIDE])]) for k in (0, 2)]  2.67 us
    add x2, other arithmetic, local(): block = lambda step: sum((wide(v[:, step]) for v in line_in))  2.63 us
  transfers between devices with their start and end apart: 34, of which 14 were waited for; matrix products, arithmetic and copies ran while one was open for 11% of the time, Pallas kernels for 29%

profile of v3, /device:TPU:1, one launch (start us, length us, event | category | flops | bytes accessed | tf_op | source)
XLA Modules:
  0.0 129.4 jit_solution(17627855348279707686)
XLA Ops:
  0.0 0.9 compare_convert_fusion
  0.9 1.0 broadcast_multiply_fusion.refs_0_
  1.9 1.5 %collective-permute-start = (bf16[8,64,384]{2,1,0:T(8,128)(2,1)S(1)}, bf16[8,64,384]{2,1,0:T(8,128)(2,1)S(1)}, u32[]{:S(2)}, u32[]{:S(2)}) collective-permute-start(bf16[8,64,384]{2,1,0:T(8,128)(2,1)S(1)} %broadcast_multiply_fusion.refs_0_), channel_id=1, source_target_pairs={{1,0},{0,1},{3,2},{2,3},{5,4},{4,5},{7,6},{6,7},{9,8},{8,9},{11,10... | collective-permute-start | bytes 1179656 | tf_op jit(solution)/shard_map/ppermute | solution.py:179
  3.4 2.6 %collective-permute-start.1 = (bf16[8,64,384]{2,1,0:T(8,128)(2,1)S(1)}, bf16[8,64,384]{2,1,0:T(8,128)(2,1)S(1)}, u32[]{:S(2)}, u32[]{:S(2)}) collective-permute-start(bf16[8,64,384]{2,1,0:T(8,128)(2,1)S(1)} %broadcast_multiply_fusion.refs_0_), channel_id=1, source_target_pairs={{6,0},{3,1},{0,2},{5,3},{2,4},{7,5},{4,6},{1,7},{14,8},{11,9},{8,1... | collective-permute-start | bytes 1179656 | tf_op jit(solution)/shard_map/ppermute | solution.py:203
  6.2 3.8 %collective-permute-start.3 = (bf16[2,4,64,384]{3,2,1,0:T(8,128)(2,1)S(1)}, bf16[2,4,64,384]{3,2,1,0:T(8,128)(2,1)S(1)}, u32[]{:S(2)}, u32[]{:S(2)}) collective-permute-start(bf16[2,4,64,384]{3,2,1,0:T(8,128)(2,1)S(1)} %get-tuple-element.73), channel_id=1, source_target_pairs={{32,0},{9,1},{34,2},{11,3},{36,4},{13,5},{38,6},{15,7},{40,8},{17,... | collective-permute-start | bytes 1179656 | tf_op jit(solution)/shard_map/ppermute | solution.py:201
  10.0 1.3 %collective-permute-start.5 = (bf16[2,4,64,384]{3,2,1,0:T(8,128)(2,1)S(1)}, bf16[2,4,64,384]{3,2,1,0:T(8,128)(2,1)S(1)}, u32[]{:S(2)}, u32[]{:S(2)}) collective-permute-start(bf16[2,4,64,384]{3,2,1,0:T(8,128)(2,1)S(1)} %get-tuple-element.73), channel_id=1, source_target_pairs={{64,0},{17,1},{66,2},{19,3},{68,4},{21,5},{70,6},{23,7},{72,8},{25... | collective-permute-start | bytes 1179656 | tf_op jit(solution)/shard_map/ppermute | solution.py:201
  11.3 1.3 %collective-permute-start.2 = (bf16[8,64,384]{2,1,0:T(8,128)(2,1)S(1)}, bf16[8,64,384]{2,1,0:T(8,128)(2,1)S(1)}, u32[]{:S(2)}, u32[]{:S(2)}) collective-permute-start(bf16[8,64,384]{2,1,0:T(8,128)(2,1)S(1)} %collective-permute-done.refs_1_), channel_id=1, source_target_pairs={{6,0},{3,1},{0,2},{5,3},{2,4},{7,5},{4,6},{1,7},{14,8},{11,9},{8,1... | collective-permute-start | bytes 1179656 | tf_op jit(solution)/shard_map/ppermute | solution.py:204
  12.6 1.2 collective-permute-start.11
  13.8 5.1 %collective-permute-done.3 = bf16[2,4,64,384]{3,2,1,0:T(8,128)(2,1)S(1)} collective-permute-done((bf16[2,4,64,384]{3,2,1,0:T(8,128)(2,1)S(1)}, bf16[2,4,64,384]{3,2,1,0:T(8,128)(2,1)S(1)}, u32[]{:S(2)}, u32[]{:S(2)}) %collective-permute-start.3) | collective-permute-done | bytes 393248 | tf_op jit(solution)/shard_map/ppermute | solution.py:201
  18.9 3.4 %collective-permute-done.4 = bf16[2,4,64,384]{3,2,1,0:T(8,128)(2,1)S(1)} collective-permute-done((bf16[2,4,64,384]{3,2,1,0:T(8,128)(2,1)S(1)}, bf16[2,4,64,384]{3,2,1,0:T(8,128)(2,1)S(1)}, u32[]{:S(2)}, u32[]{:S(2)}) %collective-permute-start.4) | collective-permute-done | bytes 393248 | tf_op jit(solution)/shard_map/ppermute | solution.py:201
  22.4 0.2 pad_maximum_fusion
  22.6 2.5 %collective-permute-start.6 = (bf16[4,2,4,64,384]{4,3,2,0,1:T(8,128)(2,1)S(1)}, bf16[4,2,4,64,384]{4,3,2,0,1:T(8,128)(2,1)S(1)}, u32[]{:S(2)}, u32[]{:S(2)}) collective-permute-start(bf16[4,2,4,64,384]{4,3,2,0,1:T(8,128)(2,1)S(1)} %pad_maximum_fusion), channel_id=1, source_target_pairs={{8,0},{33,1},{10,2},{35,3},{12,4},{37,5},{14,6},{39,7},{16,8},{41,... | collective-permute-start | bytes 4718600 | tf_op jit(solution)/shard_map/ppermute | solution.py:201
  25.1 0.6 collective-permute-start.7
  25.8 0.4 collective-permute-start.8
  26.2 1.1 collective-permute-start.9
  28.1 0.6 collective-permute-done.9.refs_4_
  28.7 0.6 collective-permute-done.12.refs_7_
  29.2 15.5 %shard_map.100 = (bf16[16,64,384]{2,1,0:T(8,128)(2,1)S(1)}, bf16[16,64,384]{2,1,0:T(8,128)(2,1)S(1)}, bf16[16,64,384]{2,1,0:T(8,128)(2,1)S(1)}, bf16[16,64,384]{...) custom-call(s32[2,48]{1,0:T(2,128)S(1)} %bitcast.91, ...), custom_call_target="tpu_custom_call" | custom-call | flops 905969664 | bytes 18874368 | tf_op jit(solution)/shard_map/pallas_call | solution.py:90
  44.7 1.5 %collective-permute-start.14 = (bf16[16,64,384]{2,1,0:T(8,128)(2,1)S(1)}, bf16[16,64,384]{2,1,0:T(8,128)(2,1)S(1)}, u32[]{:S(2)}, u32[]{:S(2)}) collective-permute-start(bf16[16,64,384]{2,1,0:T(8,128)(2,1)S(1)} %get-tuple-element.44), channel_id=1, source_target_pairs={{1,0},{0,1},{3,2},{2,3},{5,4},{4,5},{7,6},{6,7},{9,8},{8,9},{11,10... | collective-permute-start | bytes 2359304 | tf_op jit(solution)/shard_map/ppermute | solution.py:179
  46.2 0.1 collective-permute-start.13
  46.4 1.7 %collective-permute-done.14 = bf16[16,64,384]{2,1,0:T(8,128)(2,1)S(1)} collective-permute-done((bf16[16,64,384]{2,1,0:T(8,128)(2,1)S(1)}, bf16[16,64,384]{2,1,0:T(8,128)(2,1)S(1)}, u32[]{:S(2)}, u32[]{:S(2)}) %collective-permute-start.14) | collective-permute-done | bytes 786464 | tf_op jit(solution)/shard_map/ppermute | solution.py:179
  48.1 0.4 collective-permute-start.15
  48.5 1.3 %pad_maximum_fusion.2 = bf16[2,16,64,384]{3,2,1,0:T(8,128)(2,1)} fusion(bf16[1,16,64,384]{3,2,1,0:T(8,128)(2,1)S(1)} %bitcast.107, bf16[1,16,64,384]{3,2,1,0:T(8,128)(2,1)S(1)} %bitcast.90), kind=kLoop, calls=%fused_computation.8 | loop fusion | flops 786432 | bytes 3145728 | tf_op jit(solution)/shard_map/stack | solution.py:215
  49.8 0.1 collective-permute-start.27
  49.9 1.3 %pad_maximum_fusion.1 = bf16[2,16,64,384]{3,2,1,0:T(8,128)(2,1)} fusion(bf16[1,16,64,384]{3,2,1,0:T(8,128)(2,1)S(1)} %bitcast.106, bf16[1,16,64,384]{3,2,1,0:T(8,128)(2,1)S(1)} %bitcast.89), kind=kLoop, calls=%fused_computation.7 | loop fusion | flops 786432 | bytes 3145728 | tf_op jit(solution)/shard_map/stack | solution.py:215
  51.3 8.1 %collective-permute-done.6 = bf16[4,2,4,64,384]{4,3,2,0,1:T(8,128)(2,1)S(1)} collective-permute-done((bf16[4,2,4,64,384]{4,3,2,0,1:T(8,128)(2,1)S(1)}, bf16[4,2,4,64,384]{4,3,2,0,1:T(8,128)(2,1)S(1)}, u32[]{:S(2)}, u32[]{:S(2)}) %collective-permute-start.6) | collective-permute-done | bytes 1572896 | tf_op jit(solution)/shard_map/ppermute | solution.py:201
  59.4 3.7 %collective-permute-done.8 = bf16[4,2,4,64,384]{4,3,2,0,1:T(8,128)(2,1)S(1)} collective-permute-done((bf16[4,2,4,64,384]{4,3,2,0,1:T(8,128)(2,1)S(1)}, bf16[4,2,4,64,384]{4,3,2,0,1:T(8,128)(2,1)S(1)}, u32[]{:S(2)}, u32[]{:S(2)}) %collective-permute-start.8) | collective-permute-done | bytes 1572896 | tf_op jit(solution)/shard_map/ppermute | solution.py:201
  63.1 1.5 %collective-permute-start.16 = (bf16[4,4,64,384]{3,2,1,0:T(8,128)(2,1)S(1)}, bf16[4,4,64,384]{3,2,1,0:T(8,128)(2,1)S(1)}, u32[]{:S(2)}, u32[]{:S(2)}) collective-permute-start(bf16[4,4,64,384]{3,2,1,0:T(8,128)(2,1)S(1)} %slice_bitcast_fusion.3), channel_id=1, source_target_pairs={{1,0},{0,1},{3,2},{2,3},{5,4},{4,5},{7,6},{6,7},{9,8},{8,9},{11,10... | collective-permute-start | bytes 2359304 | tf_op jit(solution)/shard_map/ppermute | solution.py:179
  64.8 0.1 collective-permute-start.17
  65.0 0.6 collective-permute-start.18
  65.5 0.2 copy.14.refs_0_
  65.7 1.4 %pad_maximum_fusion.3 = bf16[2,16,64,384]{3,2,1,0:T(8,128)(2,1)} fusion(bf16[1,16,64,384]{3,2,1,0:T(8,128)(2,1)S(1)} %bitcast.105, bf16[1,16,64,384]{3,2,1,0:T(8,128)(2,1)S(1)} %bitcast.88), kind=kLoop, calls=%fused_computation.9 | loop fusion | flops 786432 | bytes 3145728 | tf_op jit(solution)/shard_map/stack | solution.py:217
  67.1 0.7 collective-permute-start.28
  67.8 0.2 copy.15.refs_1_
  68.0 0.2 copy.16.refs_2_
  68.2 0.2 copy.17.refs_3_
  68.4 0.5 collective-permute-start.26
  68.9 2.3 %collective-permute-start.29 = (bf16[2,16,64,384]{3,2,1,0:T(8,128)(2,1)}, bf16[2,16,64,384]{3,2,1,0:T(8,128)(2,1)S(1)}, u32[]{:S(2)}, u32[]{:S(2)}) collective-permute-start(bf16[2,16,64,384]{3,2,1,0:T(8,128)(2,1)} %pad_maximum_fusion.2), channel_id=1, source_target_pairs={{8,0},{33,1},{10,2},{35,3},{12,4},{37,5},{14,6},{39,7},{16,8},{41,... | collective-permute-start | bytes 4718600 | tf_op jit(solution)/shard_map/ppermute | solution.py:201
  71.2 21.6 %shard_map.101 = (bf16[16,64,384]{2,1,0:T(8,128)(2,1)S(1)}, bf16[16,64,384]{2,1,0:T(8,128)(2,1)S(1)}, bf16[16,64,384]{2,1,0:T(8,128)(2,1)S(1)}, bf16[16,64,384]{2,1,0:T(8,128)(2,1)S(1)}) custom-call(s32[2,48]{1,0:T(2,128)S(1)} %bitcast.92, s32[1]{0:T(128)S(6)} %copy.26.near_count, s32[2,96]{1,0:T(2,128)S(1)} %bitcast.94, s32[96]{0:T(128)S(1)} %copy-done.4, ...), custom_call_target="tpu_custom_call" | custom-call | flops 905969664 | bytes 18874368 | tf_op jit(solution)/shard_map/pallas_call | solution.py:90
  92.8 1.9 %collective-permute-start.19 = (bf16[16,64,384]{2,1,0:T(8,128)(2,1)S(1)}, bf16[16,64,384]{2,1,0:T(8,128)(2,1)S(1)}, u32[]{:S(2)}, u32[]{:S(2)}) collective-permute-start(bf16[16,64,384]{2,1,0:T(8,128)(2,1)S(1)} %get-tuple-element.49), channel_id=1, source_target_pairs={{1,0},{0,1},{3,2},{2,3},{5,4},{4,5},{7,6},{6,7},{9,8},{8,9},{11,10... | collective-permute-start | bytes 2359304 | tf_op jit(solution)/shard_map/ppermute | solution.py:179
  94.7 1.8 %collective-permute-done.19 = bf16[16,64,384]{2,1,0:T(8,128)(2,1)S(1)} collective-permute-done((bf16[16,64,384]{2,1,0:T(8,128)(2,1)S(1)}, bf16[16,64,384]{2,1,0:T(8,128)(2,1)S(1)}, u32[]{:S(2)}, u32[]{:S(2)}) %collective-permute-start.19) | collective-permute-done | bytes 786464 | tf_op jit(solution)/shard_map/ppermute | solution.py:179
  96.6 0.4 collective-permute-start.25
  96.9 0.2 convert_add_fusion.1
  97.2 0.5 collective-permute-done.20
  97.7 0.2 convert_add_fusion
  97.9 0.4 copy-done.5
  98.4 6.9 %collective-permute-done.26 = bf16[2,16,64,384]{3,2,1,0:T(8,128)(2,1)S(1)} collective-permute-done((bf16[2,16,64,384]{3,2,1,0:T(8,128)(2,1)}, bf16[2,16,64,384]{3,2,1,0:T(8,128)(2,1)S(1)}, u32[]{:S(2)}, u32[]{:S(2)}) %collective-permute-start.26) | collective-permute-done | bytes 1572896 | tf_op jit(solution)/shard_map/ppermute | solution.py:201
  105.2 2.5 %collective-permute-start.23 = (bf16[8,64,384]{2,1,0:T(8,128)(2,1)S(1)}, bf16[8,64,384]{2,1,0:T(8,128)(2,1)S(1)}, u32[]{:S(2)}, u32[]{:S(2)}) collective-permute-start(bf16[8,64,384]{2,1,0:T(8,128)(2,1)S(1)} %slice.239), channel_id=1, source_target_pairs={{6,0},{3,1},{0,2},{5,3},{2,4},{7,5},{4,6},{1,7},{14,8},{11,9},{8,1... | collective-permute-start | bytes 1179656 | tf_op jit(solution)/shard_map/ppermute | solution.py:224
  107.7 0.5 collective-permute-start.21
  108.3 1.6 %convert_add_fusion.2 = (f32[2,1,4,64,384]{4,3,2,1,0:T(8,128)S(1)}, bf16[2,4,64,384]{3,2,1,0:T(8,128)(2,1)}, bf16[2,4,64,384]{3,2,1,0:T(8,128)(2,1)}) fusion(bf16[2,4,4,64,384]{4,3,2,1,0:T(8,128)(2,1)S(1)} %bitcast.103, bf16[2,4,4,64,384]{4,3,2,1,0:T(8,128)(2,1)S(1)} %bitcast.99, bf16[2,4,4,64,384]{4,3,2,1,0:T(8,128)(2,1)S(1)} %bitcast.101, ...), kind=kLoop, calls=%fused_computation.23 | loop fusion | flops 5111808 | bytes 6684672 | tf_op jit(solution)/shard_map/add | solution.py:229
  109.9 1.0 fusion.5
  110.9 0.6 collective-permute-start.32
  111.5 0.8 collective-permute-start.30
  112.4 0.9 fusion
  113.3 3.1 %collective-permute-start.24 = (bf16[8,64,384]{2,1,0:T(8,128)(2,1)}, bf16[8,64,384]{2,1,0:T(8,128)(2,1)}, u32[]{:S(2)}, u32[]{:S(2)}) collective-permute-start(bf16[8,64,384]{2,1,0:T(8,128)(2,1)} %fusion), channel_id=1, source_target_pairs={{6,0},{3,1},{0,2},{5,3},{2,4},{7,5},{4,6},{1,7},{14,8},{11,9},{8,1... | collective-permute-start | bytes 1179656 | tf_op jit(solution)/shard_map/ppermute | solution.py:231
  116.4 0.2 collective-permute-done.21
  116.6 2.8 %collective-permute-start.22 = (bf16[8,64,384]{2,1,0:T(8,128)(2,1)}, bf16[8,64,384]{2,1,0:T(8,128)(2,1)}, u32[]{:S(2)}, u32[]{:S(2)}) collective-permute-start(bf16[8,64,384]{2,1,0:T(8,128)(2,1)} %collective-permute-done.21), channel_id=1, source_target_pairs={{1,0},{0,1},{3,2},{2,3},{5,4},{4,5},{7,6},{6,7},{9,8},{8,9},{11,10... | collective-permute-start | bytes 1179656 | tf_op jit(solution)/shard_map/ppermute | solution.py:179
  119.4 1.8 %fusion.21 = f32[8,64,384]{2,1,0:T(8,128)} fusion(bf16[8,64,384]{2,1,0:T(8,128)(2,1)S(1)} %broadcast_multiply_fusion.refs_0_, bf16[8,384,384]{2,1,0:T(8,128)(2,1)S(1)} %copy-done), kind=kOutput, calls=%fused_computation.60 | convolution fusion | flops 150994944 | bytes 3538944 | tf_op jit(solution)/shard_map/cld,ced->cle/dot_general | solution.py:236
  121.2 0.9 collective-permute-done.32
  122.1 1.7 %collective-permute-done.30 = bf16[2,4,64,384]{3,2,1,0:T(8,128)(2,1)} collective-permute-done((bf16[2,4,64,384]{3,2,1,0:T(8,128)(2,1)}, bf16[2,4,64,384]{3,2,1,0:T(8,128)(2,1)}, u32[]{:S(2)}, u32[]{:S(2)}) %collective-permute-start.30) | collective-permute-done | bytes 393248 | tf_op jit(solution)/shard_map/ppermute | solution.py:201
  123.8 1.5 %fusion.13 = (f32[4,64,384]{2,1,0:T(8,128)S(1)}, bf16[4,64,384]{2,1,0:T(8,128)(2,1)S(1)}) fusion(f32[2,1,4,64,384]{4,3,2,1,0:T(8,128)S(1)} %get-tuple-element.67, bf16[2,4,64,384]{3,2,1,0:T(8,128)(2,1)} %collective-permute-done.32, bf16[2,4,64,384]{3,2,1,0:T(8,128)(2,1)} %collective-permute-done.31, bf16[2,4,64,384]{3,2,1,0:T(8,128)(2,1)} %collective-permute-done.30), kind=kLoop, calls=%fused_computation.39 | loop fusion | flops 1277952 | bytes 2555904 | tf_op jit(solution)/shard_map/add | solution.py:235
  125.4 1.8 %collective-permute-start.33 = (bf16[4,64,384]{2,1,0:T(8,128)(2,1)S(1)}, bf16[4,64,384]{2,1,0:T(8,128)(2,1)S(1)}, u32[]{:S(2)}, u32[]{:S(2)}) collective-permute-start(bf16[4,64,384]{2,1,0:T(8,128)(2,1)S(1)} %get-tuple-element.71), channel_id=1, source_target_pairs={{1,0},{0,1},{3,2},{2,3},{5,4},{4,5},{7,6},{6,7},{9,8},{8,9},{11,10... | collective-permute-start | bytes 589832 | tf_op jit(solution)/shard_map/ppermute | solution.py:179
  127.1 1.3 fusion.2
  128.4 1.0 fusion.4
  (52 shorter events, 0.9 us)
Async XLA Ops:
  0.0 119.4 %copy-start = (bf16[8,384,384]{2,1,0:T(8,128)(2,1)S(1)}, bf16[8,384,384]{2,1,0:T(8,128)(2,1)}, u32[]{:S(2)}) copy-start(bf16[8,384,384]{2,1,0:T(8,128)(2,1)} %param.12) | copy-start | bytes 7077892
  1.9 4.1 %collective-permute-start = (bf16[8,64,384]{2,1,0:T(8,128)(2,1)S(1)}, bf16[8,64,384]{2,1,0:T(8,128)(2,1)S(1)}, u32[]{:S(2)}, u32[]{:S(2)}) collective-permute-start(bf16[8,64,384]{2,1,0:T(8,128)(2,1)S(1)} %broadcast_multiply_fusion.refs_0_), channel_id=1, source_target_pairs={{1,0},{0,1},{3,2},{2,3},{5,4},{4,5},{7,6},{6,7},{9,8},{8,9},{11,10... | collective-permute-start | bytes 1179656 | tf_op jit(solution)/shard_map/ppermute | solution.py:179
  3.4 9.2 %collective-permute-start.1 = (bf16[8,64,384]{2,1,0:T(8,128)(2,1)S(1)}, bf16[8,64,384]{2,1,0:T(8,128)(2,1)S(1)}, u32[]{:S(2)}, u32[]{:S(2)}) collective-permute-start(bf16[8,64,384]{2,1,0:T(8,128)(2,1)S(1)} %broadcast_multiply_fusion.refs_0_), channel_id=1, source_target_pairs={{6,0},{3,1},{0,2},{5,3},{2,4},{7,5},{4,6},{1,7},{14,8},{11,9},{8,1... | collective-permute-start | bytes 1179656 | tf_op jit(solution)/shard_map/ppermute | solution.py:203
  6.2 12.8 %collective-permute-start.3 = (bf16[2,4,64,384]{3,2,1,0:T(8,128)(2,1)S(1)}, bf16[2,4,64,384]{3,2,1,0:T(8,128)(2,1)S(1)}, u32[]{:S(2)}, u32[]{:S(2)}) collective-permute-start(bf16[2,4,64,384]{3,2,1,0:T(8,128)(2,1)S(1)} %get-tuple-element.73), channel_id=1, source_target_pairs={{32,0},{9,1},{34,2},{11,3},{36,4},{13,5},{38,6},{15,7},{40,8},{17,... | collective-permute-start | bytes 1179656 | tf_op jit(solution)/shard_map/ppermute | solution.py:201
  10.0 12.3 %collective-permute-start.4 = (bf16[2,4,64,384]{3,2,1,0:T(8,128)(2,1)S(1)}, bf16[2,4,64,384]{3,2,1,0:T(8,128)(2,1)S(1)}, u32[]{:S(2)}, u32[]{:S(2)}) collective-permute-start(bf16[2,4,64,384]{3,2,1,0:T(8,128)(2,1)S(1)} %get-tuple-element.73), channel_id=1, source_target_pairs={{96,0},{25,1},{98,2},{27,3},{100,4},{29,5},{102,6},{31,7},{104,8},... | collective-permute-start | bytes 1179656 | tf_op jit(solution)/shard_map/ppermute | solution.py:201
  10.0 12.3 %collective-permute-start.5 = (bf16[2,4,64,384]{3,2,1,0:T(8,128)(2,1)S(1)}, bf16[2,4,64,384]{3,2,1,0:T(8,128)(2,1)S(1)}, u32[]{:S(2)}, u32[]{:S(2)}) collective-permute-start(bf16[2,4,64,384]{3,2,1,0:T(8,128)(2,1)S(1)} %get-tuple-element.73), channel_id=1, source_target_pairs={{64,0},{17,1},{66,2},{19,3},{68,4},{21,5},{70,6},{23,7},{72,8},{25... | collective-permute-start | bytes 1179656 | tf_op jit(solution)/shard_map/ppermute | solution.py:201
  11.3 11.0 %collective-permute-start.2 = (bf16[8,64,384]{2,1,0:T(8,128)(2,1)S(1)}, bf16[8,64,384]{2,1,0:T(8,128)(2,1)S(1)}, u32[]{:S(2)}, u32[]{:S(2)}) collective-permute-start(bf16[8,64,384]{2,1,0:T(8,128)(2,1)S(1)} %collective-permute-done.refs_1_), channel_id=1, source_target_pairs={{6,0},{3,1},{0,2},{5,3},{2,4},{7,5},{4,6},{1,7},{14,8},{11,9},{8,1... | collective-permute-start | bytes 1179656 | tf_op jit(solution)/shard_map/ppermute | solution.py:204
  12.6 13.6 %collective-permute-start.11 = (bf16[8,64,384]{2,1,0:T(8,128)(2,1)S(1)}, bf16[8,64,384]{2,1,0:T(8,128)(2,1)S(1)}, u32[]{:S(2)}, u32[]{:S(2)}) collective-permute-start(bf16[8,64,384]{2,1,0:T(8,128)(2,1)S(1)} %collective-permute-done.1.refs_2_), channel_id=1, source_target_pairs={{6,0},{3,1},{0,2},{5,3},{2,4},{7,5},{4,6},{1,7},{14,8},{11,9},{8,1... | collective-permute-start | bytes 1179656 | tf_op jit(solution)/shard_map/ppermute | solution.py:206
  22.3 5.0 %collective-permute-start.10 = (bf16[8,64,384]{2,1,0:T(8,128)(2,1)S(1)}, bf16[8,64,384]{2,1,0:T(8,128)(2,1)S(1)}, u32[]{:S(2)}, u32[]{:S(2)}) collective-permute-start(bf16[8,64,384]{2,1,0:T(8,128)(2,1)S(1)} %collective-permute-done.2.refs_3_), channel_id=1, source_target_pairs={{1,0},{0,1},{3,2},{2,3},{5,4},{4,5},{7,6},{6,7},{9,8},{8,9},{11,10... | collective-permute-start | bytes 1179656 | tf_op jit(solution)/shard_map/ppermute | solution.py:179
  22.3 6.9 %copy-start.2 = (s32[48,2]{0,1:T(2,128)S(1)}, s32[48,2]{0,1:T(2,128)}, u32[]{:S(2)}) copy-start(s32[48,2]{0,1:T(2,128)} %param.13) | copy-start | bytes 1156
  22.4 6.9 %copy-start.3 = (s32[96,2]{0,1:T(2,128)S(1)}, s32[96,2]{0,1:T(2,128)}, u32[]{:S(2)}) copy-start(s32[96,2]{0,1:T(2,128)} %param.16) | copy-start | bytes 2308
  22.4 6.9 %copy-start.4 = (s32[96]{0:T(128)S(1)}, s32[96]{0:T(128)}, u32[]{:S(2)}) copy-start(s32[96]{0:T(128)} %far_rank.3) | copy-start | bytes 1156
  22.6 36.7 %collective-permute-start.6 = (bf16[4,2,4,64,384]{4,3,2,0,1:T(8,128)(2,1)S(1)}, bf16[4,2,4,64,384]{4,3,2,0,1:T(8,128)(2,1)S(1)}, u32[]{:S(2)}, u32[]{:S(2)}) collective-permute-start(bf16[4,2,4,64,384]{4,3,2,0,1:T(8,128)(2,1)S(1)} %pad_maximum_fusion), channel_id=1, source_target_pairs={{8,0},{33,1},{10,2},{35,3},{12,4},{37,5},{14,6},{39,7},{16,8},{41,... | collective-permute-start | bytes 4718600 | tf_op jit(solution)/shard_map/ppermute | solution.py:201
  25.1 34.2 %collective-permute-start.7 = (bf16[4,2,4,64,384]{4,3,2,0,1:T(8,128)(2,1)S(1)}, bf16[4,2,4,64,384]{4,3,2,0,1:T(8,128)(2,1)S(1)}, u32[]{:S(2)}, u32[]{:S(2)}) collective-permute-start(bf16[4,2,4,64,384]{4,3,2,0,1:T(8,128)(2,1)S(1)} %pad_maximum_fusion), channel_id=1, source_target_pairs={{16,0},{65,1},{18,2},{67,3},{20,4},{69,5},{22,6},{71,7},{24,8},{73... | collective-permute-start | bytes 4718600 | tf_op jit(solution)/shard_map/ppermute | solution.py:201
  25.8 37.3 %collective-permute-start.8 = (bf16[4,2,4,64,384]{4,3,2,0,1:T(8,128)(2,1)S(1)}, bf16[4,2,4,64,384]{4,3,2,0,1:T(8,128)(2,1)S(1)}, u32[]{:S(2)}, u32[]{:S(2)}) collective-permute-start(bf16[4,2,4,64,384]{4,3,2,0,1:T(8,128)(2,1)S(1)} %pad_maximum_fusion), channel_id=1, source_target_pairs={{24,0},{97,1},{26,2},{99,3},{28,4},{101,5},{30,6},{103,7},{0,8},{1... | collective-permute-start | bytes 4718600 | tf_op jit(solution)/shard_map/ppermute | solution.py:201
  26.2 2.5 %collective-permute-start.9 = (bf16[8,64,384]{2,1,0:T(8,128)(2,1)S(1)}, bf16[8,64,384]{2,1,0:T(8,128)(2,1)S(1)}, u32[]{:S(2)}, u32[]{:S(2)}) collective-permute-start(bf16[8,64,384]{2,1,0:T(8,128)(2,1)S(1)} %collective-permute-done.1.refs_2_), channel_id=1, source_target_pairs={{1,0},{0,1},{3,2},{2,3},{5,4},{4,5},{7,6},{6,7},{9,8},{8,9},{11,10... | collective-permute-start | bytes 1179656 | tf_op jit(solution)/shard_map/ppermute | solution.py:179
  27.3 1.9 %collective-permute-start.12 = (bf16[8,64,384]{2,1,0:T(8,128)(2,1)S(1)}, bf16[8,64,384]{2,1,0:T(8,128)(2,1)S(1)}, u32[]{:S(2)}, u32[]{:S(2)}) collective-permute-start(bf16[8,64,384]{2,1,0:T(8,128)(2,1)S(1)} %collective-permute-done.11.refs_6_), channel_id=1, source_target_pairs={{1,0},{0,1},{3,2},{2,3},{5,4},{4,5},{7,6},{6,7},{9,8},{8,9},{11,10... | collective-permute-start | bytes 1179656 | tf_op jit(solution)/shard_map/ppermute | solution.py:179
  44.7 3.4 %collective-permute-start.14 = (bf16[16,64,384]{2,1,0:T(8,128)(2,1)S(1)}, bf16[16,64,384]{2,1,0:T(8,128)(2,1)S(1)}, u32[]{:S(2)}, u32[]{:S(2)}) collective-permute-start(bf16[16,64,384]{2,1,0:T(8,128)(2,1)S(1)} %get-tuple-element.44), channel_id=1, source_target_pairs={{1,0},{0,1},{3,2},{2,3},{5,4},{4,5},{7,6},{6,7},{9,8},{8,9},{11,10... | collective-permute-start | bytes 2359304 | tf_op jit(solution)/shard_map/ppermute | solution.py:179
  46.2 3.6 %collective-permute-start.13 = (bf16[16,64,384]{2,1,0:T(8,128)(2,1)S(1)}, bf16[16,64,384]{2,1,0:T(8,128)(2,1)S(1)}, u32[]{:S(2)}, u32[]{:S(2)}) collective-permute-start(bf16[16,64,384]{2,1,0:T(8,128)(2,1)S(1)} %get-tuple-element.42), channel_id=1, source_target_pairs={{1,0},{0,1},{3,2},{2,3},{5,4},{4,5},{7,6},{6,7},{9,8},{8,9},{11,10... | collective-permute-start | bytes 2359304 | tf_op jit(solution)/shard_map/ppermute | solution.py:179
  48.1 20.3 %collective-permute-start.15 = (bf16[4,4,64,384]{3,2,1,0:T(8,128)(2,1)S(1)}, bf16[4,4,64,384]{3,2,1,0:T(8,128)(2,1)S(1)}, u32[]{:S(2)}, u32[]{:S(2)}) collective-permute-start(bf16[4,4,64,384]{3,2,1,0:T(8,128)(2,1)S(1)} %slice_bitcast_fusion), channel_id=1, source_target_pairs={{1,0},{0,1},{3,2},{2,3},{5,4},{4,5},{7,6},{6,7},{9,8},{8,9},{11,10... | collective-permute-start | bytes 2359304 | tf_op jit(solution)/shard_map/ppermute | solution.py:179
  49.8 15.9 %collective-permute-start.27 = (bf16[16,64,384]{2,1,0:T(8,128)(2,1)S(1)}, bf16[16,64,384]{2,1,0:T(8,128)(2,1)S(1)}, u32[]{:S(2)}, u32[]{:S(2)}) collective-permute-start(bf16[16,64,384]{2,1,0:T(8,128)(2,1)S(1)} %get-tuple-element.56), channel_id=1, source_target_pairs={{1,0},{0,1},{3,2},{2,3},{5,4},{4,5},{7,6},{6,7},{9,8},{8,9},{11,10... | collective-permute-start | bytes 2359304 | tf_op jit(solution)/shard_map/ppermute | solution.py:179
  63.1 5.7 %collective-permute-start.16 = (bf16[4,4,64,384]{3,2,1,0:T(8,128)(2,1)S(1)}, bf16[4,4,64,384]{3,2,1,0:T(8,128)(2,1)S(1)}, u32[]{:S(2)}, u32[]{:S(2)}) collective-permute-start(bf16[4,4,64,384]{3,2,1,0:T(8,128)(2,1)S(1)} %slice_bitcast_fusion.3), channel_id=1, source_target_pairs={{1,0},{0,1},{3,2},{2,3},{5,4},{4,5},{7,6},{6,7},{9,8},{8,9},{11,10... | collective-permute-start | bytes 2359304 | tf_op jit(solution)/shard_map/ppermute | solution.py:179
  64.8 6.4 %collective-permute-start.17 = (bf16[4,4,64,384]{3,2,1,0:T(8,128)(2,1)S(1)}, bf16[4,4,64,384]{3,2,1,0:T(8,128)(2,1)S(1)}, u32[]{:S(2)}, u32[]{:S(2)}) collective-permute-start(bf16[4,4,64,384]{3,2,1,0:T(8,128)(2,1)S(1)} %slice_bitcast_fusion.2), channel_id=1, source_target_pairs={{1,0},{0,1},{3,2},{2,3},{5,4},{4,5},{7,6},{6,7},{9,8},{8,9},{11,10... | collective-permute-start | bytes 2359304 | tf_op jit(solution)/shard_map/ppermute | solution.py:179
  65.0 6.2 %collective-permute-start.18 = (bf16[4,4,64,384]{3,2,1,0:T(8,128)(2,1)S(1)}, bf16[4,4,64,384]{3,2,1,0:T(8,128)(2,1)S(1)}, u32[]{:S(2)}, u32[]{:S(2)}) collective-permute-start(bf16[4,4,64,384]{3,2,1,0:T(8,128)(2,1)S(1)} %slice_bitcast_fusion.1), channel_id=1, source_target_pairs={{1,0},{0,1},{3,2},{2,3},{5,4},{4,5},{7,6},{6,7},{9,8},{8,9},{11,10... | collective-permute-start | bytes 2359304 | tf_op jit(solution)/shard_map/ppermute | solution.py:179
  67.1 31.3 %collective-permute-start.28 = (bf16[2,16,64,384]{3,2,1,0:T(8,128)(2,1)}, bf16[2,16,64,384]{3,2,1,0:T(8,128)(2,1)S(1)}, u32[]{:S(2)}, u32[]{:S(2)}) collective-permute-start(bf16[2,16,64,384]{3,2,1,0:T(8,128)(2,1)} %pad_maximum_fusion.3), channel_id=1, source_target_pairs={{16,0},{65,1},{18,2},{67,3},{20,4},{69,5},{22,6},{71,7},{24,8},{73... | collective-permute-start | bytes 4718600 | tf_op jit(solution)/shard_map/ppermute | solution.py:201
  68.2 3.0 %copy-start.1 = (bf16[96,384,32]{1,2,0:T(8,128)(2,1)S(1)}, bf16[96,384,32]{1,2,0:T(8,128)(2,1)}, u32[]{:S(2)}) copy-start(bf16[96,384,32]{1,2,0:T(8,128)(2,1)} %param.19) | copy-start | bytes 7077892
  68.4 36.8 %collective-permute-start.26 = (bf16[2,16,64,384]{3,2,1,0:T(8,128)(2,1)}, bf16[2,16,64,384]{3,2,1,0:T(8,128)(2,1)S(1)}, u32[]{:S(2)}, u32[]{:S(2)}) collective-permute-start(bf16[2,16,64,384]{3,2,1,0:T(8,128)(2,1)} %pad_maximum_fusion.1), channel_id=1, source_target_pairs={{24,0},{97,1},{26,2},{99,3},{28,4},{101,5},{30,6},{103,7},{0,8},{1... | collective-permute-start | bytes 4718600 | tf_op jit(solution)/shard_map/ppermute | solution.py:201
  68.9 36.3 %collective-permute-start.29 = (bf16[2,16,64,384]{3,2,1,0:T(8,128)(2,1)}, bf16[2,16,64,384]{3,2,1,0:T(8,128)(2,1)S(1)}, u32[]{:S(2)}, u32[]{:S(2)}) collective-permute-start(bf16[2,16,64,384]{3,2,1,0:T(8,128)(2,1)} %pad_maximum_fusion.2), channel_id=1, source_target_pairs={{8,0},{33,1},{10,2},{35,3},{12,4},{37,5},{14,6},{39,7},{16,8},{41,... | collective-permute-start | bytes 4718600 | tf_op jit(solution)/shard_map/ppermute | solution.py:201
  92.8 3.8 %collective-permute-start.19 = (bf16[16,64,384]{2,1,0:T(8,128)(2,1)S(1)}, bf16[16,64,384]{2,1,0:T(8,128)(2,1)S(1)}, u32[]{:S(2)}, u32[]{:S(2)}) collective-permute-start(bf16[16,64,384]{2,1,0:T(8,128)(2,1)S(1)} %get-tuple-element.49), channel_id=1, source_target_pairs={{1,0},{0,1},{3,2},{2,3},{5,4},{4,5},{7,6},{6,7},{9,8},{8,9},{11,10... | collective-permute-start | bytes 2359304 | tf_op jit(solution)/shard_map/ppermute | solution.py:179
  94.6 3.0 %collective-permute-start.20 = (bf16[16,64,384]{2,1,0:T(8,128)(2,1)S(1)}, bf16[16,64,384]{2,1,0:T(8,128)(2,1)S(1)}, u32[]{:S(2)}, u32[]{:S(2)}) collective-permute-start(bf16[16,64,384]{2,1,0:T(8,128)(2,1)S(1)} %get-tuple-element.51), channel_id=1, source_target_pairs={{1,0},{0,1},{3,2},{2,3},{5,4},{4,5},{7,6},{6,7},{9,8},{8,9},{11,10... | collective-permute-start | bytes 2359304 | tf_op jit(solution)/shard_map/ppermute | solution.py:179
  96.6 11.7 %collective-permute-start.25 = (bf16[16,64,384]{2,1,0:T(8,128)(2,1)S(1)}, bf16[16,64,384]{2,1,0:T(8,128)(2,1)S(1)}, u32[]{:S(2)}, u32[]{:S(2)}) collective-permute-start(bf16[16,64,384]{2,1,0:T(8,128)(2,1)S(1)} %get-tuple-element.53), channel_id=1, source_target_pairs={{1,0},{0,1},{3,2},{2,3},{5,4},{4,5},{7,6},{6,7},{9,8},{8,9},{11,10... | collective-permute-start | bytes 2359304 | tf_op jit(solution)/shard_map/ppermute | solution.py:179
  97.1 1.2 copy-start.5
  105.2 7.2 %collective-permute-start.23 = (bf16[8,64,384]{2,1,0:T(8,128)(2,1)S(1)}, bf16[8,64,384]{2,1,0:T(8,128)(2,1)S(1)}, u32[]{:S(2)}, u32[]{:S(2)}) collective-permute-start(bf16[8,64,384]{2,1,0:T(8,128)(2,1)S(1)} %slice.239), channel_id=1, source_target_pairs={{6,0},{3,1},{0,2},{5,3},{2,4},{7,5},{4,6},{1,7},{14,8},{11,9},{8,1... | collective-permute-start | bytes 1179656 | tf_op jit(solution)/shard_map/ppermute | solution.py:224
  107.7 8.9 %collective-permute-start.21 = (bf16[8,64,384]{2,1,0:T(8,128)(2,1)S(1)}, bf16[8,64,384]{2,1,0:T(8,128)(2,1)}, u32[]{:S(2)}, u32[]{:S(2)}) collective-permute-start(bf16[8,64,384]{2,1,0:T(8,128)(2,1)S(1)} %slice.240), channel_id=1, source_target_pairs={{6,0},{3,1},{0,2},{5,3},{2,4},{7,5},{4,6},{1,7},{14,8},{11,9},{8,1... | collective-permute-start | bytes 1179656 | tf_op jit(solution)/shard_map/ppermute | solution.py:225
  110.9 10.4 %collective-permute-start.31 = (bf16[2,4,64,384]{3,2,1,0:T(8,128)(2,1)}, bf16[2,4,64,384]{3,2,1,0:T(8,128)(2,1)}, u32[]{:S(2)}, u32[]{:S(2)}) collective-permute-start(bf16[2,4,64,384]{3,2,1,0:T(8,128)(2,1)} %get-tuple-element.69), channel_id=1, source_target_pairs={{64,0},{17,1},{66,2},{19,3},{68,4},{21,5},{70,6},{23,7},{72,8},{25... | collective-permute-start | bytes 1179656 | tf_op jit(solution)/shard_map/ppermute | solution.py:201
  110.9 11.2 %collective-permute-start.32 = (bf16[2,4,64,384]{3,2,1,0:T(8,128)(2,1)}, bf16[2,4,64,384]{3,2,1,0:T(8,128)(2,1)}, u32[]{:S(2)}, u32[]{:S(2)}) collective-permute-start(bf16[2,4,64,384]{3,2,1,0:T(8,128)(2,1)} %get-tuple-element.68), channel_id=1, source_target_pairs={{32,0},{9,1},{34,2},{11,3},{36,4},{13,5},{38,6},{15,7},{40,8},{17,... | collective-permute-start | bytes 1179656 | tf_op jit(solution)/shard_map/ppermute | solution.py:201
  111.5 12.3 %collective-permute-start.30 = (bf16[2,4,64,384]{3,2,1,0:T(8,128)(2,1)}, bf16[2,4,64,384]{3,2,1,0:T(8,128)(2,1)}, u32[]{:S(2)}, u32[]{:S(2)}) collective-permute-start(bf16[2,4,64,384]{3,2,1,0:T(8,128)(2,1)} %fusion.5), channel_id=1, source_target_pairs={{96,0},{25,1},{98,2},{27,3},{100,4},{29,5},{102,6},{31,7},{104,8},... | collective-permute-start | bytes 1179656 | tf_op jit(solution)/shard_map/ppermute | solution.py:201
  113.3 10.6 %collective-permute-start.24 = (bf16[8,64,384]{2,1,0:T(8,128)(2,1)}, bf16[8,64,384]{2,1,0:T(8,128)(2,1)}, u32[]{:S(2)}, u32[]{:S(2)}) collective-permute-start(bf16[8,64,384]{2,1,0:T(8,128)(2,1)} %fusion), channel_id=1, source_target_pairs={{6,0},{3,1},{0,2},{5,3},{2,4},{7,5},{4,6},{1,7},{14,8},{11,9},{8,1... | collective-permute-start | bytes 1179656 | tf_op jit(solution)/shard_map/ppermute | solution.py:231
  116.6 10.5 %collective-permute-start.22 = (bf16[8,64,384]{2,1,0:T(8,128)(2,1)}, bf16[8,64,384]{2,1,0:T(8,128)(2,1)}, u32[]{:S(2)}, u32[]{:S(2)}) collective-permute-start(bf16[8,64,384]{2,1,0:T(8,128)(2,1)} %collective-permute-done.21), channel_id=1, source_target_pairs={{1,0},{0,1},{3,2},{2,3},{5,4},{4,5},{7,6},{6,7},{9,8},{8,9},{11,10... | collective-permute-start | bytes 1179656 | tf_op jit(solution)/shard_map/ppermute | solution.py:179
  121.2 5.9 %copy-start.6 = (f32[16,64,384]{2,1,0:T(8,128)S(1)}, f32[16,64,384]{2,1,0:T(8,128)}, u32[]{:S(2)}) copy-start(f32[16,64,384]{2,1,0:T(8,128)} %copy-done.5) | copy-start | bytes 4718596
  121.2 5.9 %copy-start.7 = (f32[8,64,384]{2,1,0:T(8,128)S(1)}, f32[8,64,384]{2,1,0:T(8,128)}, u32[]{:S(2)}) copy-start(f32[8,64,384]{2,1,0:T(8,128)} %fusion.21) | copy-start | bytes 2359300
  125.4 3.0 %collective-permute-start.33 = (bf16[4,64,384]{2,1,0:T(8,128)(2,1)S(1)}, bf16[4,64,384]{2,1,0:T(8,128)(2,1)S(1)}, u32[]{:S(2)}, u32[]{:S(2)}) collective-permute-start(bf16[4,64,384]{2,1,0:T(8,128)(2,1)S(1)} %get-tuple-element.71), channel_id=1, source_target_pairs={{1,0},{0,1},{3,2},{2,3},{5,4},{4,5},{7,6},{6,7},{9,8},{8,9},{11,10... | collective-permute-start | bytes 589832 | tf_op jit(solution)/shard_map/ppermute | solution.py:179
